TPU v7x, 256 devices: a whole 4x4x8 slice. The times are simulated.
256 devices in a mesh: lat: 16 (over z, y_hi), lon: 16 (over y_lo, x, core).
Axes of the slice: x: 4, y: 4 (y_hi: 2, y_lo: 2; y = y_hi * 2 + y_lo), z: 8, core: 2. Of those that a mesh axis runs over, the one named last changes fastest.
Arguments:
- saved_state: bfloat16 [256, 1024, 512], P('lat', 'lon'), may hold values from -6 to 6
- cotangent: bfloat16 [256, 1024, 512], P('lat', 'lon'), may hold values from -6 to 6
- row_mask: int32 [256], P('lat'), may hold values from 0 to 1, as said below
- shifts: int32 [2], replicated, may hold values from 1 to 7, as said below
- norm_gain: float32 [512], replicated, may hold values from 0.5 to 1.5
- w_qkv: bfloat16 [512, 1536], replicated, may hold values from -0.25 to 0.25
- w_out: bfloat16 [512, 512], replicated, may hold values from -0.25 to 0.25
- bias_table: float32 [16, 225], replicated, may hold values from -4 to 260
Outputs:
- state_grad: bfloat16 [256, 1024, 512], P('lat', 'lon')
- qkv_grad: float32 [512, 1536], replicated
- out_grad: float32 [512, 512], replicated
- gain_grad: float32 [512], replicated
- bias_grad: float32 [16, 225], replicated
Inputs may be any that keep to these rules, and one draw needn't show every extreme that they name: row_mask is 1 on all rows below some L and 0 from L on, with 224 <= L <= 249. `shifts`: one of the two offsets is 7.
All inputs are finite; a program needn't handle non-finite values.
Results may differ from a plain program's by a relative error of at most 0.013.
Values may be sent and summed in bfloat16 or wider, within the bound.
No kernel may reach another device: no remote copies, remote signals or barrier semaphores. Data moves between devices by JAX's collectives and lax.ppermute only.
A program may use at most 128 MiB of HBM per device.

v0:
```python
import functools
import itertools
import math

import jax
import jax.numpy as jnp
from jax import lax
from jax.experimental import pallas as pl
from jax.experimental.pallas import tpu as pltpu
from jax.sharding import PartitionSpec as P

EPSILON = 1e-05


NT = (((1,), (1,)), ((), ()))
NN = (((1,), (0,)), ((), ()))
LANES = 128
WINDOW = 8
CELLS = WINDOW * WINDOW
TOKENS = 256
MIB = 1024 * 1024


def dot(a, b, dims=NN):
    return lax.dot_general(a, b, dims, preferred_element_type=jnp.float32)


def whole(*_):
    return pl.BlockSpec(memory_space=pltpu.VMEM)


def norm_stats(x):
    cen = x - jnp.mean(x, -1, keepdims=True)
    inv = lax.rsqrt(jnp.mean(cen * cen, -1, keepdims=True) + EPSILON)
    return cen * inv, inv


def project_cells(scale, gain, wt_ref, w_ref, xf, x_out, nrm_t, proj_t, kv):
    n_tok, n_chan = xf.shape
    x_out[...] = xf[...].astype(jnp.bfloat16)
    for base in range(0, n_tok, TOKENS):
        rows = slice(base, base + TOKENS)
        x_hat, _ = norm_stats(xf[rows])
        normed_f = x_hat * gain
        normed = normed_f.astype(jnp.bfloat16)
        nrm_t[:, rows] = normed_f.T.astype(jnp.bfloat16)
        proj_t[:n_chan, rows] = (dot(wt_ref[:n_chan], normed, NT) * scale).astype(jnp.bfloat16)
        proj_t[n_chan:, rows] = dot(wt_ref[n_chan:], normed, NT).astype(jnp.bfloat16)
        kv[rows] = dot(normed, w_ref[:, n_chan:]).astype(jnp.bfloat16)


def block_diag(block, step):
    blank = jnp.zeros((step, block.shape[1]), block.dtype)
    count = block.shape[0] // step
    columns = []
    for h in range(count):
        parts = [blank] * count
        parts[h] = block[h * step : (h + 1) * step]
        columns.append(jnp.concatenate(parts, 0))
    return jnp.concatenate(columns, 1)


def attention_unit(n_chan, dim, scale, bias_ref, mask, proj_t, kv, gm_t, mix_t, gp_t, bsum_ref, pair, group):
    lanes = pl.ds(pl.multiple_of(pair * LANES, LANES), LANES)
    c0 = group * LANES
    q_t = proj_t[pl.ds(c0, LANES), lanes]
    k_t = proj_t[pl.ds(n_chan + c0, LANES), lanes]
    v_t = proj_t[pl.ds(2 * n_chan + c0, LANES), lanes]
    g_t = gm_t[pl.ds(c0, LANES), lanes]
    k_tok = kv[lanes, pl.ds(c0, LANES)]
    v_tok = kv[lanes, pl.ds(n_chan + c0, LANES)]
    scores = dot(k_tok, block_diag(q_t, dim))
    grads = dot(v_tok, block_diag(g_t, dim))
    first = lax.broadcasted_iota(jnp.int32, (CELLS, LANES), 1) < CELLS
    heads = LANES // dim
    mixed, dq, dk, dv = [], [], [], []
    for h in range(heads):
        cut = slice(h * LANES, (h + 1) * LANES)
        rows = slice(h * dim, (h + 1) * dim)
        head = group * heads + h
        s = jnp.where(first, scores[:CELLS, cut], scores[CELLS:, cut]) + bias_ref[head] + mask
        e = jnp.exp(s - jnp.max(s, 0, keepdims=True))
        a = e * (1.0 / jnp.sum(e, 0, keepdims=True))
        d = jnp.where(first, grads[:CELLS, cut], grads[CELLS:, cut])
        ad = a * d
        ds = ad - a * jnp.sum(ad, 0, keepdims=True)
        bsum_ref[head] += ds
        zero = jnp.zeros_like(a)
        a2 = jnp.concatenate([jnp.where(first, a, zero), jnp.where(first, zero, a)], 0).astype(jnp.bfloat16)
        ds2 = jnp.concatenate([jnp.where(first, ds, zero), jnp.where(first, zero, ds)], 0).astype(jnp.bfloat16)
        mixed.append(dot(v_t[rows], a2))
        dv.append(dot(g_t[rows], a2, NT))
        dq.append(dot(k_t[rows], ds2) * scale)
        dk.append(dot(q_t[rows], ds2, NT))
    mix_t[pl.ds(c0, LANES), lanes] = jnp.concatenate(mixed, 0).astype(jnp.bfloat16)
    gp_t[pl.ds(c0, LANES), lanes] = jnp.concatenate(dq, 0).astype(jnp.bfloat16)
    gp_t[pl.ds(n_chan + c0, LANES), lanes] = jnp.concatenate(dk, 0).astype(jnp.bfloat16)
    gp_t[pl.ds(2 * n_chan + c0, LANES), lanes] = jnp.concatenate(dv, 0).astype(jnp.bfloat16)


def place_row(line, shift, out, r, live=None):
    line = line.astype(jnp.float32).reshape(-1, WINDOW, line.shape[1])
    if live is not None:
        line = line * live
    line = pltpu.roll(line, WINDOW - shift, 1)
    head = lax.broadcasted_iota(jnp.int32, line.shape[1:], 0) < WINDOW - shift
    for w in range(line.shape[0] - 1):
        start = w * CELLS + r * WINDOW
        out[start : start + WINDOW] = jnp.where(head, line[w], line[w + 1])


def window_row(n_head, cf, live, wo_ref, bias_ref, go_ref, mix_t, gp_t, bsum_ref, proj_t, kv, gm_t):
    n_tok, n_chan = cf.shape
    dim = n_chan // n_head
    scale = dim ** (-0.5)
    go_ref[...] = cf[...].astype(jnp.bfloat16)
    for base in range(0, n_tok, TOKENS):
        rows = slice(base, base + TOKENS)
        gm_t[:, rows] = dot(wo_ref[...], go_ref[rows], NT).astype(jnp.bfloat16)
    mask = jnp.concatenate([(live[r][:, :LANES] - 1.0) * 1e30 for r in range(WINDOW)], 0)
    groups = n_chan // LANES

    @pl.loop(0, n_tok // LANES)
    def _(pair):
        for group in range(groups):
            attention_unit(n_chan, dim, scale, bias_ref, mask, proj_t, kv, gm_t, mix_t, gp_t, bsum_ref, pair, group)


def weight_sums(sums, nrm_t, gp_t, mix_t, go_ref, more):
    n_proj, n_chan = gp_t.shape[0], nrm_t.shape[0]
    for base in range(0, n_proj + n_chan, TOKENS):
        cols = slice(base, base + TOKENS)
        if base < n_proj:
            part = dot(nrm_t[...], gp_t[cols], NT)
        else:
            part = dot(mix_t[...], go_ref[:, base - n_proj : base - n_proj + TOKENS])
        sums[:, cols] = part if more is None else part + more[:, cols]


def inner_kernel(n_head, meta, x_ref, cot_ref, side_ref, bias_ref, gain_ref, wt_ref, w_ref, wo_ref,
                 x_out, gp_t, sums_ref, bsum_ref, go_ref, nrm_t, mix_t, xf, cf, proj_t, kv, gm_t):
    scale = (x_ref.shape[2] // n_head) ** (-0.5)
    lat, lon = meta[0], meta[1]
    live = []
    for r in range(WINDOW):
        live.append(jnp.full((WINDOW, x_ref.shape[2]), meta[6 + lat + r].astype(jnp.float32)))
        for k, (grid, out) in enumerate(((x_ref, xf), (cot_ref, cf))):
            line = jnp.concatenate([part.astype(jnp.float32) for part in (side_ref[k, lat + r], grid[lat + r])], 0)
            place_row(line, lon, out, r, live[r] if k else None)
    bsum_ref[...] = jnp.zeros_like(bsum_ref)
    project_cells(scale, gain_ref[...], wt_ref, w_ref, xf, x_out, nrm_t, proj_t, kv)
    window_row(n_head, cf, live, wo_ref, bias_ref, go_ref, mix_t, gp_t, bsum_ref, proj_t, kv, gm_t)
    weight_sums(sums_ref, nrm_t, gp_t, mix_t, go_ref, None)


def outer_line(k, e, grid, side_ref, top, corner_ref):
    n_top = top.shape[0]
    above = e < WINDOW
    up = jnp.clip(e - (WINDOW - n_top), 0, n_top - 1)
    own = jnp.maximum(e - WINDOW, 0)
    parts = jnp.where(above, corner_ref[k, up], side_ref[k, own]), jnp.where(above, top[up], grid[own])
    return jnp.concatenate([part.astype(jnp.float32) for part in parts], 0)


def front_kernel(n_head, meta, x_ref, side_ref, top, corner_ref, gain_ref, wt_ref, w_ref, _, x_out, nrm_t, proj_t, kv, xf):
    scale = (x_ref.shape[2] // n_head) ** (-0.5)
    for r in range(WINDOW):
        place_row(outer_line(0, meta[0] + r, x_ref, side_ref, top, corner_ref), meta[1], xf, r)
    project_cells(scale, gain_ref[...], wt_ref, w_ref, xf, x_out, nrm_t, proj_t, kv)


def outer_kernel(n_head, counts, meta, cot_ref, side_ref, top, corner_ref, bias_ref, gain_ref, w_ref, wo_ref,
                 nrm_t, proj_t, kv, sums_in, bsum_in,
                 gp_t, keep_ref, send_ref,
                 go_ref, mix_t, bsum_ref, cf, gm_t, sums, spread_a, spread_b):
    n_chan = gain_ref.shape[1]
    up_mask = corner_ref[0, WINDOW - 1].astype(jnp.float32) * meta[5].astype(jnp.float32)
    line_of = lax.broadcasted_iota(jnp.int32, up_mask.shape, 0)
    live = []
    for r in range(WINDOW):
        e = meta[0] + r
        row_live = jnp.full((WINDOW, n_chan), meta[6 + jnp.maximum(e - WINDOW, 0)].astype(jnp.float32))
        up_live = jnp.sum(jnp.where(line_of == e, up_mask, 0.0), 0, keepdims=True)
        live.append(jnp.where(e < WINDOW, jnp.broadcast_to(up_live, row_live.shape), row_live))
        place_row(outer_line(1, e, cot_ref, side_ref, top, corner_ref), meta[1], cf, r, live[r])
    bsum_ref[...] = bsum_in[...]
    window_row(n_head, cf, live, wo_ref, bias_ref, go_ref, mix_t, gp_t, bsum_ref, proj_t, kv, gm_t)

    n_proj = 3 * n_chan
    weight_sums(sums, nrm_t, gp_t, mix_t, go_ref, sums_in)
    gain_sum = jnp.sum(sums[:, :n_proj] * w_ref[...].astype(jnp.float32), 1, keepdims=True)

    width = 2 * LANES
    cell = lax.broadcasted_iota(jnp.int32, (LANES, width), 0) % CELLS
    lane = lax.broadcasted_iota(jnp.int32, (LANES, width), 1)
    place = (cell // WINDOW) * 16 + cell % WINDOW + 119
    onehot = (lane == place).astype(jnp.float32).astype(jnp.bfloat16)
    flat = bsum_ref[...].reshape(n_head * CELLS, LANES)
    high = flat.astype(jnp.bfloat16)
    low = (flat - high.astype(jnp.float32)).astype(jnp.bfloat16)
    spread = dot(high, onehot) + dot(low, onehot)
    spread_a[...] = spread[:, :LANES]
    spread_b[...] = spread[:, LANES:]
    bias_sum = jnp.zeros((n_head, width), jnp.float32)
    for j in range(CELLS):
        row = jnp.concatenate([ref[pl.ds(j, n_head, stride=CELLS), :] for ref in (spread_a, spread_b)], 1)
        by = (j // WINDOW) * 16 + j % WINDOW
        bias_sum += pltpu.roll(row, width - by, 1) if by else row
    tail = lax.broadcasted_iota(jnp.int32, (n_chan, LANES), 1) == LANES - 1
    bias_rows = jnp.concatenate(
        [bias_sum[:, :LANES], bias_sum[:, LANES:], jnp.zeros((n_chan - 2 * n_head, LANES), jnp.float32)], 0
    )
    sums[:, n_proj + n_chan :] = jnp.where(tail, gain_sum * (1.0 / gain_col(gain_ref)), bias_rows)

    n_c, n_x, n_y = counts
    rows = n_chan // (n_c * n_x * n_y)
    for c in range(n_c):
        for x in range(n_x):
            for y in range(n_y):
                chunk = sums[((c * n_x + x) * n_y + y) * rows : ((c * n_x + x) * n_y + y + 1) * rows]
                at = lax.rem(x - meta[3] + n_x, n_x) * n_y + lax.rem(y - meta[4] + n_y, n_y)

                @pl.when(meta[2] == c)
                def _():
                    keep_ref[at] = chunk

                @pl.when(meta[2] != c)
                def _():
                    send_ref[at] = chunk.astype(jnp.bfloat16)


def gain_col(gain_ref):
    n_chan = gain_ref.shape[1]
    return jnp.broadcast_to(gain_ref[...], (LANES, n_chan)).T[:, :1]


def cells_kernel(meta, xi_ref, xo_ref, gpi_ref, gpo_ref, cot_ref, gain_ref, w_ref, base_ref, top_ref, side_ref, corner_ref, ext):
    n_rows, n_cols, n_chan = cot_ref.shape
    lat, lon = meta[0], meta[1]
    ext[...] = jnp.zeros_like(ext)
    for part, (x_ref, gp_t) in enumerate(((xo_ref, gpo_ref), (xi_ref, gpi_ref))):
        n_tok = x_ref.shape[0]
        cells = []
        for base in range(0, n_tok, TOKENS):
            rows = slice(base, base + TOKENS)
            x_hat, inv = norm_stats(x_ref[rows].astype(jnp.float32))
            g = dot(w_ref[...], gp_t[:, rows]).T * gain_ref[...]
            cells.append(inv * (g - jnp.mean(g, -1, keepdims=True) - x_hat * jnp.mean(g * x_hat, -1, keepdims=True)))
        blank = jnp.zeros((1, WINDOW, n_chan), jnp.float32)
        head = lax.broadcasted_iota(jnp.int32, (WINDOW, n_chan), 0) < lon
        for r in range(WINDOW):
            row = jnp.stack(
                [
                    cells[w * CELLS // TOKENS][w * CELLS % TOKENS + r * WINDOW :][:WINDOW]
                    for w in range(n_tok // CELLS)
                ],
                0,
            )
            row = jnp.concatenate([blank, pltpu.roll(row, lon, 1), blank], 0)
            for t in range(row.shape[0] - 1):
                ext[lat + part * WINDOW + r, t * WINDOW : (t + 1) * WINDOW, :] = jnp.where(head, row[t], row[t + 1])
    for r in range(n_rows):
        base_ref[r] = (cot_ref[r].astype(jnp.float32) + ext[WINDOW + r, WINDOW:]).astype(jnp.bfloat16)
        side_ref[r] = ext[WINDOW + r, :WINDOW].astype(jnp.bfloat16)
    n_top = top_ref.shape[0]
    for r in range(n_top):
        top_ref[r] = ext[WINDOW - n_top + r, WINDOW:].astype(jnp.bfloat16)
        corner_ref[r] = ext[WINDOW - n_top + r, :WINDOW].astype(jnp.bfloat16)


def prepare_kernel(bias_ref, w_ref, full_ref, wt_ref):
    n_head, n_gap = bias_ref.shape
    span = 2 * WINDOW - 1
    width = 2 * LANES
    lane = lax.broadcasted_iota(jnp.int32, (width, LANES), 0)
    cell = lax.broadcasted_iota(jnp.int32, (width, LANES), 1) % CELLS
    place = cell // WINDOW * span + cell % WINDOW + n_gap // 2
    onehot = (lane == place).astype(jnp.float32).astype(jnp.bfloat16)
    table = jnp.concatenate([bias_ref[...], jnp.zeros((n_head, width - n_gap), jnp.float32)], 1)
    for h in range(n_head):
        line = jnp.broadcast_to(table[h : h + 1], (WINDOW, width))
        rows = [pltpu.roll(line, r * span, 1, stride=1, stride_axis=0) for r in range(WINDOW)]
        rest = jnp.concatenate(rows, 0)
        total = jnp.zeros((CELLS, LANES), jnp.float32)
        for _ in range(3):
            part = rest.astype(jnp.bfloat16)
            total += dot(part, onehot)
            rest = rest - part.astype(jnp.float32)
        full_ref[h] = total
    wt_ref[...] = w_ref[...].T


def pack_kernel(n_top, x_ref, cot_ref, mask, side_ref, top_x, top_c, corner_ref, edges, sems):
    n_rows, n_cols, n_chan = x_ref.shape
    copies = []
    for k, (ref, top) in enumerate(((x_ref, top_x), (cot_ref, top_c))):
        copies.append(pltpu.make_async_copy(ref.at[:, pl.ds(n_cols - 2 * WINDOW, 2 * WINDOW)], edges.at[k], sems.at[2 * k]))
        copies.append(pltpu.make_async_copy(ref.at[pl.ds(n_rows - n_top, n_top)], top, sems.at[2 * k + 1]))
    for copy in copies:
        copy.start()
    for k in range(2):
        copies[2 * k].wait()
        for r in range(n_rows):
            edge = edges[k, r][WINDOW:]
            side_ref[k, r] = edge
            at = r - n_rows + n_top
            if at >= 0:
                corner_ref[k, at] = edge
    line = lax.broadcasted_iota(jnp.int32, (WINDOW, n_chan), 0)
    live = jnp.zeros((WINDOW, n_chan), jnp.float32)
    for r in range(WINDOW):
        live = jnp.where(line == r, mask[n_rows - WINDOW + r].astype(jnp.float32), live)
    corner_ref[0, n_top] = live.astype(jnp.bfloat16)
    corner_ref[1, n_top] = live.astype(jnp.bfloat16)
    copies[1].wait()
    copies[3].wait()


def first_add_kernel(keep_ref, got_ref, own_ref, *send_refs):
    size = own_ref.shape[0]
    for k in range(len(send_refs) + 1):
        cut = slice(k * size, (k + 1) * size)
        total = keep_ref[cut] + got_ref[cut].astype(jnp.float32)
        if k:
            send_refs[k - 1][...] = total.astype(jnp.bfloat16)
        else:
            own_ref[...] = total


def next_add_kernel(n_got, n_more, own_ref, *refs):
    got, (out_ref, *send_refs) = refs[:n_got], refs[n_got + n_more :]
    size = out_ref.shape[0]
    for k in range(len(send_refs) + 1):
        cut = slice(k * size, (k + 1) * size)
        total = own_ref[cut]
        for ref in got:
            total = total + ref[cut].astype(jnp.float32)
        if k:
            send_refs[k - 1][...] = total.astype(jnp.bfloat16)
        else:
            out_ref[...] = total.astype(out_ref.dtype)


def join_kernel(n_got, *refs):
    for k in range(n_got):
        refs[-1][k : k + 1] = refs[k][...]


def pair_add_kernel(a_ref, b_ref, *refs):
    refs[-1][...] = (a_ref[...].astype(jnp.float32) + b_ref[...].astype(jnp.float32)).astype(jnp.bfloat16)


def unpack_kernel(counts, n_proj, factor, meta, *refs):
    n_c, n_x, n_y = counts
    mine, other = refs[:n_x], refs[n_x : 2 * n_x]
    qkv_ref, out_ref, gain_ref, bias_ref, small = refs[2 * n_x :]
    rows = mine[0].shape[1]
    n_chan = out_ref.shape[1]
    for half in range(2):
        c = meta[2] if half == 0 else 1 - meta[2]
        for k, ref in enumerate(other if half else mine):
            x = lax.rem(meta[3] + k, n_x)
            for j in range(n_y):
                y = lax.rem(meta[4] + j, n_y)
                chunk = ref[j].astype(jnp.float32) * factor
                to = pl.ds(pl.multiple_of(((c * n_x + x) * n_y + y) * rows, rows), rows)
                qkv_ref[to] = chunk[:, :n_proj]
                out_ref[to] = chunk[:, n_proj : n_proj + n_chan]
                small[to] = chunk[:, n_proj + n_chan :]
    gain_ref[...] = small[...].T[LANES - 1 :]
    n_head, n_gap = bias_ref.shape
    span = 2 * WINDOW - 1
    wide = jnp.concatenate([small[:n_head], small[n_head : 2 * n_head]], 1)
    lane = lax.broadcasted_iota(jnp.int32, wide.shape, 1)
    bias = jnp.zeros_like(wide)
    for k in range(span):
        moved = pltpu.roll(wide, 2 * LANES - k, 1) if k else wide
        bias = jnp.where((lane >= k * span) & (lane < (k + 1) * span), moved, bias)
    bias_ref[...] = bias[:, :n_gap]


class Places:
    def __init__(self):
        self.n_lat, self.n_lon = lax.axis_size("lat"), lax.axis_size("lon")
        self.c = 2
        self.x = min(4, self.n_lon // self.c)
        self.y_low = self.n_lon // (self.c * self.x)
        self.y_high = 2
        self.y = self.y_low * self.y_high
        self.z = self.n_lat // self.y_high

    def index(self, z, y, x, c):
        high, low = divmod(y, self.y_low)
        return (z * self.y_high + high) * self.n_lon + (low * self.x + x) * self.c + c

    def mine(self):
        lat, lon = lax.axis_index("lat"), lax.axis_index("lon")
        return (
            lon % self.c,
            lon // self.c % self.x,
            lat % self.y_high * self.y_low + lon // (self.c * self.x),
        )

    def move(self, array, to):
        every = itertools.product(range(self.z), range(self.y), range(self.x), range(self.c))
        pairs = [(self.index(*at), self.index(*to(*at))) for at in every]
        return lax.ppermute(array, ("lat", "lon"), pairs)

    def by_c(self, array):
        return self.move(array, lambda z, y, x, c: (z, y, x, 1 - c))

    def by_x(self, array, k):
        return self.move(array, lambda z, y, x, c: (z, y, (x + k) % self.x, c))

    def by_y(self, array, k):
        return self.move(array, lambda z, y, x, c: (z, (y + k) % self.y, x, c))

    def by_z(self, array, bits):
        return self.move(array, lambda z, y, x, c: (z ^ bits, y, x, c))


def small_call(kernel, outs, name, limit, *args):
    return pl.pallas_call(
        kernel,
        out_shape=outs,
        compiler_params=pltpu.CompilerParams(vmem_limit_bytes=limit * MIB),
        name=name,
    )(*args)


def total_over_devices(places, keep, send, ahead, behind):
    shape = keep.shape[1:]
    bf = functools.partial(jax.ShapeDtypeStruct, dtype=jnp.bfloat16)
    got = places.by_c(send)
    own = jax.ShapeDtypeStruct((places.y, *shape), jnp.float32)
    own, *sends = small_call(first_add_kernel, (own,) + (bf((places.y, *shape)),) * (places.x - 1), "add_c", 12, keep, got)
    got = [places.by_x(part, k + 1) for k, part in enumerate(sends)]
    nxt = jax.ShapeDtypeStruct((1, *shape), jnp.float32)
    own, *sends = pl.pallas_call(
        functools.partial(next_add_kernel, len(got), 1),
        out_shape=(nxt,) + (bf((1, *shape)),) * (places.y - 1),
        in_specs=[whole()] * (1 + len(got)) + [pl.BlockSpec(memory_space=pl.ANY)],
        compiler_params=pltpu.CompilerParams(vmem_limit_bytes=6 * MIB),
        name="add_x",
    )(own, *got, ahead)
    got = [places.by_y(part, k + 1) for k, part in enumerate(sends)]
    (mine,) = small_call(functools.partial(next_add_kernel, len(got), 0), (bf((1, *shape)),), "add_y", 4, own, *got)
    for bits in {1: (), 2: (1,), 4: (1, 3), 8: (1, 2, 6)}[places.z]:
        other = places.by_z(mine, bits)
        mine = small_call(pair_add_kernel, bf((1, *shape)), "add_z", 2, mine, other)
    parts = [mine] + [places.by_y(mine, -k) for k in range(1, places.y)]
    mine = pl.pallas_call(
        functools.partial(join_kernel, len(parts)),
        out_shape=bf((places.y, *shape)),
        in_specs=[whole()] * len(parts) + [pl.BlockSpec(memory_space=pl.ANY)] * len(behind),
        compiler_params=pltpu.CompilerParams(vmem_limit_bytes=4 * MIB),
        name="join",
    )(*parts, *behind)
    mine = [mine] + [places.by_x(mine, -k) for k in range(1, places.x)]
    return mine, [places.by_c(part) for part in mine]


def ring(array, lat, lon):
    n_lat, n_lon = lax.axis_size("lat"), lax.axis_size("lon")
    pairs = [
        (i * n_lon + j, (i + lat) % n_lat * n_lon + (j + lon) % n_lon) for i in range(n_lat) for j in range(n_lon)
    ]
    return lax.ppermute(array, ("lat", "lon"), pairs)


def local(saved_state, cotangent, row_mask, shifts, norm_gain, w_qkv, w_out, bias_table):
    n_rows, n_cols, n_chan = saved_state.shape
    n_head = bias_table.shape[0]
    n_proj = w_qkv.shape[1]
    n_tok = n_rows // 2 * n_cols
    n_top = WINDOW - 1
    places = Places()
    counts = (places.c, places.x, places.y)
    bf, f32 = jnp.bfloat16, jnp.float32

    smem = pl.BlockSpec(memory_space=pltpu.SMEM)
    tile = functools.partial(jax.ShapeDtypeStruct, dtype=bf)
    side, top_x, top_c, corner = pl.pallas_call(
        functools.partial(pack_kernel, n_top),
        out_shape=(
            tile((2, n_rows, WINDOW, n_chan)),
            tile((n_top, n_cols, n_chan)),
            tile((n_top, n_cols, n_chan)),
            tile((2, WINDOW, WINDOW, n_chan)),
        ),
        in_specs=[pl.BlockSpec(memory_space=pltpu.HBM), pl.BlockSpec(memory_space=pltpu.HBM), smem],
        scratch_shapes=[pltpu.VMEM((2, n_rows, 2 * WINDOW, n_chan), bf), pltpu.SemaphoreType.DMA((4,))],
        compiler_params=pltpu.CompilerParams(vmem_limit_bytes=58 * MIB),
        name="pack",
    )(saved_state, cotangent, row_mask)
    side = ring(side, 0, 1)
    top_x = ring(top_x, 1, 0)
    top_c = ring(top_c, 1, 0)
    corner = ring(corner, 1, 1)
    at = jnp.stack(places.mine()).astype(jnp.int32)
    gain = norm_gain.reshape(1, n_chan)
    bias, w_t = pl.pallas_call(
        prepare_kernel,
        out_shape=(jax.ShapeDtypeStruct((n_head, CELLS, LANES), f32), tile((n_proj, n_chan))),
        compiler_params=pltpu.CompilerParams(vmem_limit_bytes=16 * MIB),
        cost_estimate=pl.CostEstimate(flops=10**9, bytes_accessed=4 * MIB, transcendentals=0),
        name="prepare",
    )(bias_table, w_qkv)

    below = jnp.minimum(lax.axis_index("lat"), 1).astype(jnp.int32).reshape(1)
    meta = jnp.concatenate([shifts, at, below, row_mask])
    cells_f, cells_t = pltpu.VMEM((n_tok, n_chan), f32), pltpu.VMEM((n_chan, n_tok), bf)
    x_in, gp_in, sums_in, bsum_in = pl.pallas_call(
        functools.partial(inner_kernel, n_head),
        out_shape=(
            tile((n_tok, n_chan)),
            tile((n_proj, n_tok)),
            jax.ShapeDtypeStruct((n_chan, n_proj + n_chan), f32),
            jax.ShapeDtypeStruct((n_head, CELLS, LANES), f32),
        ),
        in_specs=[smem] + [whole()] * 8,
        scratch_shapes=[
            pltpu.VMEM((n_tok, n_chan), bf),
            cells_t,
            cells_t,
            cells_f,
            cells_f,
            pltpu.VMEM((n_proj, n_tok), bf),
            pltpu.VMEM((n_tok, 2 * n_chan), bf),
            cells_t,
        ],
        compiler_params=pltpu.CompilerParams(vmem_limit_bytes=24 * MIB),
        cost_estimate=pl.CostEstimate(flops=8 * 10**9, bytes_accessed=16 * MIB, transcendentals=2**19),
        name="inner",
    )(meta, saved_state, cotangent, side, bias, gain, w_t, w_qkv, w_out)
    x_out, nrm_out, proj_out, kv_out = pl.pallas_call(
        functools.partial(front_kernel, n_head),
        out_shape=(tile((n_tok, n_chan)), tile((n_chan, n_tok)), tile((n_proj, n_tok)), tile((n_tok, 2 * n_chan))),
        in_specs=[smem] + [whole()] * 7 + [pl.BlockSpec(memory_space=pl.ANY)],
        scratch_shapes=[cells_f],
        compiler_params=pltpu.CompilerParams(vmem_limit_bytes=14 * MIB),
        cost_estimate=pl.CostEstimate(flops=3 * 10**9, bytes_accessed=8 * MIB, transcendentals=0),
        name="front",
    )(meta, saved_state, side, top_x, corner, gain, w_t, w_qkv, bsum_in)

    width = n_proj + n_chan + LANES
    rows = n_chan // math.prod(counts)
    half = math.prod(counts) // 2
    gp_out, keep, send = pl.pallas_call(
        functools.partial(outer_kernel, n_head, counts),
        out_shape=(
            tile((n_proj, n_tok)),
            jax.ShapeDtypeStruct((half, rows, width), f32),
            tile((half, rows, width)),
        ),
        in_specs=[smem] + [whole()] * 13,
        scratch_shapes=[
            pltpu.VMEM((n_tok, n_chan), bf),
            cells_t,
            pltpu.VMEM((n_head, CELLS, LANES), f32),
            cells_f,
            cells_t,
            pltpu.VMEM((n_chan, width), f32),
            pltpu.VMEM((n_head * CELLS, LANES), f32),
            pltpu.VMEM((n_head * CELLS, LANES), f32),
        ],
        compiler_params=pltpu.CompilerParams(vmem_limit_bytes=30 * MIB),
        cost_estimate=pl.CostEstimate(flops=10**10, bytes_accessed=24 * MIB, transcendentals=2**19),
        name="outer",
    )(meta, cotangent, side, top_c, corner, bias, gain, w_qkv, w_out, nrm_out, proj_out, kv_out, sums_in, bsum_in)

    base, *edges = pl.pallas_call(
        cells_kernel,
        out_shape=(
            tile((n_rows, n_cols, n_chan)),
            tile((n_top, n_cols, n_chan)),
            tile((n_rows, WINDOW, n_chan)),
            tile((n_top, WINDOW, n_chan)),
        ),
        in_specs=[smem] + [whole()] * 7,
        scratch_shapes=[pltpu.VMEM((n_rows + WINDOW, n_cols + WINDOW, n_chan), f32)],
        compiler_params=pltpu.CompilerParams(vmem_limit_bytes=24 * MIB),
        cost_estimate=pl.CostEstimate(flops=16 * 10**8, bytes_accessed=12 * MIB, transcendentals=0),
        name="cells",
    )(meta, x_in, x_out, gp_in, gp_out, cotangent, gain, w_qkv)
    top_back, side_back, corner_back = ring(edges[0], -1, 0), ring(edges[1], 0, -1), ring(edges[2], -1, -1)
    mine, other = total_over_devices(places, keep, send, edges[2], (top_back, side_back, corner_back))
    edge = jnp.pad(top_back, ((n_rows - n_top, 0), (0, 0), (0, 0)))
    edge = edge + jnp.pad(side_back, ((0, 0), (n_cols - WINDOW, 0), (0, 0)))
    edge = edge + jnp.pad(corner_back, ((n_rows - n_top, 0), (n_cols - WINDOW, 0), (0, 0)))
    state_grad = (base.astype(f32) + edge.astype(f32)).astype(bf)

    factor = 1.0 / math.sqrt(n_rows * places.n_lat * n_cols * places.n_lon)
    qkv_grad, out_grad, gain_grad, bias_grad = pl.pallas_call(
        functools.partial(unpack_kernel, counts, n_proj, factor),
        out_shape=(
            jax.ShapeDtypeStruct((n_chan, n_proj), f32),
            jax.ShapeDtypeStruct((n_chan, n_chan), f32),
            jax.ShapeDtypeStruct((1, n_chan), f32),
            jax.ShapeDtypeStruct(bias_table.shape, f32),
        ),
        in_specs=[smem] + [whole()] * (2 * places.x),
        scratch_shapes=[pltpu.VMEM((n_chan, LANES), f32)],
        compiler_params=pltpu.CompilerParams(vmem_limit_bytes=16 * MIB),
        name="unpack",
    )(meta, *mine, *other)
    return state_grad, qkv_grad, out_grad, gain_grad.reshape(n_chan), bias_grad


def solution(mesh):
    return jax.shard_map(
        local,
        mesh=mesh,
        in_specs=(P("lat", "lon", None), P("lat", "lon", None), P("lat"), P(), P(), P(), P(), P()),
        out_specs=(P("lat", "lon", None), P(), P(), P(), P()),
        check_vma=False,
    )
```

profile of v0, /device:TPU:1, one launch (start us, length us, event | category | flops | bytes accessed | tf_op | source)
XLA Modules:
  0.0 127.8 jit_solution(12457062086762762476)
XLA Ops:
  0.7 3.2 %pack.1 = (bf16[2,16,8,512]{3,2,1,0:T(8,128)(2,1)}, bf16[7,64,512]{2,1,0:T(8,128)(2,1)}, bf16[7,64,512]{2,1,0:T(8,128)(2,1)}, bf16[2,8,8,512]{3,2,1,0:T(8,128)(2,1)}) custom-call(bf16[16,64,512]{2,1,0:T(8,128)(2,1)} %x_ref.5, bf16[16,64,512]{2,1,0:T(8,128)(2,1)} %cot_ref.7, s32[16]{0:T(128)} %mask.1), custom_call_target="tpu_custom_call" | custom-call | tf_op jit(solution)/shard_map/pack/pallas_call | solution.py:483
  3.9 2.7 %collective-permute-start = (bf16[2,16,8,512]{3,2,1,0:T(8,128)(2,1)}, bf16[2,16,8,512]{3,2,1,0:T(8,128)(2,1)S(1)}, u32[]{:S(2)}, u32[]{:S(2)}) collective-permute-start(bf16[2,16,8,512]{3,2,1,0:T(8,128)(2,1)} %get-tuple-element.38), channel_id=1, source_target_pairs={{0,1},{1,2},{2,3},{3,4},{4,5},{5,6},{6,7},{7,8},{8,9},{9,10},{10,1... | collective-permute-start | bytes 786440 | tf_op jit(solution)/shard_map/ppermute | solution.py:468
  6.6 2.9 %collective-permute-start.1 = (bf16[7,64,512]{2,1,0:T(8,128)(2,1)}, bf16[7,64,512]{2,1,0:T(8,128)(2,1)}, u32[]{:S(2)}, u32[]{:S(2)}) collective-permute-start(bf16[7,64,512]{2,1,0:T(8,128)(2,1)} %get-tuple-element.42), channel_id=1, source_target_pairs={{0,16},{1,17},{2,18},{3,19},{4,20},{5,21},{6,22},{7,23},{8,24},{9,... | collective-permute-start | bytes 1376264 | tf_op jit(solution)/shard_map/ppermute | solution.py:468
  9.5 1.5 %collective-permute-start.2 = (bf16[2,8,8,512]{3,2,1,0:T(8,128)(2,1)}, bf16[2,8,8,512]{3,2,1,0:T(8,128)(2,1)S(1)}, u32[]{:S(2)}, u32[]{:S(2)}) collective-permute-start(bf16[2,8,8,512]{3,2,1,0:T(8,128)(2,1)} %get-tuple-element.43), channel_id=1, source_target_pairs={{0,17},{1,18},{2,19},{3,20},{4,21},{5,22},{6,23},{7,24},{8,25},{9,... | collective-permute-start | bytes 393224 | tf_op jit(solution)/shard_map/ppermute | solution.py:468
  11.0 2.9 %collective-permute-start.3 = (bf16[7,64,512]{2,1,0:T(8,128)(2,1)}, bf16[7,64,512]{2,1,0:T(8,128)(2,1)}, u32[]{:S(2)}, u32[]{:S(2)}) collective-permute-start(bf16[7,64,512]{2,1,0:T(8,128)(2,1)} %get-tuple-element.47), channel_id=1, source_target_pairs={{0,16},{1,17},{2,18},{3,19},{4,20},{5,21},{6,22},{7,23},{8,24},{9,... | collective-permute-start | bytes 1376264 | tf_op jit(solution)/shard_map/ppermute | solution.py:468
  14.0 0.7 copy-done.5
  14.7 0.8 prepare.1
  15.6 0.3 copy-done.2
  15.9 10.9 %inner.1 = (bf16[512,512]{1,0:T(8,128)(2,1)S(1)}, bf16[1536,512]{1,0:T(8,128)(2,1)S(1)}, f32[512,2048]{1,0:T(8,128)S(1)}, f32[16,64,128]{2,1,0:T(8,128)S(1)}) custom-call(s32[22]{0:T(128)S(1)} %concatenate.3.meta, bf16[16,64,512]{2,1,0:T(8,128)(2,1)S(1)} %copy-done.2, bf16[16,64,512]{2,1,0:T(8,128)(2,1)S(1)} %copy-done, ...), custom_call_target="tpu_custom_call" | custom-call | flops 8000000000 | bytes 16777216 | tf_op jit(solution)/shard_map/inner/pallas_call | solution.py:513
  26.9 0.6 collective-permute-done.2.corner_ref
  27.4 2.9 %front.1 = (bf16[512,512]{1,0:T(8,128)(2,1)S(1)}, bf16[512,512]{1,0:T(8,128)(2,1)S(1)}, bf16[1536,512]{1,0:T(8,128)(2,1)S(1)}, bf16[512,1024]{1,0:T(8,128)(2,1)S(1)}) custom-call(s32[22]{0:T(128)S(1)} %concatenate.3.meta, bf16[16,64,512]{2,1,0:T(8,128)(2,1)S(1)} %copy-done.2, bf16[2,16,8,512]{3,2,1,0:T(8,128)(2,1)S(1)} %collective-permute-done.side_ref, ...), custom_call_target="tpu_custom_call" | custom-call | flops 3000000000 | bytes 8388608 | tf_op jit(solution)/shard_map/front/pallas_call | solution.py:536
  30.3 8.1 %collective-permute-done.3.top = bf16[7,64,512]{2,1,0:T(8,128)(2,1)} collective-permute-done((bf16[7,64,512]{2,1,0:T(8,128)(2,1)}, bf16[7,64,512]{2,1,0:T(8,128)(2,1)}, u32[]{:S(2)}, u32[]{:S(2)}) %collective-permute-start.3) | collective-permute-done | bytes 458784 | tf_op jit(solution)/shard_map/ppermute | solution.py:468
  38.4 11.7 %outer.1 = (bf16[1536,512]{1,0:T(8,128)(2,1)S(1)}, f32[16,16,2176]{2,1,0:T(8,128)S(1)}, bf16[16,16,2176]{2,1,0:T(8,128)(2,1)S(1)}) custom-call(s32[22]{0:T(128)S(1)} %concatenate.3.meta, bf16[16,64,512]{2,1,0:T(8,128)(2,1)S(1)} %copy-done, bf16[2,16,8,512]{3,2,1,0:T(8,128)(2,1)S(1)} %collective-permute-done.side_ref, ...), custom_call_target="tpu_custom_call" | custom-call | flops 10000000000 | bytes 25165824 | tf_op jit(solution)/shard_map/outer/pallas_call | solution.py:549
  50.0 0.3 collective-permute-start.7
  50.4 2.7 %collective-permute-done.7.got_ref = bf16[16,16,2176]{2,1,0:T(8,128)(2,1)S(1)} collective-permute-done((bf16[16,16,2176]{2,1,0:T(8,128)(2,1)S(1)}, bf16[16,16,2176]{2,1,0:T(8,128)(2,1)S(1)}, u32[]{:S(2)}, u32[]{:S(2)}) %collective-permute-start.7) | collective-permute-done | bytes 1114144 | tf_op jit(solution)/shard_map/ppermute | solution.py:407
  53.1 0.2 add_c.1
  53.3 0.7 collective-permute-start.8
  54.0 2.5 %collective-permute-start.9 = (bf16[4,16,2176]{2,1,0:T(8,128)(2,1)S(1)}, bf16[4,16,2176]{2,1,0:T(8,128)(2,1)S(1)}, u32[]{:S(2)}, u32[]{:S(2)}) collective-permute-start(bf16[4,16,2176]{2,1,0:T(8,128)(2,1)S(1)} %get-tuple-element.61), channel_id=1, source_target_pairs={{0,4},{1,5},{2,6},{3,7},{4,0},{5,1},{6,2},{7,3},{8,12},{9,13},{10,... | collective-permute-start | bytes 835592 | tf_op jit(solution)/shard_map/ppermute | solution.py:407
  56.5 1.2 collective-permute-start.10
  57.7 3.7 %cells.1 = (bf16[16,64,512]{2,1,0:T(8,128)(2,1)S(1)}, bf16[7,64,512]{2,1,0:T(8,128)(2,1)S(1)}, bf16[16,8,512]{2,1,0:T(8,128)(2,1)S(1)}, bf16[7,8,512]{2,1,0:T(8,128)(2,1)S(1)}) custom-call(s32[22]{0:T(128)S(1)} %concatenate.3.meta, bf16[512,512]{1,0:T(8,128)(2,1)S(1)} %get-tuple-element.41.xi_ref, bf16[512,512]{1,0:T(8,128)(2,1)S(1)} %get-tuple-element.45.xo_ref, ...), custom_call_target="tpu_custom_call" | custom-call | flops 1600000000 | bytes 12582912 | tf_op jit(solution)/shard_map/cells/pallas_call | solution.py:572
  61.4 3.5 %collective-permute-start.4 = (bf16[7,64,512]{2,1,0:T(8,128)(2,1)S(1)}, bf16[7,64,512]{2,1,0:T(8,128)(2,1)S(1)}, u32[]{:S(2)}, u32[]{:S(2)}) collective-permute-start(bf16[7,64,512]{2,1,0:T(8,128)(2,1)S(1)} %get-tuple-element.54), channel_id=1, source_target_pairs={{0,240},{1,241},{2,242},{3,243},{4,244},{5,245},{6,246},{7,247},{8... | collective-permute-start | bytes 1376264 | tf_op jit(solution)/shard_map/ppermute | solution.py:468
  64.9 4.2 %collective-permute-done.9.refs_1_ = bf16[4,16,2176]{2,1,0:T(8,128)(2,1)S(1)} collective-permute-done((bf16[4,16,2176]{2,1,0:T(8,128)(2,1)S(1)}, bf16[4,16,2176]{2,1,0:T(8,128)(2,1)S(1)}, u32[]{:S(2)}, u32[]{:S(2)}) %collective-permute-start.9) | collective-permute-done | bytes 278560 | tf_op jit(solution)/shard_map/ppermute | solution.py:407
  69.0 0.1 add_x.1
  69.2 0.8 collective-permute-start.11
  70.0 2.5 %collective-permute-start.13 = (bf16[1,16,2176]{2,1,0:T(8,128)(2,1)S(1)}, bf16[1,16,2176]{2,1,0:T(8,128)(2,1)S(1)}, u32[]{:S(2)}, u32[]{:S(2)}) collective-permute-start(bf16[1,16,2176]{2,1,0:T(8,128)(2,1)S(1)} %get-tuple-element.66), channel_id=1, source_target_pairs={{0,24},{1,25},{2,26},{3,27},{4,28},{5,29},{6,30},{7,31},{8,0},{9,1... | collective-permute-start | bytes 208904 | tf_op jit(solution)/shard_map/ppermute | solution.py:407
  72.5 4.7 %collective-permute-done.11.refs_0_ = bf16[1,16,2176]{2,1,0:T(8,128)(2,1)S(1)} collective-permute-done((bf16[1,16,2176]{2,1,0:T(8,128)(2,1)S(1)}, bf16[1,16,2176]{2,1,0:T(8,128)(2,1)S(1)}, u32[]{:S(2)}, u32[]{:S(2)}) %collective-permute-start.11) | collective-permute-done | bytes 69664 | tf_op jit(solution)/shard_map/ppermute | solution.py:407
  77.4 3.1 %collective-permute-done.14.b_ref = bf16[1,16,2176]{2,1,0:T(8,128)(2,1)S(1)} collective-permute-done((bf16[1,16,2176]{2,1,0:T(8,128)(2,1)S(1)}, bf16[1,16,2176]{2,1,0:T(8,128)(2,1)S(1)}, u32[]{:S(2)}, u32[]{:S(2)}) %collective-permute-start.14) | collective-permute-done | bytes 69664 | tf_op jit(solution)/shard_map/ppermute | solution.py:407
  80.6 2.4 %collective-permute-start.15 = (bf16[1,16,2176]{2,1,0:T(8,128)(2,1)S(1)}, bf16[1,16,2176]{2,1,0:T(8,128)(2,1)S(1)}, u32[]{:S(2)}, u32[]{:S(2)}) collective-permute-start(bf16[1,16,2176]{2,1,0:T(8,128)(2,1)S(1)} %add_z.3.a_ref), channel_id=1, source_target_pairs={{0,64},{1,65},{2,66},{3,67},{4,68},{5,69},{6,70},{7,71},{8,72},{9,... | collective-permute-start | bytes 208904 | tf_op jit(solution)/shard_map/ppermute | solution.py:407
  83.0 1.7 %collective-permute-done.15.b_ref = bf16[1,16,2176]{2,1,0:T(8,128)(2,1)S(1)} collective-permute-done((bf16[1,16,2176]{2,1,0:T(8,128)(2,1)S(1)}, bf16[1,16,2176]{2,1,0:T(8,128)(2,1)S(1)}, u32[]{:S(2)}, u32[]{:S(2)}) %collective-permute-start.15) | collective-permute-done | bytes 69664 | tf_op jit(solution)/shard_map/ppermute | solution.py:407
  84.7 4.3 %collective-permute-start.16 = (bf16[1,16,2176]{2,1,0:T(8,128)(2,1)S(1)}, bf16[1,16,2176]{2,1,0:T(8,128)(2,1)S(1)}, u32[]{:S(2)}, u32[]{:S(2)}) collective-permute-start(bf16[1,16,2176]{2,1,0:T(8,128)(2,1)S(1)} %add_z.4.a_ref), channel_id=1, source_target_pairs={{0,192},{1,193},{2,194},{3,195},{4,196},{5,197},{6,198},{7,199},{8... | collective-permute-start | bytes 208904 | tf_op jit(solution)/shard_map/ppermute | solution.py:407
  89.1 3.5 %collective-permute-start.5 = (bf16[16,8,512]{2,1,0:T(8,128)(2,1)S(1)}, bf16[16,8,512]{2,1,0:T(8,128)(2,1)S(1)}, u32[]{:S(2)}, u32[]{:S(2)}) collective-permute-start(bf16[16,8,512]{2,1,0:T(8,128)(2,1)S(1)} %get-tuple-element.55), channel_id=1, source_target_pairs={{0,15},{1,0},{2,1},{3,2},{4,3},{5,4},{6,5},{7,6},{8,7},{9,8},{10,9... | collective-permute-start | bytes 393224 | tf_op jit(solution)/shard_map/ppermute | solution.py:468
  92.6 2.1 %collective-permute-start.6 = (bf16[7,8,512]{2,1,0:T(8,128)(2,1)S(1)}, bf16[7,8,512]{2,1,0:T(8,128)(2,1)S(1)}, u32[]{:S(2)}, u32[]{:S(2)}) collective-permute-start(bf16[7,8,512]{2,1,0:T(8,128)(2,1)S(1)} %get-tuple-element.56.refs_3_), channel_id=1, source_target_pairs={{0,255},{1,240},{2,241},{3,242},{4,243},{5,244},{6,245},{7,246},{8... | collective-permute-start | bytes 172040 | tf_op jit(solution)/shard_map/ppermute | solution.py:468
  94.7 0.9 collective-permute-start.17
  95.6 1.9 %collective-permute-start.18 = (bf16[1,16,2176]{2,1,0:T(8,128)(2,1)S(1)}, bf16[1,16,2176]{2,1,0:T(8,128)(2,1)S(1)}, u32[]{:S(2)}, u32[]{:S(2)}) collective-permute-start(bf16[1,16,2176]{2,1,0:T(8,128)(2,1)S(1)} %add_z.5.refs_0_), channel_id=1, source_target_pairs={{0,16},{1,17},{2,18},{3,19},{4,20},{5,21},{6,22},{7,23},{8,24},{9,... | collective-permute-start | bytes 208904 | tf_op jit(solution)/shard_map/ppermute | solution.py:407
  97.5 1.0 collective-permute-done.6.refs_6_
  98.6 0.5 collective-permute-start.19
  99.1 1.2 collective-permute-done.18.refs_2_
  100.3 4.6 %collective-permute-done.19.refs_3_ = bf16[1,16,2176]{2,1,0:T(8,128)(2,1)S(1)} collective-permute-done((bf16[1,16,2176]{2,1,0:T(8,128)(2,1)S(1)}, bf16[1,16,2176]{2,1,0:T(8,128)(2,1)S(1)}, u32[]{:S(2)}, u32[]{:S(2)}) %collective-permute-start.19) | collective-permute-done | bytes 69664 | tf_op jit(solution)/shard_map/ppermute | solution.py:407
  104.9 2.0 %collective-permute-start.20 = (bf16[4,16,2176]{2,1,0:T(8,128)(2,1)S(1)}, bf16[4,16,2176]{2,1,0:T(8,128)(2,1)S(1)}, u32[]{:S(2)}, u32[]{:S(2)}) collective-permute-start(bf16[4,16,2176]{2,1,0:T(8,128)(2,1)S(1)} %join.1.refs_0_), channel_id=1, source_target_pairs={{0,6},{1,7},{2,0},{3,1},{4,2},{5,3},{6,4},{7,5},{8,14},{9,15},{10,... | collective-permute-start | bytes 835592 | tf_op jit(solution)/shard_map/ppermute | solution.py:407
  106.9 0.3 collective-permute-start.21
  107.2 0.4 collective-permute-start.22
  107.6 1.2 collective-permute-start.23
  108.9 4.1 %collective-permute-done.20.refs_1_ = bf16[4,16,2176]{2,1,0:T(8,128)(2,1)S(1)} collective-permute-done((bf16[4,16,2176]{2,1,0:T(8,128)(2,1)S(1)}, bf16[4,16,2176]{2,1,0:T(8,128)(2,1)S(1)}, u32[]{:S(2)}, u32[]{:S(2)}) %collective-permute-start.20) | collective-permute-done | bytes 278560 | tf_op jit(solution)/shard_map/ppermute | solution.py:407
  113.0 6.8 %collective-permute-start.24 = (bf16[4,16,2176]{2,1,0:T(8,128)(2,1)S(1)}, bf16[4,16,2176]{2,1,0:T(8,128)(2,1)S(1)}, u32[]{:S(2)}, u32[]{:S(2)}) collective-permute-start(bf16[4,16,2176]{2,1,0:T(8,128)(2,1)S(1)} %collective-permute-done.20.refs_1_), channel_id=1, source_target_pairs={{0,1},{1,0},{2,3},{3,2},{4,5},{5,4},{6,7},{7,6},{8,9},{9,8},{10,11... | collective-permute-start | bytes 835592 | tf_op jit(solution)/shard_map/ppermute | solution.py:407
  119.8 3.2 %collective-permute-done.22.refs_3_ = bf16[4,16,2176]{2,1,0:T(8,128)(2,1)S(1)} collective-permute-done((bf16[4,16,2176]{2,1,0:T(8,128)(2,1)S(1)}, bf16[4,16,2176]{2,1,0:T(8,128)(2,1)S(1)}, u32[]{:S(2)}, u32[]{:S(2)}) %collective-permute-start.22) | collective-permute-done | bytes 278560 | tf_op jit(solution)/shard_map/ppermute | solution.py:407
  123.0 0.5 collective-permute-start.26
  123.5 1.2 add_convert_fusion
  124.7 3.1 %unpack.1 = (f32[512,1536]{1,0:T(8,128)}, f32[512,512]{1,0:T(8,128)}, f32[1,512]{1,0:T(1,128)}, f32[16,225]{1,0:T(8,128)}) custom-call(s32[22]{0:T(128)S(1)} %concatenate.3.meta, bf16[4,16,2176]{2,1,0:T(8,128)(2,1)S(1)} %join.1.refs_0_, bf16[4,16,2176]{2,1,0:T(8,128)(2,1)S(1)} %collective-permute-done.20.refs_1_, ...), custom_call_target="tpu_custom_call" | custom-call | tf_op jit(solution)/shard_map/unpack/pallas_call | solution.py:594
  (38 shorter events, 0.4 us)
Async XLA Ops:
  0.6 13.3 %copy-start.6 = (s32[16]{0:T(128)S(1)}, s32[16]{0:T(128)}, u32[]{:S(2)}) copy-start(s32[16]{0:T(128)} %mask.1) | copy-start | bytes 196
  0.6 13.3 %copy-start.7 = (s32[2]{0:T(128)S(1)}, s32[2]{0:T(128)}, u32[]{:S(2)}) copy-start(s32[2]{0:T(128)} %param.11) | copy-start | bytes 28
  0.7 13.3 %copy-start.1 = (bf16[512,1536]{1,0:T(8,128)(2,1)S(1)}, bf16[512,1536]{1,0:T(8,128)(2,1)}, u32[]{:S(2)}) copy-start(bf16[512,1536]{1,0:T(8,128)(2,1)} %w_ref.9) | copy-start | bytes 4718596
  3.9 11.7 %copy-start = (bf16[16,64,512]{2,1,0:T(8,128)(2,1)S(1)}, bf16[16,64,512]{2,1,0:T(8,128)(2,1)}, u32[]{:S(2)}) copy-start(bf16[16,64,512]{2,1,0:T(8,128)(2,1)} %cot_ref.7) | copy-start | bytes 3145732
  3.9 11.7 %copy-start.3 = (f32[512]{0:T(512)S(1)}, f32[512]{0:T(512)}, u32[]{:S(2)}) copy-start(f32[512]{0:T(512)} %param.12) | copy-start | bytes 6148
  3.9 11.7 %copy-start.4 = (bf16[512,512]{1,0:T(8,128)(2,1)S(1)}, bf16[512,512]{1,0:T(8,128)(2,1)}, u32[]{:S(2)}) copy-start(bf16[512,512]{1,0:T(8,128)(2,1)} %wo_ref.3) | copy-start | bytes 1572868
  3.9 11.7 %collective-permute-start = (bf16[2,16,8,512]{3,2,1,0:T(8,128)(2,1)}, bf16[2,16,8,512]{3,2,1,0:T(8,128)(2,1)S(1)}, u32[]{:S(2)}, u32[]{:S(2)}) collective-permute-start(bf16[2,16,8,512]{3,2,1,0:T(8,128)(2,1)} %get-tuple-element.38), channel_id=1, source_target_pairs={{0,1},{1,2},{2,3},{3,4},{4,5},{5,6},{6,7},{7,8},{8,9},{9,10},{10,1... | collective-permute-start | bytes 786440 | tf_op jit(solution)/shard_map/ppermute | solution.py:468
  6.6 20.9 %collective-permute-start.1 = (bf16[7,64,512]{2,1,0:T(8,128)(2,1)}, bf16[7,64,512]{2,1,0:T(8,128)(2,1)}, u32[]{:S(2)}, u32[]{:S(2)}) collective-permute-start(bf16[7,64,512]{2,1,0:T(8,128)(2,1)} %get-tuple-element.42), channel_id=1, source_target_pairs={{0,16},{1,17},{2,18},{3,19},{4,20},{5,21},{6,22},{7,23},{8,24},{9,... | collective-permute-start | bytes 1376264 | tf_op jit(solution)/shard_map/ppermute | solution.py:468
  9.5 17.9 %collective-permute-start.2 = (bf16[2,8,8,512]{3,2,1,0:T(8,128)(2,1)}, bf16[2,8,8,512]{3,2,1,0:T(8,128)(2,1)S(1)}, u32[]{:S(2)}, u32[]{:S(2)}) collective-permute-start(bf16[2,8,8,512]{3,2,1,0:T(8,128)(2,1)} %get-tuple-element.43), channel_id=1, source_target_pairs={{0,17},{1,18},{2,19},{3,20},{4,21},{5,22},{6,23},{7,24},{8,25},{9,... | collective-permute-start | bytes 393224 | tf_op jit(solution)/shard_map/ppermute | solution.py:468
  11.0 27.4 %collective-permute-start.3 = (bf16[7,64,512]{2,1,0:T(8,128)(2,1)}, bf16[7,64,512]{2,1,0:T(8,128)(2,1)}, u32[]{:S(2)}, u32[]{:S(2)}) collective-permute-start(bf16[7,64,512]{2,1,0:T(8,128)(2,1)} %get-tuple-element.47), channel_id=1, source_target_pairs={{0,16},{1,17},{2,18},{3,19},{4,20},{5,21},{6,22},{7,23},{8,24},{9,... | collective-permute-start | bytes 1376264 | tf_op jit(solution)/shard_map/ppermute | solution.py:468
  14.0 0.7 copy-start.5
  14.7 1.2 copy-start.2
  50.0 3.1 %collective-permute-start.7 = (bf16[16,16,2176]{2,1,0:T(8,128)(2,1)S(1)}, bf16[16,16,2176]{2,1,0:T(8,128)(2,1)S(1)}, u32[]{:S(2)}, u32[]{:S(2)}) collective-permute-start(bf16[16,16,2176]{2,1,0:T(8,128)(2,1)S(1)} %get-tuple-element.58), channel_id=1, source_target_pairs={{0,1},{1,0},{2,3},{3,2},{4,5},{5,4},{6,7},{7,6},{8,9},{9,8},{10,11... | collective-permute-start | bytes 3342344 | tf_op jit(solution)/shard_map/ppermute | solution.py:407
  53.3 11.6 %collective-permute-start.8 = (bf16[4,16,2176]{2,1,0:T(8,128)(2,1)S(1)}, bf16[4,16,2176]{2,1,0:T(8,128)(2,1)S(1)}, u32[]{:S(2)}, u32[]{:S(2)}) collective-permute-start(bf16[4,16,2176]{2,1,0:T(8,128)(2,1)S(1)} %get-tuple-element.60), channel_id=1, source_target_pairs={{0,2},{1,3},{2,4},{3,5},{4,6},{5,7},{6,0},{7,1},{8,10},{9,11},{10,... | collective-permute-start | bytes 835592 | tf_op jit(solution)/shard_map/ppermute | solution.py:407
  54.0 15.1 %collective-permute-start.9 = (bf16[4,16,2176]{2,1,0:T(8,128)(2,1)S(1)}, bf16[4,16,2176]{2,1,0:T(8,128)(2,1)S(1)}, u32[]{:S(2)}, u32[]{:S(2)}) collective-permute-start(bf16[4,16,2176]{2,1,0:T(8,128)(2,1)S(1)} %get-tuple-element.61), channel_id=1, source_target_pairs={{0,4},{1,5},{2,6},{3,7},{4,0},{5,1},{6,2},{7,3},{8,12},{9,13},{10,... | collective-permute-start | bytes 835592 | tf_op jit(solution)/shard_map/ppermute | solution.py:407
  56.5 12.6 %collective-permute-start.10 = (bf16[4,16,2176]{2,1,0:T(8,128)(2,1)S(1)}, bf16[4,16,2176]{2,1,0:T(8,128)(2,1)S(1)}, u32[]{:S(2)}, u32[]{:S(2)}) collective-permute-start(bf16[4,16,2176]{2,1,0:T(8,128)(2,1)S(1)} %get-tuple-element.62), channel_id=1, source_target_pairs={{0,6},{1,7},{2,0},{3,1},{4,2},{5,3},{6,4},{7,5},{8,14},{9,15},{10,... | collective-permute-start | bytes 835592 | tf_op jit(solution)/shard_map/ppermute | solution.py:407
  61.4 37.7 %collective-permute-start.4 = (bf16[7,64,512]{2,1,0:T(8,128)(2,1)S(1)}, bf16[7,64,512]{2,1,0:T(8,128)(2,1)S(1)}, u32[]{:S(2)}, u32[]{:S(2)}) collective-permute-start(bf16[7,64,512]{2,1,0:T(8,128)(2,1)S(1)} %get-tuple-element.54), channel_id=1, source_target_pairs={{0,240},{1,241},{2,242},{3,243},{4,244},{5,245},{6,246},{7,247},{8... | collective-permute-start | bytes 1376264 | tf_op jit(solution)/shard_map/ppermute | solution.py:468
  69.2 8.1 %collective-permute-start.11 = (bf16[1,16,2176]{2,1,0:T(8,128)(2,1)S(1)}, bf16[1,16,2176]{2,1,0:T(8,128)(2,1)S(1)}, u32[]{:S(2)}, u32[]{:S(2)}) collective-permute-start(bf16[1,16,2176]{2,1,0:T(8,128)(2,1)S(1)} %get-tuple-element.64), channel_id=1, source_target_pairs={{0,8},{1,9},{2,10},{3,11},{4,12},{5,13},{6,14},{7,15},{8,16},{9,17... | collective-permute-start | bytes 208904 | tf_op jit(solution)/shard_map/ppermute | solution.py:407
  70.0 7.2 %collective-permute-start.12 = (bf16[1,16,2176]{2,1,0:T(8,128)(2,1)S(1)}, bf16[1,16,2176]{2,1,0:T(8,128)(2,1)S(1)}, u32[]{:S(2)}, u32[]{:S(2)}) collective-permute-start(bf16[1,16,2176]{2,1,0:T(8,128)(2,1)S(1)} %get-tuple-element.65), channel_id=1, source_target_pairs={{0,16},{1,17},{2,18},{3,19},{4,20},{5,21},{6,22},{7,23},{8,24},{9,... | collective-permute-start | bytes 208904 | tf_op jit(solution)/shard_map/ppermute | solution.py:407
  70.0 7.2 %collective-permute-start.13 = (bf16[1,16,2176]{2,1,0:T(8,128)(2,1)S(1)}, bf16[1,16,2176]{2,1,0:T(8,128)(2,1)S(1)}, u32[]{:S(2)}, u32[]{:S(2)}) collective-permute-start(bf16[1,16,2176]{2,1,0:T(8,128)(2,1)S(1)} %get-tuple-element.66), channel_id=1, source_target_pairs={{0,24},{1,25},{2,26},{3,27},{4,28},{5,29},{6,30},{7,31},{8,0},{9,1... | collective-permute-start | bytes 208904 | tf_op jit(solution)/shard_map/ppermute | solution.py:407
  77.3 3.2 %collective-permute-start.14 = (bf16[1,16,2176]{2,1,0:T(8,128)(2,1)S(1)}, bf16[1,16,2176]{2,1,0:T(8,128)(2,1)S(1)}, u32[]{:S(2)}, u32[]{:S(2)}) collective-permute-start(bf16[1,16,2176]{2,1,0:T(8,128)(2,1)S(1)} %add_y.1.a_ref), channel_id=1, source_target_pairs={{0,32},{1,33},{2,34},{3,35},{4,36},{5,37},{6,38},{7,39},{8,40},{9,... | collective-permute-start | bytes 208904 | tf_op jit(solution)/shard_map/ppermute | solution.py:407
  80.6 4.1 %collective-permute-start.15 = (bf16[1,16,2176]{2,1,0:T(8,128)(2,1)S(1)}, bf16[1,16,2176]{2,1,0:T(8,128)(2,1)S(1)}, u32[]{:S(2)}, u32[]{:S(2)}) collective-permute-start(bf16[1,16,2176]{2,1,0:T(8,128)(2,1)S(1)} %add_z.3.a_ref), channel_id=1, source_target_pairs={{0,64},{1,65},{2,66},{3,67},{4,68},{5,69},{6,70},{7,71},{8,72},{9,... | collective-permute-start | bytes 208904 | tf_op jit(solution)/shard_map/ppermute | solution.py:407
  84.7 10.0 %collective-permute-start.16 = (bf16[1,16,2176]{2,1,0:T(8,128)(2,1)S(1)}, bf16[1,16,2176]{2,1,0:T(8,128)(2,1)S(1)}, u32[]{:S(2)}, u32[]{:S(2)}) collective-permute-start(bf16[1,16,2176]{2,1,0:T(8,128)(2,1)S(1)} %add_z.4.a_ref), channel_id=1, source_target_pairs={{0,192},{1,193},{2,194},{3,195},{4,196},{5,197},{6,198},{7,199},{8... | collective-permute-start | bytes 208904 | tf_op jit(solution)/shard_map/ppermute | solution.py:407
  89.1 10.0 %collective-permute-start.5 = (bf16[16,8,512]{2,1,0:T(8,128)(2,1)S(1)}, bf16[16,8,512]{2,1,0:T(8,128)(2,1)S(1)}, u32[]{:S(2)}, u32[]{:S(2)}) collective-permute-start(bf16[16,8,512]{2,1,0:T(8,128)(2,1)S(1)} %get-tuple-element.55), channel_id=1, source_target_pairs={{0,15},{1,0},{2,1},{3,2},{4,3},{5,4},{6,5},{7,6},{8,7},{9,8},{10,9... | collective-permute-start | bytes 393224 | tf_op jit(solution)/shard_map/ppermute | solution.py:468
  92.6 6.0 %collective-permute-start.6 = (bf16[7,8,512]{2,1,0:T(8,128)(2,1)S(1)}, bf16[7,8,512]{2,1,0:T(8,128)(2,1)S(1)}, u32[]{:S(2)}, u32[]{:S(2)}) collective-permute-start(bf16[7,8,512]{2,1,0:T(8,128)(2,1)S(1)} %get-tuple-element.56.refs_3_), channel_id=1, source_target_pairs={{0,255},{1,240},{2,241},{3,242},{4,243},{5,244},{6,245},{7,246},{8... | collective-permute-start | bytes 172040 | tf_op jit(solution)/shard_map/ppermute | solution.py:468
  94.7 4.4 %collective-permute-start.17 = (bf16[1,16,2176]{2,1,0:T(8,128)(2,1)S(1)}, bf16[1,16,2176]{2,1,0:T(8,128)(2,1)S(1)}, u32[]{:S(2)}, u32[]{:S(2)}) collective-permute-start(bf16[1,16,2176]{2,1,0:T(8,128)(2,1)S(1)} %add_z.5.refs_0_), channel_id=1, source_target_pairs={{0,24},{1,25},{2,26},{3,27},{4,28},{5,29},{6,30},{7,31},{8,0},{9,1... | collective-permute-start | bytes 208904 | tf_op jit(solution)/shard_map/ppermute | solution.py:407
  95.6 4.7 %collective-permute-start.18 = (bf16[1,16,2176]{2,1,0:T(8,128)(2,1)S(1)}, bf16[1,16,2176]{2,1,0:T(8,128)(2,1)S(1)}, u32[]{:S(2)}, u32[]{:S(2)}) collective-permute-start(bf16[1,16,2176]{2,1,0:T(8,128)(2,1)S(1)} %add_z.5.refs_0_), channel_id=1, source_target_pairs={{0,16},{1,17},{2,18},{3,19},{4,20},{5,21},{6,22},{7,23},{8,24},{9,... | collective-permute-start | bytes 208904 | tf_op jit(solution)/shard_map/ppermute | solution.py:407
  98.6 6.3 %collective-permute-start.19 = (bf16[1,16,2176]{2,1,0:T(8,128)(2,1)S(1)}, bf16[1,16,2176]{2,1,0:T(8,128)(2,1)S(1)}, u32[]{:S(2)}, u32[]{:S(2)}) collective-permute-start(bf16[1,16,2176]{2,1,0:T(8,128)(2,1)S(1)} %add_z.5.refs_0_), channel_id=1, source_target_pairs={{0,8},{1,9},{2,10},{3,11},{4,12},{5,13},{6,14},{7,15},{8,16},{9,17... | collective-permute-start | bytes 208904 | tf_op jit(solution)/shard_map/ppermute | solution.py:407
  104.9 8.2 %collective-permute-start.20 = (bf16[4,16,2176]{2,1,0:T(8,128)(2,1)S(1)}, bf16[4,16,2176]{2,1,0:T(8,128)(2,1)S(1)}, u32[]{:S(2)}, u32[]{:S(2)}) collective-permute-start(bf16[4,16,2176]{2,1,0:T(8,128)(2,1)S(1)} %join.1.refs_0_), channel_id=1, source_target_pairs={{0,6},{1,7},{2,0},{3,1},{4,2},{5,3},{6,4},{7,5},{8,14},{9,15},{10,... | collective-permute-start | bytes 835592 | tf_op jit(solution)/shard_map/ppermute | solution.py:407
  106.9 12.9 %collective-permute-start.21 = (bf16[4,16,2176]{2,1,0:T(8,128)(2,1)S(1)}, bf16[4,16,2176]{2,1,0:T(8,128)(2,1)S(1)}, u32[]{:S(2)}, u32[]{:S(2)}) collective-permute-start(bf16[4,16,2176]{2,1,0:T(8,128)(2,1)S(1)} %join.1.refs_0_), channel_id=1, source_target_pairs={{0,4},{1,5},{2,6},{3,7},{4,0},{5,1},{6,2},{7,3},{8,12},{9,13},{10,... | collective-permute-start | bytes 835592 | tf_op jit(solution)/shard_map/ppermute | solution.py:407
  107.2 15.8 %collective-permute-start.22 = (bf16[4,16,2176]{2,1,0:T(8,128)(2,1)S(1)}, bf16[4,16,2176]{2,1,0:T(8,128)(2,1)S(1)}, u32[]{:S(2)}, u32[]{:S(2)}) collective-permute-start(bf16[4,16,2176]{2,1,0:T(8,128)(2,1)S(1)} %join.1.refs_0_), channel_id=1, source_target_pairs={{0,2},{1,3},{2,4},{3,5},{4,6},{5,7},{6,0},{7,1},{8,10},{9,11},{10,... | collective-permute-start | bytes 835592 | tf_op jit(solution)/shard_map/ppermute | solution.py:407
  107.6 17.0 %collective-permute-start.23 = (bf16[4,16,2176]{2,1,0:T(8,128)(2,1)S(1)}, bf16[4,16,2176]{2,1,0:T(8,128)(2,1)S(1)}, u32[]{:S(2)}, u32[]{:S(2)}) collective-permute-start(bf16[4,16,2176]{2,1,0:T(8,128)(2,1)S(1)} %join.1.refs_0_), channel_id=1, source_target_pairs={{0,1},{1,0},{2,3},{3,2},{4,5},{5,4},{6,7},{7,6},{8,9},{9,8},{10,11... | collective-permute-start | bytes 835592 | tf_op jit(solution)/shard_map/ppermute | solution.py:407
  113.0 11.6 %collective-permute-start.24 = (bf16[4,16,2176]{2,1,0:T(8,128)(2,1)S(1)}, bf16[4,16,2176]{2,1,0:T(8,128)(2,1)S(1)}, u32[]{:S(2)}, u32[]{:S(2)}) collective-permute-start(bf16[4,16,2176]{2,1,0:T(8,128)(2,1)S(1)} %collective-permute-done.20.refs_1_), channel_id=1, source_target_pairs={{0,1},{1,0},{2,3},{3,2},{4,5},{5,4},{6,7},{7,6},{8,9},{9,8},{10,11... | collective-permute-start | bytes 835592 | tf_op jit(solution)/shard_map/ppermute | solution.py:407
  119.8 4.9 %collective-permute-start.25 = (bf16[4,16,2176]{2,1,0:T(8,128)(2,1)S(1)}, bf16[4,16,2176]{2,1,0:T(8,128)(2,1)S(1)}, u32[]{:S(2)}, u32[]{:S(2)}) collective-permute-start(bf16[4,16,2176]{2,1,0:T(8,128)(2,1)S(1)} %collective-permute-done.21.refs_2_), channel_id=1, source_target_pairs={{0,1},{1,0},{2,3},{3,2},{4,5},{5,4},{6,7},{7,6},{8,9},{9,8},{10,11... | collective-permute-start | bytes 835592 | tf_op jit(solution)/shard_map/ppermute | solution.py:407
  123.0 1.7 %collective-permute-start.26 = (bf16[4,16,2176]{2,1,0:T(8,128)(2,1)S(1)}, bf16[4,16,2176]{2,1,0:T(8,128)(2,1)S(1)}, u32[]{:S(2)}, u32[]{:S(2)}) collective-permute-start(bf16[4,16,2176]{2,1,0:T(8,128)(2,1)S(1)} %collective-permute-done.22.refs_3_), channel_id=1, source_target_pairs={{0,1},{1,0},{2,3},{3,2},{4,5},{5,4},{6,7},{7,6},{8,9},{9,8},{10,11... | collective-permute-start | bytes 835592 | tf_op jit(solution)/shard_map/ppermute | solution.py:407
where the time goes:
time: 128 us
  starting transfers between devices  48.5 us (38%)
  waiting for transfers between devices  39.3 us (31%)
  Pallas kernels  36.8 us (29%)
    ppermute x20, waiting for transfers between devices, move(): return lax.ppermute(array, ('lat', 'lon'), pairs)  29.6 us
    ppermute x20, starting transfers between devices, move(): return lax.ppermute(array, ('lat', 'lon'), pairs)  29.4 us
    ppermute x7, starting transfers between devices, ring(): return lax.ppermute(array, ('lat', 'lon'), pairs)  19.1 us
    pallas_call x1, Pallas kernels, local(): pl.pallas_call(functools.partial(outer_kernel, n_head, counts), out_shape...  11.7 us
    pallas_call x1, Pallas kernels, local(): pl.pallas_call(functools.partial(inner_kernel, n_head), out_shape=(tile((...  10.9 us
    ppermute x7, waiting for transfers between devices, ring(): return lax.ppermute(array, ('lat', 'lon'), pairs)  9.67 us
    pallas_call x1, Pallas kernels, local(): pl.pallas_call(cells_kernel, out_shape=(tile((n_rows, n_cols, n_chan)), t...  3.75 us
    pallas_call x1, Pallas kernels, local(): pl.pallas_call(functools.partial(pack_kernel, n_top), out_shape=(tile((2,...  3.19 us
  transfers between devices with their start and end apart: 27, of which 12 were waited for; matrix products, arithmetic and copies ran while one was open for 1% of the time, Pallas kernels for 15%

commit v1 on v0

--- a/solution.py
+++ b/solution.py
@@ -234,7 +234,7 @@
     return jnp.broadcast_to(gain_ref[...], (LANES, n_chan)).T[:, :1]
 
 
-def cells_kernel(meta, xi_ref, xo_ref, gpi_ref, gpo_ref, cot_ref, gain_ref, w_ref, base_ref, top_ref, side_ref, corner_ref, ext):
+def cells_kernel(meta, xi_ref, xo_ref, gpi_ref, gpo_ref, cot_ref, gain_ref, w_ref, _, base_ref, top_ref, side_ref, ext):
     n_rows, n_cols, n_chan = cot_ref.shape
     lat, lon = meta[0], meta[1]
     ext[...] = jnp.zeros_like(ext)
@@ -264,8 +264,17 @@
         side_ref[r] = ext[WINDOW + r, :WINDOW].astype(jnp.bfloat16)
     n_top = top_ref.shape[0]
     for r in range(n_top):
-        top_ref[r] = ext[WINDOW - n_top + r, WINDOW:].astype(jnp.bfloat16)
-        corner_ref[r] = ext[WINDOW - n_top + r, :WINDOW].astype(jnp.bfloat16)
+        top_ref[r] = ext[WINDOW - n_top + r].astype(jnp.bfloat16)
+
+
+def edge_kernel(side_ref, top_ref, _, out_ref):
+    n_rows, n_top = side_ref.shape[0], top_ref.shape[0]
+    for r in range(n_rows):
+        edge = side_ref[r].astype(jnp.float32)
+        at = r - n_rows + n_top
+        if at >= 0:
+            edge = edge + top_ref[at].astype(jnp.float32)[:WINDOW]
+        out_ref[r] = edge.astype(jnp.bfloat16)
 
 
 def prepare_kernel(bias_ref, w_ref, full_ref, wt_ref):
@@ -346,8 +355,11 @@
         refs[-1][k : k + 1] = refs[k][...]
 
 
-def pair_add_kernel(a_ref, b_ref, *refs):
-    refs[-1][...] = (a_ref[...].astype(jnp.float32) + b_ref[...].astype(jnp.float32)).astype(jnp.bfloat16)
+def tree_add_kernel(*refs):
+    parts = [ref[...].astype(jnp.float32) for ref in refs[:-1]]
+    while len(parts) > 1:
+        parts = [parts[k] + parts[k + 1] for k in range(0, len(parts), 2)]
+    refs[-1][...] = parts[0].astype(jnp.bfloat16)
 
 
 def unpack_kernel(counts, n_proj, factor, meta, *refs):
@@ -428,7 +440,7 @@
     )(*args)
 
 
-def total_over_devices(places, keep, send, ahead, behind):
+def total_over_devices(places, keep, send, beside):
     shape = keep.shape[1:]
     bf = functools.partial(jax.ShapeDtypeStruct, dtype=jnp.bfloat16)
     got = places.by_c(send)
@@ -436,6 +448,7 @@
     own, *sends = small_call(first_add_kernel, (own,) + (bf((places.y, *shape)),) * (places.x - 1), "add_c", 12, keep, got)
     got = [places.by_x(part, k + 1) for k, part in enumerate(sends)]
     nxt = jax.ShapeDtypeStruct((1, *shape), jnp.float32)
+    ahead, finish = beside(own)
     own, *sends = pl.pallas_call(
         functools.partial(next_add_kernel, len(got), 1),
         out_shape=(nxt,) + (bf((1, *shape)),) * (places.y - 1),
@@ -445,19 +458,14 @@
     )(own, *got, ahead)
     got = [places.by_y(part, k + 1) for k, part in enumerate(sends)]
     (mine,) = small_call(functools.partial(next_add_kernel, len(got), 0), (bf((1, *shape)),), "add_y", 4, own, *got)
-    for bits in {1: (), 2: (1,), 4: (1, 3), 8: (1, 2, 6)}[places.z]:
-        other = places.by_z(mine, bits)
-        mine = small_call(pair_add_kernel, bf((1, *shape)), "add_z", 2, mine, other)
+    for group in {1: (), 2: ((1,),), 4: ((1, 2, 3),), 8: ((1, 2, 3), (6,))}[places.z]:
+        others = [places.by_z(mine, bits) for bits in group]
+        mine = small_call(tree_add_kernel, bf((1, *shape)), "add_z", 2, mine, *others)
     parts = [mine] + [places.by_y(mine, -k) for k in range(1, places.y)]
-    mine = pl.pallas_call(
-        functools.partial(join_kernel, len(parts)),
-        out_shape=bf((places.y, *shape)),
-        in_specs=[whole()] * len(parts) + [pl.BlockSpec(memory_space=pl.ANY)] * len(behind),
-        compiler_params=pltpu.CompilerParams(vmem_limit_bytes=4 * MIB),
-        name="join",
-    )(*parts, *behind)
+    mine = small_call(functools.partial(join_kernel, len(parts)), bf((places.y, *shape)), "join", 4, *parts)
+    result = finish(mine)
     mine = [mine] + [places.by_x(mine, -k) for k in range(1, places.x)]
-    return mine, [places.by_c(part) for part in mine]
+    return mine, [places.by_c(part) for part in mine], result
 
 
 def ring(array, lat, lon):
@@ -569,25 +577,37 @@
         name="outer",
     )(meta, cotangent, side, top_c, corner, bias, gain, w_qkv, w_out, nrm_out, proj_out, kv_out, sums_in, bsum_in)
 
-    base, *edges = pl.pallas_call(
-        cells_kernel,
-        out_shape=(
-            tile((n_rows, n_cols, n_chan)),
-            tile((n_top, n_cols, n_chan)),
-            tile((n_rows, WINDOW, n_chan)),
-            tile((n_top, WINDOW, n_chan)),
-        ),
-        in_specs=[smem] + [whole()] * 7,
-        scratch_shapes=[pltpu.VMEM((n_rows + WINDOW, n_cols + WINDOW, n_chan), f32)],
-        compiler_params=pltpu.CompilerParams(vmem_limit_bytes=24 * MIB),
-        cost_estimate=pl.CostEstimate(flops=16 * 10**8, bytes_accessed=12 * MIB, transcendentals=0),
-        name="cells",
-    )(meta, x_in, x_out, gp_in, gp_out, cotangent, gain, w_qkv)
-    top_back, side_back, corner_back = ring(edges[0], -1, 0), ring(edges[1], 0, -1), ring(edges[2], -1, -1)
-    mine, other = total_over_devices(places, keep, send, edges[2], (top_back, side_back, corner_back))
-    edge = jnp.pad(top_back, ((n_rows - n_top, 0), (0, 0), (0, 0)))
+    def input_grad(start):
+        base, *edges = pl.pallas_call(
+            cells_kernel,
+            out_shape=(
+                tile((n_rows, n_cols, n_chan)),
+                tile((n_top, n_cols + WINDOW, n_chan)),
+                tile((n_rows, WINDOW, n_chan)),
+            ),
+            in_specs=[smem] + [whole()] * 7 + [pl.BlockSpec(memory_space=pl.ANY)],
+            scratch_shapes=[pltpu.VMEM((n_rows + WINDOW, n_cols + WINDOW, n_chan), f32)],
+            compiler_params=pltpu.CompilerParams(vmem_limit_bytes=24 * MIB),
+            cost_estimate=pl.CostEstimate(flops=16 * 10**8, bytes_accessed=12 * MIB, transcendentals=0),
+            name="cells",
+        )(meta, x_in, x_out, gp_in, gp_out, cotangent, gain, w_qkv, start)
+        top_back = ring(edges[0], -1, 0)
+
+        def finish(later):
+            side = pl.pallas_call(
+                edge_kernel,
+                out_shape=tile((n_rows, WINDOW, n_chan)),
+                in_specs=[whole()] * 2 + [pl.BlockSpec(memory_space=pl.ANY)],
+                compiler_params=pltpu.CompilerParams(vmem_limit_bytes=4 * MIB),
+                name="edge",
+            )(edges[1], top_back, later)
+            return base, top_back, ring(side, 0, -1)
+
+        return edges[1], finish
+
+    mine, other, (base, top_back, side_back) = total_over_devices(places, keep, send, input_grad)
+    edge = jnp.pad(top_back[:, WINDOW:], ((n_rows - n_top, 0), (0, 0), (0, 0)))
     edge = edge + jnp.pad(side_back, ((0, 0), (n_cols - WINDOW, 0), (0, 0)))
-    edge = edge + jnp.pad(corner_back, ((n_rows - n_top, 0), (n_cols - WINDOW, 0), (0, 0)))
     state_grad = (base.astype(f32) + edge.astype(f32)).astype(bf)
 
     factor = 1.0 / math.sqrt(n_rows * places.n_lat * n_cols * places.n_lon)

time: 128 us -> 123 us (0.961)
  waiting for transfers between devices: 39.3 us -> 33 us
    ppermute x20 -> x21, waiting for transfers between devices: 29.6 us -> 24.3 us  [move(): return lax.ppermute(array, ('lat', 'lon'), pairs)]
    ppermute x20 -> x21, starting transfers between devices: 29.4 us -> 30.4 us  [move(): return lax.ppermute(array, ('lat', 'lon'), pairs)]
    ppermute x7 -> x6, waiting for transfers between devices: 9.67 us -> 8.63 us  [ring(): return lax.ppermute(array, ('lat', 'lon'), pairs)]
    ppermute x7 -> x6, starting transfers between devices: 19.1 us -> 18.9 us  [ring(): return lax.ppermute(array, ('lat', 'lon'), pairs)]
  transfers between devices with their start and end apart: 27 -> 27, of which waited for: 12 -> 11; matrix products, arithmetic and copies ran while one was open for 1% -> 1% of each run, Pallas kernels for 15% -> 15%
where the time goes in v1:
time: 123 us; the launch traced here: 122 us
  starting transfers between devices  49.3 us (40%)
  Pallas kernels  36.8 us (30%)
  waiting for transfers between devices  33 us (27%)
    ppermute x21, starting transfers between devices, move(): return lax.ppermute(array, ('lat', 'lon'), pairs)  30.4 us
    ppermute x21, waiting for transfers between devices, move(): return lax.ppermute(array, ('lat', 'lon'), pairs)  24.3 us
    ppermute x6, starting transfers between devices, ring(): return lax.ppermute(array, ('lat', 'lon'), pairs)  18.9 us
    pallas_call x1, Pallas kernels, local(): pl.pallas_call(functools.partial(outer_kernel, n_head, counts), out_shape...  11.7 us
    pallas_call x1, Pallas kernels, local(): pl.pallas_call(functools.partial(inner_kernel, n_head), out_shape=(tile((...  10.9 us
    ppermute x6, waiting for transfers between devices, ring(): return lax.ppermute(array, ('lat', 'lon'), pairs)  8.63 us
    pallas_call x1, Pallas kernels, input_grad(): pl.pallas_call(cells_kernel, out_shape=(tile((n_rows, n_cols, n_chan)), t...  3.74 us
    pallas_call x1, Pallas kernels, local(): pl.pallas_call(functools.partial(pack_kernel, n_top), out_shape=(tile((2,...  3.19 us
  transfers between devices with their start and end apart: 27, of which 11 were waited for; matrix products, arithmetic and copies ran while one was open for 1% of the time, Pallas kernels for 15%

profile of v1, /device:TPU:1, one launch (start us, length us, event | category | flops | bytes accessed | tf_op | source)
XLA Modules:
  0.0 122.3 jit_solution(13975313876079287651)
XLA Ops:
  0.7 3.2 %pack.1 = (bf16[2,16,8,512]{3,2,1,0:T(8,128)(2,1)}, bf16[7,64,512]{2,1,0:T(8,128)(2,1)}, bf16[7,64,512]{2,1,0:T(8,128)(2,1)}, bf16[2,8,8,512]{3,2,1,0:T(8,128)(2,1)}) custom-call(bf16[16,64,512]{2,1,0:T(8,128)(2,1)} %x_ref.5, bf16[16,64,512]{2,1,0:T(8,128)(2,1)} %cot_ref.7, s32[16]{0:T(128)} %mask.1), custom_call_target="tpu_custom_call" | custom-call | tf_op jit(solution)/shard_map/pack/pallas_call | solution.py:491
  3.9 2.7 %collective-permute-start = (bf16[2,16,8,512]{3,2,1,0:T(8,128)(2,1)}, bf16[2,16,8,512]{3,2,1,0:T(8,128)(2,1)S(1)}, u32[]{:S(2)}, u32[]{:S(2)}) collective-permute-start(bf16[2,16,8,512]{3,2,1,0:T(8,128)(2,1)} %get-tuple-element.37), channel_id=1, source_target_pairs={{0,1},{1,2},{2,3},{3,4},{4,5},{5,6},{6,7},{7,8},{8,9},{9,10},{10,1... | collective-permute-start | bytes 786440 | tf_op jit(solution)/shard_map/ppermute | solution.py:476
  6.6 2.9 %collective-permute-start.1 = (bf16[7,64,512]{2,1,0:T(8,128)(2,1)}, bf16[7,64,512]{2,1,0:T(8,128)(2,1)}, u32[]{:S(2)}, u32[]{:S(2)}) collective-permute-start(bf16[7,64,512]{2,1,0:T(8,128)(2,1)} %get-tuple-element.41), channel_id=1, source_target_pairs={{0,16},{1,17},{2,18},{3,19},{4,20},{5,21},{6,22},{7,23},{8,24},{9,... | collective-permute-start | bytes 1376264 | tf_op jit(solution)/shard_map/ppermute | solution.py:476
  9.5 1.5 %collective-permute-start.2 = (bf16[2,8,8,512]{3,2,1,0:T(8,128)(2,1)}, bf16[2,8,8,512]{3,2,1,0:T(8,128)(2,1)S(1)}, u32[]{:S(2)}, u32[]{:S(2)}) collective-permute-start(bf16[2,8,8,512]{3,2,1,0:T(8,128)(2,1)} %get-tuple-element.42), channel_id=1, source_target_pairs={{0,17},{1,18},{2,19},{3,20},{4,21},{5,22},{6,23},{7,24},{8,25},{9,... | collective-permute-start | bytes 393224 | tf_op jit(solution)/shard_map/ppermute | solution.py:476
  11.0 2.9 %collective-permute-start.3 = (bf16[7,64,512]{2,1,0:T(8,128)(2,1)}, bf16[7,64,512]{2,1,0:T(8,128)(2,1)}, u32[]{:S(2)}, u32[]{:S(2)}) collective-permute-start(bf16[7,64,512]{2,1,0:T(8,128)(2,1)} %get-tuple-element.46), channel_id=1, source_target_pairs={{0,16},{1,17},{2,18},{3,19},{4,20},{5,21},{6,22},{7,23},{8,24},{9,... | collective-permute-start | bytes 1376264 | tf_op jit(solution)/shard_map/ppermute | solution.py:476
  13.9 0.1 concatenate.3.meta
  14.0 0.7 copy-done.5
  14.7 0.8 prepare.1
  15.6 0.3 copy-done.2
  15.9 10.9 %inner.1 = (bf16[512,512]{1,0:T(8,128)(2,1)S(1)}, bf16[1536,512]{1,0:T(8,128)(2,1)S(1)}, f32[512,2048]{1,0:T(8,128)S(1)}, f32[16,64,128]{2,1,0:T(8,128)S(1)}) custom-call(s32[22]{0:T(128)S(1)} %concatenate.3.meta, bf16[16,64,512]{2,1,0:T(8,128)(2,1)S(1)} %copy-done.2, bf16[16,64,512]{2,1,0:T(8,128)(2,1)S(1)} %copy-done, ...), custom_call_target="tpu_custom_call" | custom-call | flops 8000000000 | bytes 16777216 | tf_op jit(solution)/shard_map/inner/pallas_call | solution.py:521
  26.9 0.6 collective-permute-done.2.corner_ref
  27.4 2.9 %front.1 = (bf16[512,512]{1,0:T(8,128)(2,1)S(1)}, bf16[512,512]{1,0:T(8,128)(2,1)S(1)}, bf16[1536,512]{1,0:T(8,128)(2,1)S(1)}, bf16[512,1024]{1,0:T(8,128)(2,1)S(1)}) custom-call(s32[22]{0:T(128)S(1)} %concatenate.3.meta, bf16[16,64,512]{2,1,0:T(8,128)(2,1)S(1)} %copy-done.2, bf16[2,16,8,512]{3,2,1,0:T(8,128)(2,1)S(1)} %collective-permute-done.side_ref, ...), custom_call_target="tpu_custom_call" | custom-call | flops 3000000000 | bytes 8388608 | tf_op jit(solution)/shard_map/front/pallas_call | solution.py:544
  30.3 8.1 %collective-permute-done.3.top = bf16[7,64,512]{2,1,0:T(8,128)(2,1)} collective-permute-done((bf16[7,64,512]{2,1,0:T(8,128)(2,1)}, bf16[7,64,512]{2,1,0:T(8,128)(2,1)}, u32[]{:S(2)}, u32[]{:S(2)}) %collective-permute-start.3) | collective-permute-done | bytes 458784 | tf_op jit(solution)/shard_map/ppermute | solution.py:476
  38.4 11.7 %outer.1 = (bf16[1536,512]{1,0:T(8,128)(2,1)S(1)}, f32[16,16,2176]{2,1,0:T(8,128)S(1)}, bf16[16,16,2176]{2,1,0:T(8,128)(2,1)S(1)}) custom-call(s32[22]{0:T(128)S(1)} %concatenate.3.meta, bf16[16,64,512]{2,1,0:T(8,128)(2,1)S(1)} %copy-done, bf16[2,16,8,512]{3,2,1,0:T(8,128)(2,1)S(1)} %collective-permute-done.side_ref, ...), custom_call_target="tpu_custom_call" | custom-call | flops 10000000000 | bytes 25165824 | tf_op jit(solution)/shard_map/outer/pallas_call | solution.py:557
  50.0 0.3 collective-permute-start.4
  50.4 2.7 %collective-permute-done.4.got_ref = bf16[16,16,2176]{2,1,0:T(8,128)(2,1)S(1)} collective-permute-done((bf16[16,16,2176]{2,1,0:T(8,128)(2,1)S(1)}, bf16[16,16,2176]{2,1,0:T(8,128)(2,1)S(1)}, u32[]{:S(2)}, u32[]{:S(2)}) %collective-permute-start.4) | collective-permute-done | bytes 1114144 | tf_op jit(solution)/shard_map/ppermute | solution.py:419
  53.1 0.2 add_c.1
  53.3 0.7 collective-permute-start.6
  54.0 2.5 %collective-permute-start.7 = (bf16[4,16,2176]{2,1,0:T(8,128)(2,1)S(1)}, bf16[4,16,2176]{2,1,0:T(8,128)(2,1)S(1)}, u32[]{:S(2)}, u32[]{:S(2)}) collective-permute-start(bf16[4,16,2176]{2,1,0:T(8,128)(2,1)S(1)} %get-tuple-element.59), channel_id=1, source_target_pairs={{0,4},{1,5},{2,6},{3,7},{4,0},{5,1},{6,2},{7,3},{8,12},{9,13},{10,... | collective-permute-start | bytes 835592 | tf_op jit(solution)/shard_map/ppermute | solution.py:419
  56.5 1.2 collective-permute-start.8
  57.7 3.7 %cells.1 = (bf16[16,64,512]{2,1,0:T(8,128)(2,1)S(1)}, bf16[7,72,512]{2,1,0:T(8,128)(2,1)S(1)}, bf16[16,8,512]{2,1,0:T(8,128)(2,1)S(1)}) custom-call(s32[22]{0:T(128)S(1)} %concatenate.3.meta, bf16[512,512]{1,0:T(8,128)(2,1)S(1)} %get-tuple-element.40.xi_ref, bf16[512,512]{1,0:T(8,128)(2,1)S(1)} %get-tuple-element.44.xo_ref, ...), custom_call_target="tpu_custom_call" | custom-call | flops 1600000000 | bytes 12582912 | tf_op jit(solution)/shard_map/cells/pallas_call | solution.py:581
  61.4 3.5 %collective-permute-start.5 = (bf16[7,72,512]{2,1,0:T(8,128)(2,1)S(1)}, bf16[7,72,512]{2,1,0:T(8,128)(2,1)S(1)}, u32[]{:S(2)}, u32[]{:S(2)}) collective-permute-start(bf16[7,72,512]{2,1,0:T(8,128)(2,1)S(1)} %get-tuple-element.56), channel_id=1, source_target_pairs={{0,240},{1,241},{2,242},{3,243},{4,244},{5,245},{6,246},{7,247},{8... | collective-permute-start | bytes 1548296 | tf_op jit(solution)/shard_map/ppermute | solution.py:476
  64.9 4.2 %collective-permute-done.7.refs_1_ = bf16[4,16,2176]{2,1,0:T(8,128)(2,1)S(1)} collective-permute-done((bf16[4,16,2176]{2,1,0:T(8,128)(2,1)S(1)}, bf16[4,16,2176]{2,1,0:T(8,128)(2,1)S(1)}, u32[]{:S(2)}, u32[]{:S(2)}) %collective-permute-start.7) | collective-permute-done | bytes 278560 | tf_op jit(solution)/shard_map/ppermute | solution.py:419
  69.0 0.1 add_x.1
  69.2 0.8 collective-permute-start.9
  70.0 2.5 %collective-permute-start.11 = (bf16[1,16,2176]{2,1,0:T(8,128)(2,1)S(1)}, bf16[1,16,2176]{2,1,0:T(8,128)(2,1)S(1)}, u32[]{:S(2)}, u32[]{:S(2)}) collective-permute-start(bf16[1,16,2176]{2,1,0:T(8,128)(2,1)S(1)} %get-tuple-element.64), channel_id=1, source_target_pairs={{0,24},{1,25},{2,26},{3,27},{4,28},{5,29},{6,30},{7,31},{8,0},{9,1... | collective-permute-start | bytes 208904 | tf_op jit(solution)/shard_map/ppermute | solution.py:419
  72.5 6.4 %collective-permute-done.9.refs_0_ = bf16[1,16,2176]{2,1,0:T(8,128)(2,1)S(1)} collective-permute-done((bf16[1,16,2176]{2,1,0:T(8,128)(2,1)S(1)}, bf16[1,16,2176]{2,1,0:T(8,128)(2,1)S(1)}, u32[]{:S(2)}, u32[]{:S(2)}) %collective-permute-start.9) | collective-permute-done | bytes 69664 | tf_op jit(solution)/shard_map/ppermute | solution.py:419
  78.9 0.1 collective-permute-start.12
  79.0 3.5 %collective-permute-start.13 = (bf16[1,16,2176]{2,1,0:T(8,128)(2,1)S(1)}, bf16[1,16,2176]{2,1,0:T(8,128)(2,1)S(1)}, u32[]{:S(2)}, u32[]{:S(2)}) collective-permute-start(bf16[1,16,2176]{2,1,0:T(8,128)(2,1)S(1)} %add_y.1.refs_0_), channel_id=1, source_target_pairs={{0,64},{1,65},{2,66},{3,67},{4,68},{5,69},{6,70},{7,71},{8,72},{9,... | collective-permute-start | bytes 208904 | tf_op jit(solution)/shard_map/ppermute | solution.py:419
  82.6 1.8 %collective-permute-done.13.refs_2_ = bf16[1,16,2176]{2,1,0:T(8,128)(2,1)S(1)} collective-permute-done((bf16[1,16,2176]{2,1,0:T(8,128)(2,1)S(1)}, bf16[1,16,2176]{2,1,0:T(8,128)(2,1)S(1)}, u32[]{:S(2)}, u32[]{:S(2)}) %collective-permute-start.13) | collective-permute-done | bytes 69664 | tf_op jit(solution)/shard_map/ppermute | solution.py:419
  84.4 3.1 %collective-permute-done.14.refs_3_ = bf16[1,16,2176]{2,1,0:T(8,128)(2,1)S(1)} collective-permute-done((bf16[1,16,2176]{2,1,0:T(8,128)(2,1)S(1)}, bf16[1,16,2176]{2,1,0:T(8,128)(2,1)S(1)}, u32[]{:S(2)}, u32[]{:S(2)}) %collective-permute-start.14) | collective-permute-done | bytes 69664 | tf_op jit(solution)/shard_map/ppermute | solution.py:419
  87.5 4.4 %collective-permute-start.15 = (bf16[1,16,2176]{2,1,0:T(8,128)(2,1)S(1)}, bf16[1,16,2176]{2,1,0:T(8,128)(2,1)S(1)}, u32[]{:S(2)}, u32[]{:S(2)}) collective-permute-start(bf16[1,16,2176]{2,1,0:T(8,128)(2,1)S(1)} %add_z.2.refs_0_), channel_id=1, source_target_pairs={{0,192},{1,193},{2,194},{3,195},{4,196},{5,197},{6,198},{7,199},{8... | collective-permute-start | bytes 208904 | tf_op jit(solution)/shard_map/ppermute | solution.py:419
  91.9 1.8 %collective-permute-done.15.refs_1_ = bf16[1,16,2176]{2,1,0:T(8,128)(2,1)S(1)} collective-permute-done((bf16[1,16,2176]{2,1,0:T(8,128)(2,1)S(1)}, bf16[1,16,2176]{2,1,0:T(8,128)(2,1)S(1)}, u32[]{:S(2)}, u32[]{:S(2)}) %collective-permute-start.15) | collective-permute-done | bytes 69664 | tf_op jit(solution)/shard_map/ppermute | solution.py:419
  93.7 2.4 %collective-permute-start.16 = (bf16[1,16,2176]{2,1,0:T(8,128)(2,1)S(1)}, bf16[1,16,2176]{2,1,0:T(8,128)(2,1)S(1)}, u32[]{:S(2)}, u32[]{:S(2)}) collective-permute-start(bf16[1,16,2176]{2,1,0:T(8,128)(2,1)S(1)} %add_z.3.refs_0_), channel_id=1, source_target_pairs={{0,24},{1,25},{2,26},{3,27},{4,28},{5,29},{6,30},{7,31},{8,0},{9,1... | collective-permute-start | bytes 208904 | tf_op jit(solution)/shard_map/ppermute | solution.py:419
  96.1 0.8 collective-permute-start.18
  96.9 0.6 collective-permute-done.16.refs_1_
  97.5 3.4 %collective-permute-done.17.refs_2_ = bf16[1,16,2176]{2,1,0:T(8,128)(2,1)S(1)} collective-permute-done((bf16[1,16,2176]{2,1,0:T(8,128)(2,1)S(1)}, bf16[1,16,2176]{2,1,0:T(8,128)(2,1)S(1)}, u32[]{:S(2)}, u32[]{:S(2)}) %collective-permute-start.17) | collective-permute-done | bytes 69664 | tf_op jit(solution)/shard_map/ppermute | solution.py:419
  100.9 0.4 collective-permute-done.18.refs_3_
  101.3 0.1 collective-permute-start.20
  101.4 2.4 %collective-permute-start.21 = (bf16[4,16,2176]{2,1,0:T(8,128)(2,1)S(1)}, bf16[4,16,2176]{2,1,0:T(8,128)(2,1)S(1)}, u32[]{:S(2)}, u32[]{:S(2)}) collective-permute-start(bf16[4,16,2176]{2,1,0:T(8,128)(2,1)S(1)} %join.1._.refs_0_), channel_id=1, source_target_pairs={{0,4},{1,5},{2,6},{3,7},{4,0},{5,1},{6,2},{7,3},{8,12},{9,13},{10,... | collective-permute-start | bytes 835592 | tf_op jit(solution)/shard_map/ppermute | solution.py:419
  103.7 0.8 collective-permute-start.22
  104.5 5.5 %collective-permute-start.19 = (bf16[16,8,512]{2,1,0:T(8,128)(2,1)S(1)}, bf16[16,8,512]{2,1,0:T(8,128)(2,1)S(1)}, u32[]{:S(2)}, u32[]{:S(2)}) collective-permute-start(bf16[16,8,512]{2,1,0:T(8,128)(2,1)S(1)} %edge.1), channel_id=1, source_target_pairs={{0,15},{1,0},{2,1},{3,2},{4,3},{5,4},{6,5},{7,6},{8,7},{9,8},{10,9... | collective-permute-start | bytes 393224 | tf_op jit(solution)/shard_map/ppermute | solution.py:476
  110.0 0.1 collective-permute-start.23
  110.1 3.3 %collective-permute-start.24 = (bf16[4,16,2176]{2,1,0:T(8,128)(2,1)S(1)}, bf16[4,16,2176]{2,1,0:T(8,128)(2,1)S(1)}, u32[]{:S(2)}, u32[]{:S(2)}) collective-permute-start(bf16[4,16,2176]{2,1,0:T(8,128)(2,1)S(1)} %collective-permute-done.20.refs_1_), channel_id=1, source_target_pairs={{0,1},{1,0},{2,3},{3,2},{4,5},{5,4},{6,7},{7,6},{8,9},{9,8},{10,11... | collective-permute-start | bytes 835592 | tf_op jit(solution)/shard_map/ppermute | solution.py:419
  113.4 1.7 %collective-permute-start.25 = (bf16[4,16,2176]{2,1,0:T(8,128)(2,1)S(1)}, bf16[4,16,2176]{2,1,0:T(8,128)(2,1)S(1)}, u32[]{:S(2)}, u32[]{:S(2)}) collective-permute-start(bf16[4,16,2176]{2,1,0:T(8,128)(2,1)S(1)} %collective-permute-done.21.refs_2_), channel_id=1, source_target_pairs={{0,1},{1,0},{2,3},{3,2},{4,5},{5,4},{6,7},{7,6},{8,9},{9,8},{10,11... | collective-permute-start | bytes 835592 | tf_op jit(solution)/shard_map/ppermute | solution.py:419
  115.1 2.9 %collective-permute-start.26 = (bf16[4,16,2176]{2,1,0:T(8,128)(2,1)S(1)}, bf16[4,16,2176]{2,1,0:T(8,128)(2,1)S(1)}, u32[]{:S(2)}, u32[]{:S(2)}) collective-permute-start(bf16[4,16,2176]{2,1,0:T(8,128)(2,1)S(1)} %collective-permute-done.22.refs_3_), channel_id=1, source_target_pairs={{0,1},{1,0},{2,3},{3,2},{4,5},{5,4},{6,7},{7,6},{8,9},{9,8},{10,11... | collective-permute-start | bytes 835592 | tf_op jit(solution)/shard_map/ppermute | solution.py:419
  118.0 1.2 add_convert_fusion
  119.2 3.1 %unpack.1 = (f32[512,1536]{1,0:T(8,128)}, f32[512,512]{1,0:T(8,128)}, f32[1,512]{1,0:T(1,128)}, f32[16,225]{1,0:T(8,128)}) custom-call(s32[22]{0:T(128)S(1)} %concatenate.3.meta, bf16[4,16,2176]{2,1,0:T(8,128)(2,1)S(1)} %join.1._.refs_0_, bf16[4,16,2176]{2,1,0:T(8,128)(2,1)S(1)} %collective-permute-done.20.refs_1_, ...), custom_call_target="tpu_custom_call" | custom-call | tf_op jit(solution)/shard_map/unpack/pallas_call | solution.py:614
  (39 shorter events, 0.4 us)
Async XLA Ops:
  0.6 13.3 %copy-start.6 = (s32[16]{0:T(128)S(1)}, s32[16]{0:T(128)}, u32[]{:S(2)}) copy-start(s32[16]{0:T(128)} %mask.1) | copy-start | bytes 196
  0.6 13.3 %copy-start.7 = (s32[2]{0:T(128)S(1)}, s32[2]{0:T(128)}, u32[]{:S(2)}) copy-start(s32[2]{0:T(128)} %param.11) | copy-start | bytes 28
  0.7 13.3 %copy-start.1 = (bf16[512,1536]{1,0:T(8,128)(2,1)S(1)}, bf16[512,1536]{1,0:T(8,128)(2,1)}, u32[]{:S(2)}) copy-start(bf16[512,1536]{1,0:T(8,128)(2,1)} %w_ref.9) | copy-start | bytes 4718596
  3.9 11.7 %copy-start = (bf16[16,64,512]{2,1,0:T(8,128)(2,1)S(1)}, bf16[16,64,512]{2,1,0:T(8,128)(2,1)}, u32[]{:S(2)}) copy-start(bf16[16,64,512]{2,1,0:T(8,128)(2,1)} %cot_ref.7) | copy-start | bytes 3145732
  3.9 11.7 %copy-start.3 = (f32[512]{0:T(512)S(1)}, f32[512]{0:T(512)}, u32[]{:S(2)}) copy-start(f32[512]{0:T(512)} %param.12) | copy-start | bytes 6148
  3.9 11.7 %copy-start.4 = (bf16[512,512]{1,0:T(8,128)(2,1)S(1)}, bf16[512,512]{1,0:T(8,128)(2,1)}, u32[]{:S(2)}) copy-start(bf16[512,512]{1,0:T(8,128)(2,1)} %wo_ref.3) | copy-start | bytes 1572868
  3.9 11.7 %collective-permute-start = (bf16[2,16,8,512]{3,2,1,0:T(8,128)(2,1)}, bf16[2,16,8,512]{3,2,1,0:T(8,128)(2,1)S(1)}, u32[]{:S(2)}, u32[]{:S(2)}) collective-permute-start(bf16[2,16,8,512]{3,2,1,0:T(8,128)(2,1)} %get-tuple-element.37), channel_id=1, source_target_pairs={{0,1},{1,2},{2,3},{3,4},{4,5},{5,6},{6,7},{7,8},{8,9},{9,10},{10,1... | collective-permute-start | bytes 786440 | tf_op jit(solution)/shard_map/ppermute | solution.py:476
  6.6 20.9 %collective-permute-start.1 = (bf16[7,64,512]{2,1,0:T(8,128)(2,1)}, bf16[7,64,512]{2,1,0:T(8,128)(2,1)}, u32[]{:S(2)}, u32[]{:S(2)}) collective-permute-start(bf16[7,64,512]{2,1,0:T(8,128)(2,1)} %get-tuple-element.41), channel_id=1, source_target_pairs={{0,16},{1,17},{2,18},{3,19},{4,20},{5,21},{6,22},{7,23},{8,24},{9,... | collective-permute-start | bytes 1376264 | tf_op jit(solution)/shard_map/ppermute | solution.py:476
  9.5 17.9 %collective-permute-start.2 = (bf16[2,8,8,512]{3,2,1,0:T(8,128)(2,1)}, bf16[2,8,8,512]{3,2,1,0:T(8,128)(2,1)S(1)}, u32[]{:S(2)}, u32[]{:S(2)}) collective-permute-start(bf16[2,8,8,512]{3,2,1,0:T(8,128)(2,1)} %get-tuple-element.42), channel_id=1, source_target_pairs={{0,17},{1,18},{2,19},{3,20},{4,21},{5,22},{6,23},{7,24},{8,25},{9,... | collective-permute-start | bytes 393224 | tf_op jit(solution)/shard_map/ppermute | solution.py:476
  11.0 27.4 %collective-permute-start.3 = (bf16[7,64,512]{2,1,0:T(8,128)(2,1)}, bf16[7,64,512]{2,1,0:T(8,128)(2,1)}, u32[]{:S(2)}, u32[]{:S(2)}) collective-permute-start(bf16[7,64,512]{2,1,0:T(8,128)(2,1)} %get-tuple-element.46), channel_id=1, source_target_pairs={{0,16},{1,17},{2,18},{3,19},{4,20},{5,21},{6,22},{7,23},{8,24},{9,... | collective-permute-start | bytes 1376264 | tf_op jit(solution)/shard_map/ppermute | solution.py:476
  14.0 0.7 copy-start.5
  14.7 1.2 %copy-start.2 = (bf16[16,64,512]{2,1,0:T(8,128)(2,1)S(1)}, bf16[16,64,512]{2,1,0:T(8,128)(2,1)}, u32[]{:S(2)}) copy-start(bf16[16,64,512]{2,1,0:T(8,128)(2,1)} %x_ref.5) | copy-start | bytes 3145732
  50.0 3.1 %collective-permute-start.4 = (bf16[16,16,2176]{2,1,0:T(8,128)(2,1)S(1)}, bf16[16,16,2176]{2,1,0:T(8,128)(2,1)S(1)}, u32[]{:S(2)}, u32[]{:S(2)}) collective-permute-start(bf16[16,16,2176]{2,1,0:T(8,128)(2,1)S(1)} %get-tuple-element.53), channel_id=1, source_target_pairs={{0,1},{1,0},{2,3},{3,2},{4,5},{5,4},{6,7},{7,6},{8,9},{9,8},{10,11... | collective-permute-start | bytes 3342344 | tf_op jit(solution)/shard_map/ppermute | solution.py:419
  53.3 11.6 %collective-permute-start.6 = (bf16[4,16,2176]{2,1,0:T(8,128)(2,1)S(1)}, bf16[4,16,2176]{2,1,0:T(8,128)(2,1)S(1)}, u32[]{:S(2)}, u32[]{:S(2)}) collective-permute-start(bf16[4,16,2176]{2,1,0:T(8,128)(2,1)S(1)} %get-tuple-element.58), channel_id=1, source_target_pairs={{0,2},{1,3},{2,4},{3,5},{4,6},{5,7},{6,0},{7,1},{8,10},{9,11},{10,... | collective-permute-start | bytes 835592 | tf_op jit(solution)/shard_map/ppermute | solution.py:419
  54.0 15.1 %collective-permute-start.7 = (bf16[4,16,2176]{2,1,0:T(8,128)(2,1)S(1)}, bf16[4,16,2176]{2,1,0:T(8,128)(2,1)S(1)}, u32[]{:S(2)}, u32[]{:S(2)}) collective-permute-start(bf16[4,16,2176]{2,1,0:T(8,128)(2,1)S(1)} %get-tuple-element.59), channel_id=1, source_target_pairs={{0,4},{1,5},{2,6},{3,7},{4,0},{5,1},{6,2},{7,3},{8,12},{9,13},{10,... | collective-permute-start | bytes 835592 | tf_op jit(solution)/shard_map/ppermute | solution.py:419
  56.5 12.6 %collective-permute-start.8 = (bf16[4,16,2176]{2,1,0:T(8,128)(2,1)S(1)}, bf16[4,16,2176]{2,1,0:T(8,128)(2,1)S(1)}, u32[]{:S(2)}, u32[]{:S(2)}) collective-permute-start(bf16[4,16,2176]{2,1,0:T(8,128)(2,1)S(1)} %get-tuple-element.60), channel_id=1, source_target_pairs={{0,6},{1,7},{2,0},{3,1},{4,2},{5,3},{6,4},{7,5},{8,14},{9,15},{10,... | collective-permute-start | bytes 835592 | tf_op jit(solution)/shard_map/ppermute | solution.py:419
  61.4 43.1 %collective-permute-start.5 = (bf16[7,72,512]{2,1,0:T(8,128)(2,1)S(1)}, bf16[7,72,512]{2,1,0:T(8,128)(2,1)S(1)}, u32[]{:S(2)}, u32[]{:S(2)}) collective-permute-start(bf16[7,72,512]{2,1,0:T(8,128)(2,1)S(1)} %get-tuple-element.56), channel_id=1, source_target_pairs={{0,240},{1,241},{2,242},{3,243},{4,244},{5,245},{6,246},{7,247},{8... | collective-permute-start | bytes 1548296 | tf_op jit(solution)/shard_map/ppermute | solution.py:476
  69.2 9.7 %collective-permute-start.9 = (bf16[1,16,2176]{2,1,0:T(8,128)(2,1)S(1)}, bf16[1,16,2176]{2,1,0:T(8,128)(2,1)S(1)}, u32[]{:S(2)}, u32[]{:S(2)}) collective-permute-start(bf16[1,16,2176]{2,1,0:T(8,128)(2,1)S(1)} %get-tuple-element.62), channel_id=1, source_target_pairs={{0,8},{1,9},{2,10},{3,11},{4,12},{5,13},{6,14},{7,15},{8,16},{9,17... | collective-permute-start | bytes 208904 | tf_op jit(solution)/shard_map/ppermute | solution.py:419
  70.0 8.9 %collective-permute-start.10 = (bf16[1,16,2176]{2,1,0:T(8,128)(2,1)S(1)}, bf16[1,16,2176]{2,1,0:T(8,128)(2,1)S(1)}, u32[]{:S(2)}, u32[]{:S(2)}) collective-permute-start(bf16[1,16,2176]{2,1,0:T(8,128)(2,1)S(1)} %get-tuple-element.63), channel_id=1, source_target_pairs={{0,16},{1,17},{2,18},{3,19},{4,20},{5,21},{6,22},{7,23},{8,24},{9,... | collective-permute-start | bytes 208904 | tf_op jit(solution)/shard_map/ppermute | solution.py:419
  70.0 8.9 %collective-permute-start.11 = (bf16[1,16,2176]{2,1,0:T(8,128)(2,1)S(1)}, bf16[1,16,2176]{2,1,0:T(8,128)(2,1)S(1)}, u32[]{:S(2)}, u32[]{:S(2)}) collective-permute-start(bf16[1,16,2176]{2,1,0:T(8,128)(2,1)S(1)} %get-tuple-element.64), channel_id=1, source_target_pairs={{0,24},{1,25},{2,26},{3,27},{4,28},{5,29},{6,30},{7,31},{8,0},{9,1... | collective-permute-start | bytes 208904 | tf_op jit(solution)/shard_map/ppermute | solution.py:419
  78.9 3.6 %collective-permute-start.12 = (bf16[1,16,2176]{2,1,0:T(8,128)(2,1)S(1)}, bf16[1,16,2176]{2,1,0:T(8,128)(2,1)S(1)}, u32[]{:S(2)}, u32[]{:S(2)}) collective-permute-start(bf16[1,16,2176]{2,1,0:T(8,128)(2,1)S(1)} %add_y.1.refs_0_), channel_id=1, source_target_pairs={{0,32},{1,33},{2,34},{3,35},{4,36},{5,37},{6,38},{7,39},{8,40},{9,... | collective-permute-start | bytes 208904 | tf_op jit(solution)/shard_map/ppermute | solution.py:419
  79.0 5.3 %collective-permute-start.13 = (bf16[1,16,2176]{2,1,0:T(8,128)(2,1)S(1)}, bf16[1,16,2176]{2,1,0:T(8,128)(2,1)S(1)}, u32[]{:S(2)}, u32[]{:S(2)}) collective-permute-start(bf16[1,16,2176]{2,1,0:T(8,128)(2,1)S(1)} %add_y.1.refs_0_), channel_id=1, source_target_pairs={{0,64},{1,65},{2,66},{3,67},{4,68},{5,69},{6,70},{7,71},{8,72},{9,... | collective-permute-start | bytes 208904 | tf_op jit(solution)/shard_map/ppermute | solution.py:419
  82.5 5.0 %collective-permute-start.14 = (bf16[1,16,2176]{2,1,0:T(8,128)(2,1)S(1)}, bf16[1,16,2176]{2,1,0:T(8,128)(2,1)S(1)}, u32[]{:S(2)}, u32[]{:S(2)}) collective-permute-start(bf16[1,16,2176]{2,1,0:T(8,128)(2,1)S(1)} %add_y.1.refs_0_), channel_id=1, source_target_pairs={{0,96},{1,97},{2,98},{3,99},{4,100},{5,101},{6,102},{7,103},{8,104... | collective-permute-start | bytes 208904 | tf_op jit(solution)/shard_map/ppermute | solution.py:419
  87.5 6.2 %collective-permute-start.15 = (bf16[1,16,2176]{2,1,0:T(8,128)(2,1)S(1)}, bf16[1,16,2176]{2,1,0:T(8,128)(2,1)S(1)}, u32[]{:S(2)}, u32[]{:S(2)}) collective-permute-start(bf16[1,16,2176]{2,1,0:T(8,128)(2,1)S(1)} %add_z.2.refs_0_), channel_id=1, source_target_pairs={{0,192},{1,193},{2,194},{3,195},{4,196},{5,197},{6,198},{7,199},{8... | collective-permute-start | bytes 208904 | tf_op jit(solution)/shard_map/ppermute | solution.py:419
  93.7 3.8 %collective-permute-start.16 = (bf16[1,16,2176]{2,1,0:T(8,128)(2,1)S(1)}, bf16[1,16,2176]{2,1,0:T(8,128)(2,1)S(1)}, u32[]{:S(2)}, u32[]{:S(2)}) collective-permute-start(bf16[1,16,2176]{2,1,0:T(8,128)(2,1)S(1)} %add_z.3.refs_0_), channel_id=1, source_target_pairs={{0,24},{1,25},{2,26},{3,27},{4,28},{5,29},{6,30},{7,31},{8,0},{9,1... | collective-permute-start | bytes 208904 | tf_op jit(solution)/shard_map/ppermute | solution.py:419
  96.1 4.8 %collective-permute-start.17 = (bf16[1,16,2176]{2,1,0:T(8,128)(2,1)S(1)}, bf16[1,16,2176]{2,1,0:T(8,128)(2,1)S(1)}, u32[]{:S(2)}, u32[]{:S(2)}) collective-permute-start(bf16[1,16,2176]{2,1,0:T(8,128)(2,1)S(1)} %add_z.3.refs_0_), channel_id=1, source_target_pairs={{0,16},{1,17},{2,18},{3,19},{4,20},{5,21},{6,22},{7,23},{8,24},{9,... | collective-permute-start | bytes 208904 | tf_op jit(solution)/shard_map/ppermute | solution.py:419
  96.1 5.1 %collective-permute-start.18 = (bf16[1,16,2176]{2,1,0:T(8,128)(2,1)S(1)}, bf16[1,16,2176]{2,1,0:T(8,128)(2,1)S(1)}, u32[]{:S(2)}, u32[]{:S(2)}) collective-permute-start(bf16[1,16,2176]{2,1,0:T(8,128)(2,1)S(1)} %add_z.3.refs_0_), channel_id=1, source_target_pairs={{0,8},{1,9},{2,10},{3,11},{4,12},{5,13},{6,14},{7,15},{8,16},{9,17... | collective-permute-start | bytes 208904 | tf_op jit(solution)/shard_map/ppermute | solution.py:419
  101.3 8.8 %collective-permute-start.20 = (bf16[4,16,2176]{2,1,0:T(8,128)(2,1)S(1)}, bf16[4,16,2176]{2,1,0:T(8,128)(2,1)S(1)}, u32[]{:S(2)}, u32[]{:S(2)}) collective-permute-start(bf16[4,16,2176]{2,1,0:T(8,128)(2,1)S(1)} %join.1._.refs_0_), channel_id=1, source_target_pairs={{0,6},{1,7},{2,0},{3,1},{4,2},{5,3},{6,4},{7,5},{8,14},{9,15},{10,... | collective-permute-start | bytes 835592 | tf_op jit(solution)/shard_map/ppermute | solution.py:419
  101.4 12.0 %collective-permute-start.21 = (bf16[4,16,2176]{2,1,0:T(8,128)(2,1)S(1)}, bf16[4,16,2176]{2,1,0:T(8,128)(2,1)S(1)}, u32[]{:S(2)}, u32[]{:S(2)}) collective-permute-start(bf16[4,16,2176]{2,1,0:T(8,128)(2,1)S(1)} %join.1._.refs_0_), channel_id=1, source_target_pairs={{0,4},{1,5},{2,6},{3,7},{4,0},{5,1},{6,2},{7,3},{8,12},{9,13},{10,... | collective-permute-start | bytes 835592 | tf_op jit(solution)/shard_map/ppermute | solution.py:419
  103.7 11.4 %collective-permute-start.22 = (bf16[4,16,2176]{2,1,0:T(8,128)(2,1)S(1)}, bf16[4,16,2176]{2,1,0:T(8,128)(2,1)S(1)}, u32[]{:S(2)}, u32[]{:S(2)}) collective-permute-start(bf16[4,16,2176]{2,1,0:T(8,128)(2,1)S(1)} %join.1._.refs_0_), channel_id=1, source_target_pairs={{0,2},{1,3},{2,4},{3,5},{4,6},{5,7},{6,0},{7,1},{8,10},{9,11},{10,... | collective-permute-start | bytes 835592 | tf_op jit(solution)/shard_map/ppermute | solution.py:419
  104.5 13.5 %collective-permute-start.19 = (bf16[16,8,512]{2,1,0:T(8,128)(2,1)S(1)}, bf16[16,8,512]{2,1,0:T(8,128)(2,1)S(1)}, u32[]{:S(2)}, u32[]{:S(2)}) collective-permute-start(bf16[16,8,512]{2,1,0:T(8,128)(2,1)S(1)} %edge.1), channel_id=1, source_target_pairs={{0,15},{1,0},{2,1},{3,2},{4,3},{5,4},{6,5},{7,6},{8,7},{9,8},{10,9... | collective-permute-start | bytes 393224 | tf_op jit(solution)/shard_map/ppermute | solution.py:476
  110.0 9.3 %collective-permute-start.23 = (bf16[4,16,2176]{2,1,0:T(8,128)(2,1)S(1)}, bf16[4,16,2176]{2,1,0:T(8,128)(2,1)S(1)}, u32[]{:S(2)}, u32[]{:S(2)}) collective-permute-start(bf16[4,16,2176]{2,1,0:T(8,128)(2,1)S(1)} %join.1._.refs_0_), channel_id=1, source_target_pairs={{0,1},{1,0},{2,3},{3,2},{4,5},{5,4},{6,7},{7,6},{8,9},{9,8},{10,11... | collective-permute-start | bytes 835592 | tf_op jit(solution)/shard_map/ppermute | solution.py:419
  110.1 9.2 %collective-permute-start.24 = (bf16[4,16,2176]{2,1,0:T(8,128)(2,1)S(1)}, bf16[4,16,2176]{2,1,0:T(8,128)(2,1)S(1)}, u32[]{:S(2)}, u32[]{:S(2)}) collective-permute-start(bf16[4,16,2176]{2,1,0:T(8,128)(2,1)S(1)} %collective-permute-done.20.refs_1_), channel_id=1, source_target_pairs={{0,1},{1,0},{2,3},{3,2},{4,5},{5,4},{6,7},{7,6},{8,9},{9,8},{10,11... | collective-permute-start | bytes 835592 | tf_op jit(solution)/shard_map/ppermute | solution.py:419
  113.4 5.8 %collective-permute-start.25 = (bf16[4,16,2176]{2,1,0:T(8,128)(2,1)S(1)}, bf16[4,16,2176]{2,1,0:T(8,128)(2,1)S(1)}, u32[]{:S(2)}, u32[]{:S(2)}) collective-permute-start(bf16[4,16,2176]{2,1,0:T(8,128)(2,1)S(1)} %collective-permute-done.21.refs_2_), channel_id=1, source_target_pairs={{0,1},{1,0},{2,3},{3,2},{4,5},{5,4},{6,7},{7,6},{8,9},{9,8},{10,11... | collective-permute-start | bytes 835592 | tf_op jit(solution)/shard_map/ppermute | solution.py:419
  115.1 4.1 %collective-permute-start.26 = (bf16[4,16,2176]{2,1,0:T(8,128)(2,1)S(1)}, bf16[4,16,2176]{2,1,0:T(8,128)(2,1)S(1)}, u32[]{:S(2)}, u32[]{:S(2)}) collective-permute-start(bf16[4,16,2176]{2,1,0:T(8,128)(2,1)S(1)} %collective-permute-done.22.refs_3_), channel_id=1, source_target_pairs={{0,1},{1,0},{2,3},{3,2},{4,5},{5,4},{6,7},{7,6},{8,9},{9,8},{10,11... | collective-permute-start | bytes 835592 | tf_op jit(solution)/shard_map/ppermute | solution.py:419

commit v2 on v1

--- a/solution.py
+++ b/solution.py
@@ -69,8 +69,10 @@
     g_t = gm_t[pl.ds(c0, LANES), lanes]
     k_tok = kv[lanes, pl.ds(c0, LANES)]
     v_tok = kv[lanes, pl.ds(n_chan + c0, LANES)]
-    scores = dot(k_tok, block_diag(q_t, dim))
-    grads = dot(v_tok, block_diag(g_t, dim))
+    q_bd = block_diag(q_t, dim)
+    g_bd = block_diag(g_t, dim)
+    scores = dot(k_tok, q_bd)
+    grads = dot(v_tok, g_bd)
     first = lax.broadcasted_iota(jnp.int32, (CELLS, LANES), 1) < CELLS
     heads = LANES // dim
     mixed, dq, dk, dv = [], [], [], []
@@ -89,13 +91,13 @@
         a2 = jnp.concatenate([jnp.where(first, a, zero), jnp.where(first, zero, a)], 0).astype(jnp.bfloat16)
         ds2 = jnp.concatenate([jnp.where(first, ds, zero), jnp.where(first, zero, ds)], 0).astype(jnp.bfloat16)
         mixed.append(dot(v_t[rows], a2))
-        dv.append(dot(g_t[rows], a2, NT))
+        dv.append(a2)
         dq.append(dot(k_t[rows], ds2) * scale)
-        dk.append(dot(q_t[rows], ds2, NT))
+        dk.append(ds2)
     mix_t[pl.ds(c0, LANES), lanes] = jnp.concatenate(mixed, 0).astype(jnp.bfloat16)
     gp_t[pl.ds(c0, LANES), lanes] = jnp.concatenate(dq, 0).astype(jnp.bfloat16)
-    gp_t[pl.ds(n_chan + c0, LANES), lanes] = jnp.concatenate(dk, 0).astype(jnp.bfloat16)
-    gp_t[pl.ds(2 * n_chan + c0, LANES), lanes] = jnp.concatenate(dv, 0).astype(jnp.bfloat16)
+    gp_t[pl.ds(n_chan + c0, LANES), lanes] = dot(q_bd, jnp.concatenate(dk, 1), NT).astype(jnp.bfloat16)
+    gp_t[pl.ds(2 * n_chan + c0, LANES), lanes] = dot(g_bd, jnp.concatenate(dv, 1), NT).astype(jnp.bfloat16)
 
 
 def place_row(line, shift, out, r, live=None):
@@ -362,33 +364,53 @@
     refs[-1][...] = parts[0].astype(jnp.bfloat16)
 
 
-def unpack_kernel(counts, n_proj, factor, meta, *refs):
-    n_c, n_x, n_y = counts
-    mine, other = refs[:n_x], refs[n_x : 2 * n_x]
-    qkv_ref, out_ref, gain_ref, bias_ref, small = refs[2 * n_x :]
-    rows = mine[0].shape[1]
-    n_chan = out_ref.shape[1]
-    for half in range(2):
-        c = meta[2] if half == 0 else 1 - meta[2]
-        for k, ref in enumerate(other if half else mine):
-            x = lax.rem(meta[3] + k, n_x)
-            for j in range(n_y):
-                y = lax.rem(meta[4] + j, n_y)
-                chunk = ref[j].astype(jnp.float32) * factor
-                to = pl.ds(pl.multiple_of(((c * n_x + x) * n_y + y) * rows, rows), rows)
-                qkv_ref[to] = chunk[:, :n_proj]
-                out_ref[to] = chunk[:, n_proj : n_proj + n_chan]
-                small[to] = chunk[:, n_proj + n_chan :]
-    gain_ref[...] = small[...].T[LANES - 1 :]
+def unpack_half(counts, n_proj, factor, meta, c, parts, qkv_ref, out_ref, small, qkv_half, out_half, sems):
+    _, n_x, n_y = counts
+    rows = parts[0].shape[1]
+    n_half, n_chan = out_half.shape
+    for k, ref in enumerate(parts):
+        x = lax.rem(meta[3] + k, n_x)
+        for j in range(n_y):
+            y = lax.rem(meta[4] + j, n_y)
+            chunk = ref[j].astype(jnp.float32) * factor
+            to = pl.ds(pl.multiple_of((x * n_y + y) * rows, rows), rows)
+            qkv_half[to] = chunk[:, :n_proj]
+            out_half[to] = chunk[:, n_proj : n_proj + n_chan]
+            small[to] = chunk[:, n_proj + n_chan :]
+    place = pl.ds(pl.multiple_of(c * n_half, n_half), n_half)
+    copies = [
+        pltpu.make_async_copy(qkv_half, qkv_ref.at[place], sems.at[0]),
+        pltpu.make_async_copy(out_half, out_ref.at[place], sems.at[1]),
+    ]
+    for copy in copies:
+        copy.start()
+    return copies
+
+
+def first_unpack_kernel(counts, n_proj, factor, meta, *refs):
+    parts, (qkv_ref, out_ref, small, *work) = refs[: counts[1]], refs[counts[1] :]
+    for copy in unpack_half(counts, n_proj, factor, meta, meta[2], parts, qkv_ref, out_ref, small, *work):
+        copy.wait()
+
+
+def second_unpack_kernel(counts, n_proj, factor, meta, *refs):
+    parts, (_, _, small_in, qkv_ref, out_ref, gain_ref, bias_ref, small, *work) = refs[: counts[1]], refs[counts[1] :]
+    copies = unpack_half(counts, n_proj, factor, meta, 1 - meta[2], parts, qkv_ref, out_ref, small, *work)
+    first = meta[2] == 0
+    upper = jnp.where(first, small_in[...], small[...])
+    lower = jnp.where(first, small[...], small_in[...])
+    gain_ref[...] = jnp.concatenate([upper, lower], 0).T[LANES - 1 :]
     n_head, n_gap = bias_ref.shape
     span = 2 * WINDOW - 1
-    wide = jnp.concatenate([small[:n_head], small[n_head : 2 * n_head]], 1)
+    wide = jnp.concatenate([upper[:n_head], upper[n_head : 2 * n_head]], 1)
     lane = lax.broadcasted_iota(jnp.int32, wide.shape, 1)
     bias = jnp.zeros_like(wide)
     for k in range(span):
         moved = pltpu.roll(wide, 2 * LANES - k, 1) if k else wide
         bias = jnp.where((lane >= k * span) & (lane < (k + 1) * span), moved, bias)
     bias_ref[...] = bias[:, :n_gap]
+    for copy in copies:
+        copy.wait()
 
 
 class Places:
@@ -611,19 +633,29 @@
     state_grad = (base.astype(f32) + edge.astype(f32)).astype(bf)
 
     factor = 1.0 / math.sqrt(n_rows * places.n_lat * n_cols * places.n_lon)
+    here = pl.BlockSpec(memory_space=pl.ANY)
+    n_half = n_chan // places.c
+    grads = (jax.ShapeDtypeStruct((n_chan, n_proj), f32), jax.ShapeDtypeStruct((n_chan, n_chan), f32))
+    staged = [pltpu.VMEM((n_half, n_proj), f32), pltpu.VMEM((n_half, n_chan), f32), pltpu.SemaphoreType.DMA((2,))]
+    qkv_grad, out_grad, small = pl.pallas_call(
+        functools.partial(first_unpack_kernel, counts, n_proj, factor),
+        out_shape=(*grads, jax.ShapeDtypeStruct((n_half, LANES), f32)),
+        in_specs=[smem] + [whole()] * places.x,
+        out_specs=(here, here, whole()),
+        scratch_shapes=staged,
+        compiler_params=pltpu.CompilerParams(vmem_limit_bytes=8 * MIB),
+        name="unpack_mine",
+    )(meta, *mine)
     qkv_grad, out_grad, gain_grad, bias_grad = pl.pallas_call(
-        functools.partial(unpack_kernel, counts, n_proj, factor),
-        out_shape=(
-            jax.ShapeDtypeStruct((n_chan, n_proj), f32),
-            jax.ShapeDtypeStruct((n_chan, n_chan), f32),
-            jax.ShapeDtypeStruct((1, n_chan), f32),
-            jax.ShapeDtypeStruct(bias_table.shape, f32),
-        ),
-        in_specs=[smem] + [whole()] * (2 * places.x),
-        scratch_shapes=[pltpu.VMEM((n_chan, LANES), f32)],
-        compiler_params=pltpu.CompilerParams(vmem_limit_bytes=16 * MIB),
-        name="unpack",
-    )(meta, *mine, *other)
+        functools.partial(second_unpack_kernel, counts, n_proj, factor),
+        out_shape=(*grads, jax.ShapeDtypeStruct((1, n_chan), f32), jax.ShapeDtypeStruct(bias_table.shape, f32)),
+        in_specs=[smem] + [whole()] * places.x + [here, here, whole()],
+        out_specs=(here, here, whole(), whole()),
+        input_output_aliases={places.x + 1: 0, places.x + 2: 1},
+        scratch_shapes=[pltpu.VMEM((n_half, LANES), f32), *staged],
+        compiler_params=pltpu.CompilerParams(vmem_limit_bytes=8 * MIB),
+        name="unpack_other",
+    )(meta, *other, qkv_grad, out_grad, small)
     return state_grad, qkv_grad, out_grad, gain_grad.reshape(n_chan), bias_grad
 
 

time: 123 us -> 124 us (level)
    pallas_call x1 -> x2, Pallas kernels: 3.1 us -> 4.73 us  [the longest x1 2.71 us: local(): pl.pallas_call(functools.partial(second_unpack_kernel, counts, n_proj, fa...]
  transfers between devices with their start and end apart: 27 -> 27, of which waited for: 11 -> 11; matrix products, arithmetic and copies ran while one was open for 1% -> 1% of each run, Pallas kernels for 15% -> 16%
where the time goes in v2:
time: 124 us
  starting transfers between devices  49.4 us (40%)
  Pallas kernels  37.5 us (30%)
  waiting for transfers between devices  33.4 us (27%)
    ppermute x21, starting transfers between devices, move(): return lax.ppermute(array, ('lat', 'lon'), pairs)  30.4 us
    ppermute x21, waiting for transfers between devices, move(): return lax.ppermute(array, ('lat', 'lon'), pairs)  24.3 us
    ppermute x6, starting transfers between devices, ring(): return lax.ppermute(array, ('lat', 'lon'), pairs)  18.9 us
    pallas_call x1, Pallas kernels, local(): pl.pallas_call(functools.partial(outer_kernel, n_head, counts), out_shape...  11.2 us
    pallas_call x1, Pallas kernels, local(): pl.pallas_call(functools.partial(inner_kernel, n_head), out_shape=(tile((...  10.5 us
    ppermute x6, waiting for transfers between devices, ring(): return lax.ppermute(array, ('lat', 'lon'), pairs)  9.09 us
    pallas_call x1, Pallas kernels, input_grad(): pl.pallas_call(cells_kernel, out_shape=(tile((n_rows, n_cols, n_chan)), t...  3.74 us
    pallas_call x1, Pallas kernels, local(): pl.pallas_call(functools.partial(pack_kernel, n_top), out_shape=(tile((2,...  3.19 us
  transfers between devices with their start and end apart: 27, of which 11 were waited for; matrix products, arithmetic and copies ran while one was open for 1% of the time, Pallas kernels for 16%

profile of v2, /device:TPU:1, one launch (start us, length us, event | category | flops | bytes accessed | tf_op | source)
XLA Modules:
  0.0 123.7 jit_solution(6489214836774763514)
XLA Ops:
  0.7 3.2 %pack.1 = (bf16[2,16,8,512]{3,2,1,0:T(8,128)(2,1)}, bf16[7,64,512]{2,1,0:T(8,128)(2,1)}, bf16[7,64,512]{2,1,0:T(8,128)(2,1)}, bf16[2,8,8,512]{3,2,1,0:T(8,128)(2,1)}) custom-call(bf16[16,64,512]{2,1,0:T(8,128)(2,1)} %x_ref.5, bf16[16,64,512]{2,1,0:T(8,128)(2,1)} %cot_ref.7, s32[16]{0:T(128)} %mask.1), custom_call_target="tpu_custom_call" | custom-call | tf_op jit(solution)/shard_map/pack/pallas_call | solution.py:513
  3.9 2.7 %collective-permute-start = (bf16[2,16,8,512]{3,2,1,0:T(8,128)(2,1)}, bf16[2,16,8,512]{3,2,1,0:T(8,128)(2,1)S(1)}, u32[]{:S(2)}, u32[]{:S(2)}) collective-permute-start(bf16[2,16,8,512]{3,2,1,0:T(8,128)(2,1)} %get-tuple-element.40), channel_id=1, source_target_pairs={{0,1},{1,2},{2,3},{3,4},{4,5},{5,6},{6,7},{7,8},{8,9},{9,10},{10,1... | collective-permute-start | bytes 786440 | tf_op jit(solution)/shard_map/ppermute | solution.py:498
  6.6 2.9 %collective-permute-start.1 = (bf16[7,64,512]{2,1,0:T(8,128)(2,1)}, bf16[7,64,512]{2,1,0:T(8,128)(2,1)}, u32[]{:S(2)}, u32[]{:S(2)}) collective-permute-start(bf16[7,64,512]{2,1,0:T(8,128)(2,1)} %get-tuple-element.44), channel_id=1, source_target_pairs={{0,16},{1,17},{2,18},{3,19},{4,20},{5,21},{6,22},{7,23},{8,24},{9,... | collective-permute-start | bytes 1376264 | tf_op jit(solution)/shard_map/ppermute | solution.py:498
  9.5 1.5 %collective-permute-start.2 = (bf16[2,8,8,512]{3,2,1,0:T(8,128)(2,1)}, bf16[2,8,8,512]{3,2,1,0:T(8,128)(2,1)S(1)}, u32[]{:S(2)}, u32[]{:S(2)}) collective-permute-start(bf16[2,8,8,512]{3,2,1,0:T(8,128)(2,1)} %get-tuple-element.45), channel_id=1, source_target_pairs={{0,17},{1,18},{2,19},{3,20},{4,21},{5,22},{6,23},{7,24},{8,25},{9,... | collective-permute-start | bytes 393224 | tf_op jit(solution)/shard_map/ppermute | solution.py:498
  11.0 2.9 %collective-permute-start.3 = (bf16[7,64,512]{2,1,0:T(8,128)(2,1)}, bf16[7,64,512]{2,1,0:T(8,128)(2,1)}, u32[]{:S(2)}, u32[]{:S(2)}) collective-permute-start(bf16[7,64,512]{2,1,0:T(8,128)(2,1)} %get-tuple-element.49), channel_id=1, source_target_pairs={{0,16},{1,17},{2,18},{3,19},{4,20},{5,21},{6,22},{7,23},{8,24},{9,... | collective-permute-start | bytes 1376264 | tf_op jit(solution)/shard_map/ppermute | solution.py:498
  14.0 0.7 copy-done.5
  14.7 0.8 prepare.1
  15.6 0.3 copy-done.2
  15.9 10.5 %inner.1 = (bf16[512,512]{1,0:T(8,128)(2,1)S(1)}, bf16[1536,512]{1,0:T(8,128)(2,1)S(1)}, f32[512,2048]{1,0:T(8,128)S(1)}, f32[16,64,128]{2,1,0:T(8,128)S(1)}) custom-call(s32[22]{0:T(128)S(1)} %concatenate.3.meta, bf16[16,64,512]{2,1,0:T(8,128)(2,1)S(1)} %copy-done.2, bf16[16,64,512]{2,1,0:T(8,128)(2,1)S(1)} %copy-done, ...), custom_call_target="tpu_custom_call" | custom-call | flops 8000000000 | bytes 16777216 | tf_op jit(solution)/shard_map/inner/pallas_call | solution.py:543
  26.4 1.0 collective-permute-done.2.corner_ref
  27.4 2.9 %front.1 = (bf16[512,512]{1,0:T(8,128)(2,1)S(1)}, bf16[512,512]{1,0:T(8,128)(2,1)S(1)}, bf16[1536,512]{1,0:T(8,128)(2,1)S(1)}, bf16[512,1024]{1,0:T(8,128)(2,1)S(1)}) custom-call(s32[22]{0:T(128)S(1)} %concatenate.3.meta, bf16[16,64,512]{2,1,0:T(8,128)(2,1)S(1)} %copy-done.2, bf16[2,16,8,512]{3,2,1,0:T(8,128)(2,1)S(1)} %collective-permute-done.side_ref, ...), custom_call_target="tpu_custom_call" | custom-call | flops 3000000000 | bytes 8388608 | tf_op jit(solution)/shard_map/front/pallas_call | solution.py:566
  30.3 8.1 %collective-permute-done.3.top = bf16[7,64,512]{2,1,0:T(8,128)(2,1)} collective-permute-done((bf16[7,64,512]{2,1,0:T(8,128)(2,1)}, bf16[7,64,512]{2,1,0:T(8,128)(2,1)}, u32[]{:S(2)}, u32[]{:S(2)}) %collective-permute-start.3) | collective-permute-done | bytes 458784 | tf_op jit(solution)/shard_map/ppermute | solution.py:498
  38.4 11.2 %outer.1 = (bf16[1536,512]{1,0:T(8,128)(2,1)S(1)}, f32[16,16,2176]{2,1,0:T(8,128)S(1)}, bf16[16,16,2176]{2,1,0:T(8,128)(2,1)S(1)}) custom-call(s32[22]{0:T(128)S(1)} %concatenate.3.meta, bf16[16,64,512]{2,1,0:T(8,128)(2,1)S(1)} %copy-done, bf16[2,16,8,512]{3,2,1,0:T(8,128)(2,1)S(1)} %collective-permute-done.side_ref, ...), custom_call_target="tpu_custom_call" | custom-call | flops 10000000000 | bytes 25165824 | tf_op jit(solution)/shard_map/outer/pallas_call | solution.py:579
  49.6 0.3 collective-permute-start.4
  49.9 2.7 %collective-permute-done.4.got_ref = bf16[16,16,2176]{2,1,0:T(8,128)(2,1)S(1)} collective-permute-done((bf16[16,16,2176]{2,1,0:T(8,128)(2,1)S(1)}, bf16[16,16,2176]{2,1,0:T(8,128)(2,1)S(1)}, u32[]{:S(2)}, u32[]{:S(2)}) %collective-permute-start.4) | collective-permute-done | bytes 1114144 | tf_op jit(solution)/shard_map/ppermute | solution.py:441
  52.6 0.2 add_c.1
  52.8 0.7 collective-permute-start.6
  53.5 2.5 %collective-permute-start.7 = (bf16[4,16,2176]{2,1,0:T(8,128)(2,1)S(1)}, bf16[4,16,2176]{2,1,0:T(8,128)(2,1)S(1)}, u32[]{:S(2)}, u32[]{:S(2)}) collective-permute-start(bf16[4,16,2176]{2,1,0:T(8,128)(2,1)S(1)} %get-tuple-element.62), channel_id=1, source_target_pairs={{0,4},{1,5},{2,6},{3,7},{4,0},{5,1},{6,2},{7,3},{8,12},{9,13},{10,... | collective-permute-start | bytes 835592 | tf_op jit(solution)/shard_map/ppermute | solution.py:441
  56.0 1.2 collective-permute-start.8
  57.2 3.7 %cells.1 = (bf16[16,64,512]{2,1,0:T(8,128)(2,1)S(1)}, bf16[7,72,512]{2,1,0:T(8,128)(2,1)S(1)}, bf16[16,8,512]{2,1,0:T(8,128)(2,1)S(1)}) custom-call(s32[22]{0:T(128)S(1)} %concatenate.3.meta, bf16[512,512]{1,0:T(8,128)(2,1)S(1)} %get-tuple-element.43.xi_ref, bf16[512,512]{1,0:T(8,128)(2,1)S(1)} %get-tuple-element.47.xo_ref, ...), custom_call_target="tpu_custom_call" | custom-call | flops 1600000000 | bytes 12582912 | tf_op jit(solution)/shard_map/cells/pallas_call | solution.py:603
  60.9 3.5 %collective-permute-start.5 = (bf16[7,72,512]{2,1,0:T(8,128)(2,1)S(1)}, bf16[7,72,512]{2,1,0:T(8,128)(2,1)S(1)}, u32[]{:S(2)}, u32[]{:S(2)}) collective-permute-start(bf16[7,72,512]{2,1,0:T(8,128)(2,1)S(1)} %get-tuple-element.59), channel_id=1, source_target_pairs={{0,240},{1,241},{2,242},{3,243},{4,244},{5,245},{6,246},{7,247},{8... | collective-permute-start | bytes 1548296 | tf_op jit(solution)/shard_map/ppermute | solution.py:498
  64.4 4.1 %collective-permute-done.7.refs_1_ = bf16[4,16,2176]{2,1,0:T(8,128)(2,1)S(1)} collective-permute-done((bf16[4,16,2176]{2,1,0:T(8,128)(2,1)S(1)}, bf16[4,16,2176]{2,1,0:T(8,128)(2,1)S(1)}, u32[]{:S(2)}, u32[]{:S(2)}) %collective-permute-start.7) | collective-permute-done | bytes 278560 | tf_op jit(solution)/shard_map/ppermute | solution.py:441
  68.5 0.1 add_x.1
  68.7 0.9 collective-permute-start.9
  69.5 2.5 %collective-permute-start.11 = (bf16[1,16,2176]{2,1,0:T(8,128)(2,1)S(1)}, bf16[1,16,2176]{2,1,0:T(8,128)(2,1)S(1)}, u32[]{:S(2)}, u32[]{:S(2)}) collective-permute-start(bf16[1,16,2176]{2,1,0:T(8,128)(2,1)S(1)} %get-tuple-element.67), channel_id=1, source_target_pairs={{0,24},{1,25},{2,26},{3,27},{4,28},{5,29},{6,30},{7,31},{8,0},{9,1... | collective-permute-start | bytes 208904 | tf_op jit(solution)/shard_map/ppermute | solution.py:441
  72.0 6.4 %collective-permute-done.9.refs_0_ = bf16[1,16,2176]{2,1,0:T(8,128)(2,1)S(1)} collective-permute-done((bf16[1,16,2176]{2,1,0:T(8,128)(2,1)S(1)}, bf16[1,16,2176]{2,1,0:T(8,128)(2,1)S(1)}, u32[]{:S(2)}, u32[]{:S(2)}) %collective-permute-start.9) | collective-permute-done | bytes 69664 | tf_op jit(solution)/shard_map/ppermute | solution.py:441
  78.5 0.1 collective-permute-start.12
  78.6 3.4 %collective-permute-start.13 = (bf16[1,16,2176]{2,1,0:T(8,128)(2,1)S(1)}, bf16[1,16,2176]{2,1,0:T(8,128)(2,1)S(1)}, u32[]{:S(2)}, u32[]{:S(2)}) collective-permute-start(bf16[1,16,2176]{2,1,0:T(8,128)(2,1)S(1)} %add_y.1.refs_0_), channel_id=1, source_target_pairs={{0,64},{1,65},{2,66},{3,67},{4,68},{5,69},{6,70},{7,71},{8,72},{9,... | collective-permute-start | bytes 208904 | tf_op jit(solution)/shard_map/ppermute | solution.py:441
  82.0 0.1 collective-permute-start.14
  82.1 1.8 %collective-permute-done.13.refs_2_ = bf16[1,16,2176]{2,1,0:T(8,128)(2,1)S(1)} collective-permute-done((bf16[1,16,2176]{2,1,0:T(8,128)(2,1)S(1)}, bf16[1,16,2176]{2,1,0:T(8,128)(2,1)S(1)}, u32[]{:S(2)}, u32[]{:S(2)}) %collective-permute-start.13) | collective-permute-done | bytes 69664 | tf_op jit(solution)/shard_map/ppermute | solution.py:441
  83.9 3.1 %collective-permute-done.14.refs_3_ = bf16[1,16,2176]{2,1,0:T(8,128)(2,1)S(1)} collective-permute-done((bf16[1,16,2176]{2,1,0:T(8,128)(2,1)S(1)}, bf16[1,16,2176]{2,1,0:T(8,128)(2,1)S(1)}, u32[]{:S(2)}, u32[]{:S(2)}) %collective-permute-start.14) | collective-permute-done | bytes 69664 | tf_op jit(solution)/shard_map/ppermute | solution.py:441
  87.0 4.4 %collective-permute-start.15 = (bf16[1,16,2176]{2,1,0:T(8,128)(2,1)S(1)}, bf16[1,16,2176]{2,1,0:T(8,128)(2,1)S(1)}, u32[]{:S(2)}, u32[]{:S(2)}) collective-permute-start(bf16[1,16,2176]{2,1,0:T(8,128)(2,1)S(1)} %add_z.2.refs_0_), channel_id=1, source_target_pairs={{0,192},{1,193},{2,194},{3,195},{4,196},{5,197},{6,198},{7,199},{8... | collective-permute-start | bytes 208904 | tf_op jit(solution)/shard_map/ppermute | solution.py:441
  91.4 1.8 %collective-permute-done.15.refs_1_ = bf16[1,16,2176]{2,1,0:T(8,128)(2,1)S(1)} collective-permute-done((bf16[1,16,2176]{2,1,0:T(8,128)(2,1)S(1)}, bf16[1,16,2176]{2,1,0:T(8,128)(2,1)S(1)}, u32[]{:S(2)}, u32[]{:S(2)}) %collective-permute-start.15) | collective-permute-done | bytes 69664 | tf_op jit(solution)/shard_map/ppermute | solution.py:441
  93.2 2.4 %collective-permute-start.16 = (bf16[1,16,2176]{2,1,0:T(8,128)(2,1)S(1)}, bf16[1,16,2176]{2,1,0:T(8,128)(2,1)S(1)}, u32[]{:S(2)}, u32[]{:S(2)}) collective-permute-start(bf16[1,16,2176]{2,1,0:T(8,128)(2,1)S(1)} %add_z.3.refs_0_), channel_id=1, source_target_pairs={{0,24},{1,25},{2,26},{3,27},{4,28},{5,29},{6,30},{7,31},{8,0},{9,1... | collective-permute-start | bytes 208904 | tf_op jit(solution)/shard_map/ppermute | solution.py:441
  95.7 0.8 collective-permute-start.18
  96.4 0.6 collective-permute-done.16.refs_1_
  97.0 3.4 %collective-permute-done.17.refs_2_ = bf16[1,16,2176]{2,1,0:T(8,128)(2,1)S(1)} collective-permute-done((bf16[1,16,2176]{2,1,0:T(8,128)(2,1)S(1)}, bf16[1,16,2176]{2,1,0:T(8,128)(2,1)S(1)}, u32[]{:S(2)}, u32[]{:S(2)}) %collective-permute-start.17) | collective-permute-done | bytes 69664 | tf_op jit(solution)/shard_map/ppermute | solution.py:441
  100.4 0.4 collective-permute-done.18.refs_3_
  100.9 2.3 %collective-permute-start.23 = (bf16[4,16,2176]{2,1,0:T(8,128)(2,1)S(1)}, bf16[4,16,2176]{2,1,0:T(8,128)(2,1)S(1)}, u32[]{:S(2)}, u32[]{:S(2)}) collective-permute-start(bf16[4,16,2176]{2,1,0:T(8,128)(2,1)S(1)} %join.1._.refs_0_), channel_id=1, source_target_pairs={{0,4},{1,5},{2,6},{3,7},{4,0},{5,1},{6,2},{7,3},{8,12},{9,13},{10,... | collective-permute-start | bytes 835592 | tf_op jit(solution)/shard_map/ppermute | solution.py:441
  103.2 0.8 collective-permute-start.25
  104.0 5.5 %collective-permute-start.19 = (bf16[16,8,512]{2,1,0:T(8,128)(2,1)S(1)}, bf16[16,8,512]{2,1,0:T(8,128)(2,1)S(1)}, u32[]{:S(2)}, u32[]{:S(2)}) collective-permute-start(bf16[16,8,512]{2,1,0:T(8,128)(2,1)S(1)} %edge.1), channel_id=1, source_target_pairs={{0,15},{1,0},{2,1},{3,2},{4,3},{5,4},{6,5},{7,6},{8,7},{9,8},{10,9... | collective-permute-start | bytes 393224 | tf_op jit(solution)/shard_map/ppermute | solution.py:498
  109.5 0.1 collective-permute-start.20
  109.6 3.3 %collective-permute-start.22 = (bf16[4,16,2176]{2,1,0:T(8,128)(2,1)S(1)}, bf16[4,16,2176]{2,1,0:T(8,128)(2,1)S(1)}, u32[]{:S(2)}, u32[]{:S(2)}) collective-permute-start(bf16[4,16,2176]{2,1,0:T(8,128)(2,1)S(1)} %collective-permute-done.21.refs_1_), channel_id=1, source_target_pairs={{0,1},{1,0},{2,3},{3,2},{4,5},{5,4},{6,7},{7,6},{8,9},{9,8},{10,11... | collective-permute-start | bytes 835592 | tf_op jit(solution)/shard_map/ppermute | solution.py:441
  112.9 1.7 %collective-permute-start.24 = (bf16[4,16,2176]{2,1,0:T(8,128)(2,1)S(1)}, bf16[4,16,2176]{2,1,0:T(8,128)(2,1)S(1)}, u32[]{:S(2)}, u32[]{:S(2)}) collective-permute-start(bf16[4,16,2176]{2,1,0:T(8,128)(2,1)S(1)} %collective-permute-done.23.refs_2_), channel_id=1, source_target_pairs={{0,1},{1,0},{2,3},{3,2},{4,5},{5,4},{6,7},{7,6},{8,9},{9,8},{10,11... | collective-permute-start | bytes 835592 | tf_op jit(solution)/shard_map/ppermute | solution.py:441
  114.6 2.9 %collective-permute-start.26 = (bf16[4,16,2176]{2,1,0:T(8,128)(2,1)S(1)}, bf16[4,16,2176]{2,1,0:T(8,128)(2,1)S(1)}, u32[]{:S(2)}, u32[]{:S(2)}) collective-permute-start(bf16[4,16,2176]{2,1,0:T(8,128)(2,1)S(1)} %collective-permute-done.25.refs_3_), channel_id=1, source_target_pairs={{0,1},{1,0},{2,3},{3,2},{4,5},{5,4},{6,7},{7,6},{8,9},{9,8},{10,11... | collective-permute-start | bytes 835592 | tf_op jit(solution)/shard_map/ppermute | solution.py:441
  117.6 1.2 add_convert_fusion
  118.8 2.0 %unpack_mine.1 = (f32[512,1536]{1,0:T(8,128)}, f32[512,512]{1,0:T(8,128)}, f32[256,128]{1,0:T(8,128)S(1)}) custom-call(s32[22]{0:T(128)S(1)} %concatenate.3.meta, bf16[4,16,2176]{2,1,0:T(8,128)(2,1)S(1)} %join.1._.refs_0_, bf16[4,16,2176]{2,1,0:T(8,128)(2,1)S(1)} %collective-permute-done.21.refs_1_, ...), custom_call_target="tpu_custom_call" | custom-call | tf_op jit(solution)/shard_map/unpack_mine/pallas_call | solution.py:640
  120.8 2.7 %unpack_other.1 = (f32[512,1536]{1,0:T(8,128)}, f32[512,512]{1,0:T(8,128)}, f32[1,512]{1,0:T(1,128)}, f32[16,225]{1,0:T(8,128)}) custom-call(s32[22]{0:T(128)S(1)} %concatenate.3.meta, bf16[4,16,2176]{2,1,0:T(8,128)(2,1)S(1)} %collective-permute-done.20.refs_0_, ...), custom_call_target="tpu_custom_call", output_to_operand_aliasing={{0}: (5, {}), {1}: (6, {})} | custom-call | tf_op jit(solution)/shard_map/unpack_other/pallas_call | solution.py:649
  (40 shorter events, 0.4 us)
Async XLA Ops:
  0.6 13.3 %copy-start.6 = (s32[16]{0:T(128)S(1)}, s32[16]{0:T(128)}, u32[]{:S(2)}) copy-start(s32[16]{0:T(128)} %mask.1) | copy-start | bytes 196
  0.6 13.3 %copy-start.7 = (s32[2]{0:T(128)S(1)}, s32[2]{0:T(128)}, u32[]{:S(2)}) copy-start(s32[2]{0:T(128)} %param.11) | copy-start | bytes 28
  0.7 13.3 %copy-start.1 = (bf16[512,1536]{1,0:T(8,128)(2,1)S(1)}, bf16[512,1536]{1,0:T(8,128)(2,1)}, u32[]{:S(2)}) copy-start(bf16[512,1536]{1,0:T(8,128)(2,1)} %w_ref.9) | copy-start | bytes 4718596
  3.9 11.7 %copy-start = (bf16[16,64,512]{2,1,0:T(8,128)(2,1)S(1)}, bf16[16,64,512]{2,1,0:T(8,128)(2,1)}, u32[]{:S(2)}) copy-start(bf16[16,64,512]{2,1,0:T(8,128)(2,1)} %cot_ref.7) | copy-start | bytes 3145732
  3.9 11.7 %copy-start.3 = (f32[512]{0:T(512)S(1)}, f32[512]{0:T(512)}, u32[]{:S(2)}) copy-start(f32[512]{0:T(512)} %param.12) | copy-start | bytes 6148
  3.9 11.7 %copy-start.4 = (bf16[512,512]{1,0:T(8,128)(2,1)S(1)}, bf16[512,512]{1,0:T(8,128)(2,1)}, u32[]{:S(2)}) copy-start(bf16[512,512]{1,0:T(8,128)(2,1)} %wo_ref.3) | copy-start | bytes 1572868
  3.9 11.7 %collective-permute-start = (bf16[2,16,8,512]{3,2,1,0:T(8,128)(2,1)}, bf16[2,16,8,512]{3,2,1,0:T(8,128)(2,1)S(1)}, u32[]{:S(2)}, u32[]{:S(2)}) collective-permute-start(bf16[2,16,8,512]{3,2,1,0:T(8,128)(2,1)} %get-tuple-element.40), channel_id=1, source_target_pairs={{0,1},{1,2},{2,3},{3,4},{4,5},{5,6},{6,7},{7,8},{8,9},{9,10},{10,1... | collective-permute-start | bytes 786440 | tf_op jit(solution)/shard_map/ppermute | solution.py:498
  6.6 20.9 %collective-permute-start.1 = (bf16[7,64,512]{2,1,0:T(8,128)(2,1)}, bf16[7,64,512]{2,1,0:T(8,128)(2,1)}, u32[]{:S(2)}, u32[]{:S(2)}) collective-permute-start(bf16[7,64,512]{2,1,0:T(8,128)(2,1)} %get-tuple-element.44), channel_id=1, source_target_pairs={{0,16},{1,17},{2,18},{3,19},{4,20},{5,21},{6,22},{7,23},{8,24},{9,... | collective-permute-start | bytes 1376264 | tf_op jit(solution)/shard_map/ppermute | solution.py:498
  9.5 17.9 %collective-permute-start.2 = (bf16[2,8,8,512]{3,2,1,0:T(8,128)(2,1)}, bf16[2,8,8,512]{3,2,1,0:T(8,128)(2,1)S(1)}, u32[]{:S(2)}, u32[]{:S(2)}) collective-permute-start(bf16[2,8,8,512]{3,2,1,0:T(8,128)(2,1)} %get-tuple-element.45), channel_id=1, source_target_pairs={{0,17},{1,18},{2,19},{3,20},{4,21},{5,22},{6,23},{7,24},{8,25},{9,... | collective-permute-start | bytes 393224 | tf_op jit(solution)/shard_map/ppermute | solution.py:498
  11.0 27.4 %collective-permute-start.3 = (bf16[7,64,512]{2,1,0:T(8,128)(2,1)}, bf16[7,64,512]{2,1,0:T(8,128)(2,1)}, u32[]{:S(2)}, u32[]{:S(2)}) collective-permute-start(bf16[7,64,512]{2,1,0:T(8,128)(2,1)} %get-tuple-element.49), channel_id=1, source_target_pairs={{0,16},{1,17},{2,18},{3,19},{4,20},{5,21},{6,22},{7,23},{8,24},{9,... | collective-permute-start | bytes 1376264 | tf_op jit(solution)/shard_map/ppermute | solution.py:498
  14.0 0.7 copy-start.5
  14.7 1.2 copy-start.2
  49.6 3.1 %collective-permute-start.4 = (bf16[16,16,2176]{2,1,0:T(8,128)(2,1)S(1)}, bf16[16,16,2176]{2,1,0:T(8,128)(2,1)S(1)}, u32[]{:S(2)}, u32[]{:S(2)}) collective-permute-start(bf16[16,16,2176]{2,1,0:T(8,128)(2,1)S(1)} %get-tuple-element.56), channel_id=1, source_target_pairs={{0,1},{1,0},{2,3},{3,2},{4,5},{5,4},{6,7},{7,6},{8,9},{9,8},{10,11... | collective-permute-start | bytes 3342344 | tf_op jit(solution)/shard_map/ppermute | solution.py:441
  52.8 11.6 %collective-permute-start.6 = (bf16[4,16,2176]{2,1,0:T(8,128)(2,1)S(1)}, bf16[4,16,2176]{2,1,0:T(8,128)(2,1)S(1)}, u32[]{:S(2)}, u32[]{:S(2)}) collective-permute-start(bf16[4,16,2176]{2,1,0:T(8,128)(2,1)S(1)} %get-tuple-element.61), channel_id=1, source_target_pairs={{0,2},{1,3},{2,4},{3,5},{4,6},{5,7},{6,0},{7,1},{8,10},{9,11},{10,... | collective-permute-start | bytes 835592 | tf_op jit(solution)/shard_map/ppermute | solution.py:441
  53.5 15.0 %collective-permute-start.7 = (bf16[4,16,2176]{2,1,0:T(8,128)(2,1)S(1)}, bf16[4,16,2176]{2,1,0:T(8,128)(2,1)S(1)}, u32[]{:S(2)}, u32[]{:S(2)}) collective-permute-start(bf16[4,16,2176]{2,1,0:T(8,128)(2,1)S(1)} %get-tuple-element.62), channel_id=1, source_target_pairs={{0,4},{1,5},{2,6},{3,7},{4,0},{5,1},{6,2},{7,3},{8,12},{9,13},{10,... | collective-permute-start | bytes 835592 | tf_op jit(solution)/shard_map/ppermute | solution.py:441
  56.0 12.5 %collective-permute-start.8 = (bf16[4,16,2176]{2,1,0:T(8,128)(2,1)S(1)}, bf16[4,16,2176]{2,1,0:T(8,128)(2,1)S(1)}, u32[]{:S(2)}, u32[]{:S(2)}) collective-permute-start(bf16[4,16,2176]{2,1,0:T(8,128)(2,1)S(1)} %get-tuple-element.63), channel_id=1, source_target_pairs={{0,6},{1,7},{2,0},{3,1},{4,2},{5,3},{6,4},{7,5},{8,14},{9,15},{10,... | collective-permute-start | bytes 835592 | tf_op jit(solution)/shard_map/ppermute | solution.py:441
  60.9 43.1 %collective-permute-start.5 = (bf16[7,72,512]{2,1,0:T(8,128)(2,1)S(1)}, bf16[7,72,512]{2,1,0:T(8,128)(2,1)S(1)}, u32[]{:S(2)}, u32[]{:S(2)}) collective-permute-start(bf16[7,72,512]{2,1,0:T(8,128)(2,1)S(1)} %get-tuple-element.59), channel_id=1, source_target_pairs={{0,240},{1,241},{2,242},{3,243},{4,244},{5,245},{6,246},{7,247},{8... | collective-permute-start | bytes 1548296 | tf_op jit(solution)/shard_map/ppermute | solution.py:498
  68.7 9.7 %collective-permute-start.9 = (bf16[1,16,2176]{2,1,0:T(8,128)(2,1)S(1)}, bf16[1,16,2176]{2,1,0:T(8,128)(2,1)S(1)}, u32[]{:S(2)}, u32[]{:S(2)}) collective-permute-start(bf16[1,16,2176]{2,1,0:T(8,128)(2,1)S(1)} %get-tuple-element.65), channel_id=1, source_target_pairs={{0,8},{1,9},{2,10},{3,11},{4,12},{5,13},{6,14},{7,15},{8,16},{9,17... | collective-permute-start | bytes 208904 | tf_op jit(solution)/shard_map/ppermute | solution.py:441
  69.5 8.9 %collective-permute-start.10 = (bf16[1,16,2176]{2,1,0:T(8,128)(2,1)S(1)}, bf16[1,16,2176]{2,1,0:T(8,128)(2,1)S(1)}, u32[]{:S(2)}, u32[]{:S(2)}) collective-permute-start(bf16[1,16,2176]{2,1,0:T(8,128)(2,1)S(1)} %get-tuple-element.66), channel_id=1, source_target_pairs={{0,16},{1,17},{2,18},{3,19},{4,20},{5,21},{6,22},{7,23},{8,24},{9,... | collective-permute-start | bytes 208904 | tf_op jit(solution)/shard_map/ppermute | solution.py:441
  69.5 8.9 %collective-permute-start.11 = (bf16[1,16,2176]{2,1,0:T(8,128)(2,1)S(1)}, bf16[1,16,2176]{2,1,0:T(8,128)(2,1)S(1)}, u32[]{:S(2)}, u32[]{:S(2)}) collective-permute-start(bf16[1,16,2176]{2,1,0:T(8,128)(2,1)S(1)} %get-tuple-element.67), channel_id=1, source_target_pairs={{0,24},{1,25},{2,26},{3,27},{4,28},{5,29},{6,30},{7,31},{8,0},{9,1... | collective-permute-start | bytes 208904 | tf_op jit(solution)/shard_map/ppermute | solution.py:441
  78.5 3.6 %collective-permute-start.12 = (bf16[1,16,2176]{2,1,0:T(8,128)(2,1)S(1)}, bf16[1,16,2176]{2,1,0:T(8,128)(2,1)S(1)}, u32[]{:S(2)}, u32[]{:S(2)}) collective-permute-start(bf16[1,16,2176]{2,1,0:T(8,128)(2,1)S(1)} %add_y.1.refs_0_), channel_id=1, source_target_pairs={{0,32},{1,33},{2,34},{3,35},{4,36},{5,37},{6,38},{7,39},{8,40},{9,... | collective-permute-start | bytes 208904 | tf_op jit(solution)/shard_map/ppermute | solution.py:441
  78.6 5.3 %collective-permute-start.13 = (bf16[1,16,2176]{2,1,0:T(8,128)(2,1)S(1)}, bf16[1,16,2176]{2,1,0:T(8,128)(2,1)S(1)}, u32[]{:S(2)}, u32[]{:S(2)}) collective-permute-start(bf16[1,16,2176]{2,1,0:T(8,128)(2,1)S(1)} %add_y.1.refs_0_), channel_id=1, source_target_pairs={{0,64},{1,65},{2,66},{3,67},{4,68},{5,69},{6,70},{7,71},{8,72},{9,... | collective-permute-start | bytes 208904 | tf_op jit(solution)/shard_map/ppermute | solution.py:441
  82.0 5.0 %collective-permute-start.14 = (bf16[1,16,2176]{2,1,0:T(8,128)(2,1)S(1)}, bf16[1,16,2176]{2,1,0:T(8,128)(2,1)S(1)}, u32[]{:S(2)}, u32[]{:S(2)}) collective-permute-start(bf16[1,16,2176]{2,1,0:T(8,128)(2,1)S(1)} %add_y.1.refs_0_), channel_id=1, source_target_pairs={{0,96},{1,97},{2,98},{3,99},{4,100},{5,101},{6,102},{7,103},{8,104... | collective-permute-start | bytes 208904 | tf_op jit(solution)/shard_map/ppermute | solution.py:441
  87.0 6.2 %collective-permute-start.15 = (bf16[1,16,2176]{2,1,0:T(8,128)(2,1)S(1)}, bf16[1,16,2176]{2,1,0:T(8,128)(2,1)S(1)}, u32[]{:S(2)}, u32[]{:S(2)}) collective-permute-start(bf16[1,16,2176]{2,1,0:T(8,128)(2,1)S(1)} %add_z.2.refs_0_), channel_id=1, source_target_pairs={{0,192},{1,193},{2,194},{3,195},{4,196},{5,197},{6,198},{7,199},{8... | collective-permute-start | bytes 208904 | tf_op jit(solution)/shard_map/ppermute | solution.py:441
  93.2 3.8 %collective-permute-start.16 = (bf16[1,16,2176]{2,1,0:T(8,128)(2,1)S(1)}, bf16[1,16,2176]{2,1,0:T(8,128)(2,1)S(1)}, u32[]{:S(2)}, u32[]{:S(2)}) collective-permute-start(bf16[1,16,2176]{2,1,0:T(8,128)(2,1)S(1)} %add_z.3.refs_0_), channel_id=1, source_target_pairs={{0,24},{1,25},{2,26},{3,27},{4,28},{5,29},{6,30},{7,31},{8,0},{9,1... | collective-permute-start | bytes 208904 | tf_op jit(solution)/shard_map/ppermute | solution.py:441
  95.6 4.8 %collective-permute-start.17 = (bf16[1,16,2176]{2,1,0:T(8,128)(2,1)S(1)}, bf16[1,16,2176]{2,1,0:T(8,128)(2,1)S(1)}, u32[]{:S(2)}, u32[]{:S(2)}) collective-permute-start(bf16[1,16,2176]{2,1,0:T(8,128)(2,1)S(1)} %add_z.3.refs_0_), channel_id=1, source_target_pairs={{0,16},{1,17},{2,18},{3,19},{4,20},{5,21},{6,22},{7,23},{8,24},{9,... | collective-permute-start | bytes 208904 | tf_op jit(solution)/shard_map/ppermute | solution.py:441
  95.7 5.1 %collective-permute-start.18 = (bf16[1,16,2176]{2,1,0:T(8,128)(2,1)S(1)}, bf16[1,16,2176]{2,1,0:T(8,128)(2,1)S(1)}, u32[]{:S(2)}, u32[]{:S(2)}) collective-permute-start(bf16[1,16,2176]{2,1,0:T(8,128)(2,1)S(1)} %add_z.3.refs_0_), channel_id=1, source_target_pairs={{0,8},{1,9},{2,10},{3,11},{4,12},{5,13},{6,14},{7,15},{8,16},{9,17... | collective-permute-start | bytes 208904 | tf_op jit(solution)/shard_map/ppermute | solution.py:441
  100.8 8.8 %collective-permute-start.21 = (bf16[4,16,2176]{2,1,0:T(8,128)(2,1)S(1)}, bf16[4,16,2176]{2,1,0:T(8,128)(2,1)S(1)}, u32[]{:S(2)}, u32[]{:S(2)}) collective-permute-start(bf16[4,16,2176]{2,1,0:T(8,128)(2,1)S(1)} %join.1._.refs_0_), channel_id=1, source_target_pairs={{0,6},{1,7},{2,0},{3,1},{4,2},{5,3},{6,4},{7,5},{8,14},{9,15},{10,... | collective-permute-start | bytes 835592 | tf_op jit(solution)/shard_map/ppermute | solution.py:441
  100.9 12.0 %collective-permute-start.23 = (bf16[4,16,2176]{2,1,0:T(8,128)(2,1)S(1)}, bf16[4,16,2176]{2,1,0:T(8,128)(2,1)S(1)}, u32[]{:S(2)}, u32[]{:S(2)}) collective-permute-start(bf16[4,16,2176]{2,1,0:T(8,128)(2,1)S(1)} %join.1._.refs_0_), channel_id=1, source_target_pairs={{0,4},{1,5},{2,6},{3,7},{4,0},{5,1},{6,2},{7,3},{8,12},{9,13},{10,... | collective-permute-start | bytes 835592 | tf_op jit(solution)/shard_map/ppermute | solution.py:441
  103.2 11.4 %collective-permute-start.25 = (bf16[4,16,2176]{2,1,0:T(8,128)(2,1)S(1)}, bf16[4,16,2176]{2,1,0:T(8,128)(2,1)S(1)}, u32[]{:S(2)}, u32[]{:S(2)}) collective-permute-start(bf16[4,16,2176]{2,1,0:T(8,128)(2,1)S(1)} %join.1._.refs_0_), channel_id=1, source_target_pairs={{0,2},{1,3},{2,4},{3,5},{4,6},{5,7},{6,0},{7,1},{8,10},{9,11},{10,... | collective-permute-start | bytes 835592 | tf_op jit(solution)/shard_map/ppermute | solution.py:441
  104.0 13.5 %collective-permute-start.19 = (bf16[16,8,512]{2,1,0:T(8,128)(2,1)S(1)}, bf16[16,8,512]{2,1,0:T(8,128)(2,1)S(1)}, u32[]{:S(2)}, u32[]{:S(2)}) collective-permute-start(bf16[16,8,512]{2,1,0:T(8,128)(2,1)S(1)} %edge.1), channel_id=1, source_target_pairs={{0,15},{1,0},{2,1},{3,2},{4,3},{5,4},{6,5},{7,6},{8,7},{9,8},{10,9... | collective-permute-start | bytes 393224 | tf_op jit(solution)/shard_map/ppermute | solution.py:498
  109.5 11.3 %collective-permute-start.20 = (bf16[4,16,2176]{2,1,0:T(8,128)(2,1)S(1)}, bf16[4,16,2176]{2,1,0:T(8,128)(2,1)S(1)}, u32[]{:S(2)}, u32[]{:S(2)}) collective-permute-start(bf16[4,16,2176]{2,1,0:T(8,128)(2,1)S(1)} %join.1._.refs_0_), channel_id=1, source_target_pairs={{0,1},{1,0},{2,3},{3,2},{4,5},{5,4},{6,7},{7,6},{8,9},{9,8},{10,11... | collective-permute-start | bytes 835592 | tf_op jit(solution)/shard_map/ppermute | solution.py:441
  109.6 11.2 %collective-permute-start.22 = (bf16[4,16,2176]{2,1,0:T(8,128)(2,1)S(1)}, bf16[4,16,2176]{2,1,0:T(8,128)(2,1)S(1)}, u32[]{:S(2)}, u32[]{:S(2)}) collective-permute-start(bf16[4,16,2176]{2,1,0:T(8,128)(2,1)S(1)} %collective-permute-done.21.refs_1_), channel_id=1, source_target_pairs={{0,1},{1,0},{2,3},{3,2},{4,5},{5,4},{6,7},{7,6},{8,9},{9,8},{10,11... | collective-permute-start | bytes 835592 | tf_op jit(solution)/shard_map/ppermute | solution.py:441
  112.9 7.9 %collective-permute-start.24 = (bf16[4,16,2176]{2,1,0:T(8,128)(2,1)S(1)}, bf16[4,16,2176]{2,1,0:T(8,128)(2,1)S(1)}, u32[]{:S(2)}, u32[]{:S(2)}) collective-permute-start(bf16[4,16,2176]{2,1,0:T(8,128)(2,1)S(1)} %collective-permute-done.23.refs_2_), channel_id=1, source_target_pairs={{0,1},{1,0},{2,3},{3,2},{4,5},{5,4},{6,7},{7,6},{8,9},{9,8},{10,11... | collective-permute-start | bytes 835592 | tf_op jit(solution)/shard_map/ppermute | solution.py:441
  114.6 6.2 %collective-permute-start.26 = (bf16[4,16,2176]{2,1,0:T(8,128)(2,1)S(1)}, bf16[4,16,2176]{2,1,0:T(8,128)(2,1)S(1)}, u32[]{:S(2)}, u32[]{:S(2)}) collective-permute-start(bf16[4,16,2176]{2,1,0:T(8,128)(2,1)S(1)} %collective-permute-done.25.refs_3_), channel_id=1, source_target_pairs={{0,1},{1,0},{2,3},{3,2},{4,5},{5,4},{6,7},{7,6},{8,9},{9,8},{10,11... | collective-permute-start | bytes 835592 | tf_op jit(solution)/shard_map/ppermute | solution.py:441

commit v3 on v1

--- a/solution.py
+++ b/solution.py
@@ -69,8 +69,10 @@
     g_t = gm_t[pl.ds(c0, LANES), lanes]
     k_tok = kv[lanes, pl.ds(c0, LANES)]
     v_tok = kv[lanes, pl.ds(n_chan + c0, LANES)]
-    scores = dot(k_tok, block_diag(q_t, dim))
-    grads = dot(v_tok, block_diag(g_t, dim))
+    q_bd = block_diag(q_t, dim)
+    g_bd = block_diag(g_t, dim)
+    scores = dot(k_tok, q_bd)
+    grads = dot(v_tok, g_bd)
     first = lax.broadcasted_iota(jnp.int32, (CELLS, LANES), 1) < CELLS
     heads = LANES // dim
     mixed, dq, dk, dv = [], [], [], []
@@ -89,13 +91,13 @@
         a2 = jnp.concatenate([jnp.where(first, a, zero), jnp.where(first, zero, a)], 0).astype(jnp.bfloat16)
         ds2 = jnp.concatenate([jnp.where(first, ds, zero), jnp.where(first, zero, ds)], 0).astype(jnp.bfloat16)
         mixed.append(dot(v_t[rows], a2))
-        dv.append(dot(g_t[rows], a2, NT))
+        dv.append(a2)
         dq.append(dot(k_t[rows], ds2) * scale)
-        dk.append(dot(q_t[rows], ds2, NT))
+        dk.append(ds2)
     mix_t[pl.ds(c0, LANES), lanes] = jnp.concatenate(mixed, 0).astype(jnp.bfloat16)
     gp_t[pl.ds(c0, LANES), lanes] = jnp.concatenate(dq, 0).astype(jnp.bfloat16)
-    gp_t[pl.ds(n_chan + c0, LANES), lanes] = jnp.concatenate(dk, 0).astype(jnp.bfloat16)
-    gp_t[pl.ds(2 * n_chan + c0, LANES), lanes] = jnp.concatenate(dv, 0).astype(jnp.bfloat16)
+    gp_t[pl.ds(n_chan + c0, LANES), lanes] = dot(q_bd, jnp.concatenate(dk, 1), NT).astype(jnp.bfloat16)
+    gp_t[pl.ds(2 * n_chan + c0, LANES), lanes] = dot(g_bd, jnp.concatenate(dv, 1), NT).astype(jnp.bfloat16)
 
 
 def place_row(line, shift, out, r, live=None):
@@ -364,21 +366,26 @@
 
 def unpack_kernel(counts, n_proj, factor, meta, *refs):
     n_c, n_x, n_y = counts
-    mine, other = refs[:n_x], refs[n_x : 2 * n_x]
-    qkv_ref, out_ref, gain_ref, bias_ref, small = refs[2 * n_x :]
-    rows = mine[0].shape[1]
-    n_chan = out_ref.shape[1]
+    parts, (qkv_ref, out_ref, gain_ref, bias_ref, qkv_all, out_all, small, sems) = refs[: 2 * n_x], refs[2 * n_x :]
+    rows = parts[0].shape[1]
+    n_chan = out_all.shape[0]
+    n_half = n_chan // n_c
+    copies = []
     for half in range(2):
         c = meta[2] if half == 0 else 1 - meta[2]
-        for k, ref in enumerate(other if half else mine):
+        for k in range(n_x):
             x = lax.rem(meta[3] + k, n_x)
             for j in range(n_y):
                 y = lax.rem(meta[4] + j, n_y)
-                chunk = ref[j].astype(jnp.float32) * factor
+                chunk = parts[half * n_x + k][j].astype(jnp.float32) * factor
                 to = pl.ds(pl.multiple_of(((c * n_x + x) * n_y + y) * rows, rows), rows)
-                qkv_ref[to] = chunk[:, :n_proj]
-                out_ref[to] = chunk[:, n_proj : n_proj + n_chan]
+                qkv_all[to] = chunk[:, :n_proj]
+                out_all[to] = chunk[:, n_proj : n_proj + n_chan]
                 small[to] = chunk[:, n_proj + n_chan :]
+        place = pl.ds(pl.multiple_of(c * n_half, n_half), n_half)
+        for k, (ref, full) in enumerate(((qkv_ref, qkv_all), (out_ref, out_all))):
+            copies.append(pltpu.make_async_copy(full.at[place], ref.at[place], sems.at[2 * half + k]))
+            copies[-1].start()
     gain_ref[...] = small[...].T[LANES - 1 :]
     n_head, n_gap = bias_ref.shape
     span = 2 * WINDOW - 1
@@ -389,6 +396,8 @@
         moved = pltpu.roll(wide, 2 * LANES - k, 1) if k else wide
         bias = jnp.where((lane >= k * span) & (lane < (k + 1) * span), moved, bias)
     bias_ref[...] = bias[:, :n_gap]
+    for copy in copies:
+        copy.wait()
 
 
 class Places:
@@ -471,7 +480,10 @@
 def ring(array, lat, lon):
     n_lat, n_lon = lax.axis_size("lat"), lax.axis_size("lon")
     pairs = [
-        (i * n_lon + j, (i + lat) % n_lat * n_lon + (j + lon) % n_lon) for i in range(n_lat) for j in range(n_lon)
+        (i * n_lon + j, (i + lat) * n_lon + (j + lon) % n_lon)
+        for i in range(n_lat)
+        for j in range(n_lon)
+        if 0 <= i + lat < n_lat
     ]
     return lax.ppermute(array, ("lat", "lon"), pairs)
 
@@ -611,6 +623,7 @@
     state_grad = (base.astype(f32) + edge.astype(f32)).astype(bf)
 
     factor = 1.0 / math.sqrt(n_rows * places.n_lat * n_cols * places.n_lon)
+    here = pl.BlockSpec(memory_space=pl.ANY)
     qkv_grad, out_grad, gain_grad, bias_grad = pl.pallas_call(
         functools.partial(unpack_kernel, counts, n_proj, factor),
         out_shape=(
@@ -620,7 +633,13 @@
             jax.ShapeDtypeStruct(bias_table.shape, f32),
         ),
         in_specs=[smem] + [whole()] * (2 * places.x),
-        scratch_shapes=[pltpu.VMEM((n_chan, LANES), f32)],
+        out_specs=(here, here, whole(), whole()),
+        scratch_shapes=[
+            pltpu.VMEM((n_chan, n_proj), f32),
+            pltpu.VMEM((n_chan, n_chan), f32),
+            pltpu.VMEM((n_chan, LANES), f32),
+            pltpu.SemaphoreType.DMA((4,)),
+        ],
         compiler_params=pltpu.CompilerParams(vmem_limit_bytes=16 * MIB),
         name="unpack",
     )(meta, *mine, *other)

time: 123 us -> 127 us (1.033)
  starting transfers between devices: 49.3 us -> 58.2 us
  waiting for transfers between devices: 33 us -> 28.1 us
    ppermute x6, waiting for transfers between devices: 8.63 us -> 0.02 us  [ring(): return lax.ppermute(array, ('lat', 'lon'), pairs)]
    ppermute x21, starting transfers between devices: 30.4 us -> 35.2 us  [move(): return lax.ppermute(array, ('lat', 'lon'), pairs)]
    ppermute x6, starting transfers between devices: 18.9 us -> 23 us  [ring(): return lax.ppermute(array, ('lat', 'lon'), pairs)]
    ppermute x21, waiting for transfers between devices: 24.3 us -> 28.1 us  [move(): return lax.ppermute(array, ('lat', 'lon'), pairs)]
  transfers between devices with their start and end apart: 27 -> 27, of which waited for: 11 -> 11; matrix products, arithmetic and copies ran while one was open for 1% -> 1% of each run, Pallas kernels for 15% -> 14%
where the time goes in v3:
time: 127 us; the launch traced here: 126 us
  starting transfers between devices  58.2 us (46%)
  Pallas kernels  36.5 us (29%)
  waiting for transfers between devices  28.1 us (22%)
    ppermute x21, starting transfers between devices, move(): return lax.ppermute(array, ('lat', 'lon'), pairs)  35.2 us
    ppermute x21, waiting for transfers between devices, move(): return lax.ppermute(array, ('lat', 'lon'), pairs)  28.1 us
    ppermute x6, starting transfers between devices, ring(): return lax.ppermute(array, ('lat', 'lon'), pairs)  23 us
    pallas_call x1, Pallas kernels, local(): pl.pallas_call(functools.partial(outer_kernel, n_head, counts), out_shape...  11.4 us
    pallas_call x1, Pallas kernels, local(): pl.pallas_call(functools.partial(inner_kernel, n_head), out_shape=(tile((...  10.5 us
    pallas_call x1, Pallas kernels, input_grad(): pl.pallas_call(cells_kernel, out_shape=(tile((n_rows, n_cols, n_chan)), t...  3.74 us
    pallas_call x1, Pallas kernels, local(): pl.pallas_call(functools.partial(unpack_kernel, counts, n_proj, factor),...  3.49 us
    pallas_call x1, Pallas kernels, local(): pl.pallas_call(functools.partial(pack_kernel, n_top), out_shape=(tile((2,...  3.19 us
  transfers between devices with their start and end apart: 27, of which 11 were waited for; matrix products, arithmetic and copies ran while one was open for 1% of the time, Pallas kernels for 14%

profile of v3, /device:TPU:1, one launch (start us, length us, event | category | flops | bytes accessed | tf_op | source)
XLA Modules:
  0.0 126.3 jit_solution(3630525611368800218)
XLA Ops:
  0.7 3.2 %pack.1 = (bf16[2,16,8,512]{3,2,1,0:T(8,128)(2,1)}, bf16[7,64,512]{2,1,0:T(8,128)(2,1)}, bf16[7,64,512]{2,1,0:T(8,128)(2,1)}, bf16[2,8,8,512]{3,2,1,0:T(8,128)(2,1)}) custom-call(bf16[16,64,512]{2,1,0:T(8,128)(2,1)} %x_ref.5, bf16[16,64,512]{2,1,0:T(8,128)(2,1)} %cot_ref.7, s32[16]{0:T(128)} %mask.1), custom_call_target="tpu_custom_call" | custom-call | tf_op jit(solution)/shard_map/pack/pallas_call | solution.py:503
  3.9 2.7 %collective-permute-start = (bf16[2,16,8,512]{3,2,1,0:T(8,128)(2,1)}, bf16[2,16,8,512]{3,2,1,0:T(8,128)(2,1)S(1)}, u32[]{:S(2)}, u32[]{:S(2)}) collective-permute-start(bf16[2,16,8,512]{3,2,1,0:T(8,128)(2,1)} %get-tuple-element.37), channel_id=1, source_target_pairs={{0,1},{1,2},{2,3},{3,4},{4,5},{5,6},{6,7},{7,8},{8,9},{9,10},{10,1... | collective-permute-start | bytes 786440 | tf_op jit(solution)/shard_map/ppermute | solution.py:488
  6.6 5.6 %collective-permute-start.1 = (bf16[7,64,512]{2,1,0:T(8,128)(2,1)}, bf16[7,64,512]{2,1,0:T(8,128)(2,1)}, u32[]{:S(2)}, u32[]{:S(2)}) collective-permute-start(bf16[7,64,512]{2,1,0:T(8,128)(2,1)} %get-tuple-element.41), channel_id=1, source_target_pairs={{0,16},{1,17},{2,18},{3,19},{4,20},{5,21},{6,22},{7,23},{8,24},{9,... | collective-permute-start | bytes 1376264 | tf_op jit(solution)/shard_map/ppermute | solution.py:488
  12.2 2.7 %collective-permute-start.2 = (bf16[2,8,8,512]{3,2,1,0:T(8,128)(2,1)}, bf16[2,8,8,512]{3,2,1,0:T(8,128)(2,1)S(1)}, u32[]{:S(2)}, u32[]{:S(2)}) collective-permute-start(bf16[2,8,8,512]{3,2,1,0:T(8,128)(2,1)} %get-tuple-element.42), channel_id=1, source_target_pairs={{0,17},{1,18},{2,19},{3,20},{4,21},{5,22},{6,23},{7,24},{8,25},{9,... | collective-permute-start | bytes 393224 | tf_op jit(solution)/shard_map/ppermute | solution.py:488
  14.9 5.6 %collective-permute-start.3 = (bf16[7,64,512]{2,1,0:T(8,128)(2,1)}, bf16[7,64,512]{2,1,0:T(8,128)(2,1)}, u32[]{:S(2)}, u32[]{:S(2)}) collective-permute-start(bf16[7,64,512]{2,1,0:T(8,128)(2,1)} %get-tuple-element.46), channel_id=1, source_target_pairs={{0,16},{1,17},{2,18},{3,19},{4,20},{5,21},{6,22},{7,23},{8,24},{9,... | collective-permute-start | bytes 1376264 | tf_op jit(solution)/shard_map/ppermute | solution.py:488
  20.5 0.1 concatenate.3.meta
  20.6 0.7 copy-done.5
  21.3 0.8 prepare.1
  22.2 0.3 copy-done.2
  22.5 10.5 %inner.1 = (bf16[512,512]{1,0:T(8,128)(2,1)S(1)}, bf16[1536,512]{1,0:T(8,128)(2,1)S(1)}, f32[512,2048]{1,0:T(8,128)S(1)}, f32[16,64,128]{2,1,0:T(8,128)S(1)}) custom-call(s32[22]{0:T(128)S(1)} %concatenate.3.meta, bf16[16,64,512]{2,1,0:T(8,128)(2,1)S(1)} %copy-done.2, bf16[16,64,512]{2,1,0:T(8,128)(2,1)S(1)} %copy-done, ...), custom_call_target="tpu_custom_call" | custom-call | flops 8000000000 | bytes 16777216 | tf_op jit(solution)/shard_map/inner/pallas_call | solution.py:533
  33.0 2.9 %front.1 = (bf16[512,512]{1,0:T(8,128)(2,1)S(1)}, bf16[512,512]{1,0:T(8,128)(2,1)S(1)}, bf16[1536,512]{1,0:T(8,128)(2,1)S(1)}, bf16[512,1024]{1,0:T(8,128)(2,1)S(1)}) custom-call(s32[22]{0:T(128)S(1)} %concatenate.3.meta, bf16[16,64,512]{2,1,0:T(8,128)(2,1)S(1)} %copy-done.2, bf16[2,16,8,512]{3,2,1,0:T(8,128)(2,1)S(1)} %collective-permute-done.side_ref, ...), custom_call_target="tpu_custom_call" | custom-call | flops 3000000000 | bytes 8388608 | tf_op jit(solution)/shard_map/front/pallas_call | solution.py:556
  35.9 11.4 %outer.1 = (bf16[1536,512]{1,0:T(8,128)(2,1)S(1)}, f32[16,16,2176]{2,1,0:T(8,128)S(1)}, bf16[16,16,2176]{2,1,0:T(8,128)(2,1)S(1)}) custom-call(s32[22]{0:T(128)S(1)} %concatenate.3.meta, bf16[16,64,512]{2,1,0:T(8,128)(2,1)S(1)} %copy-done, bf16[2,16,8,512]{3,2,1,0:T(8,128)(2,1)S(1)} %collective-permute-done.side_ref, ...), custom_call_target="tpu_custom_call" | custom-call | flops 10000000000 | bytes 25165824 | tf_op jit(solution)/shard_map/outer/pallas_call | solution.py:569
  47.3 0.6 collective-permute-start.4
  47.9 2.4 %collective-permute-done.4.got_ref = bf16[16,16,2176]{2,1,0:T(8,128)(2,1)S(1)} collective-permute-done((bf16[16,16,2176]{2,1,0:T(8,128)(2,1)S(1)}, bf16[16,16,2176]{2,1,0:T(8,128)(2,1)S(1)}, u32[]{:S(2)}, u32[]{:S(2)}) %collective-permute-start.4) | collective-permute-done | bytes 1114144 | tf_op jit(solution)/shard_map/ppermute | solution.py:428
  50.3 0.2 add_c.1
  50.5 1.3 %collective-permute-start.6 = (bf16[4,16,2176]{2,1,0:T(8,128)(2,1)S(1)}, bf16[4,16,2176]{2,1,0:T(8,128)(2,1)S(1)}, u32[]{:S(2)}, u32[]{:S(2)}) collective-permute-start(bf16[4,16,2176]{2,1,0:T(8,128)(2,1)S(1)} %get-tuple-element.58), channel_id=1, source_target_pairs={{0,2},{1,3},{2,4},{3,5},{4,6},{5,7},{6,0},{7,1},{8,10},{9,11},{10,... | collective-permute-start | bytes 835592 | tf_op jit(solution)/shard_map/ppermute | solution.py:428
  51.8 2.1 %collective-permute-start.7 = (bf16[4,16,2176]{2,1,0:T(8,128)(2,1)S(1)}, bf16[4,16,2176]{2,1,0:T(8,128)(2,1)S(1)}, u32[]{:S(2)}, u32[]{:S(2)}) collective-permute-start(bf16[4,16,2176]{2,1,0:T(8,128)(2,1)S(1)} %get-tuple-element.59), channel_id=1, source_target_pairs={{0,4},{1,5},{2,6},{3,7},{4,0},{5,1},{6,2},{7,3},{8,12},{9,13},{10,... | collective-permute-start | bytes 835592 | tf_op jit(solution)/shard_map/ppermute | solution.py:428
  53.9 1.2 collective-permute-start.8
  55.1 3.7 %cells.1 = (bf16[16,64,512]{2,1,0:T(8,128)(2,1)S(1)}, bf16[7,72,512]{2,1,0:T(8,128)(2,1)S(1)}, bf16[16,8,512]{2,1,0:T(8,128)(2,1)S(1)}) custom-call(s32[22]{0:T(128)S(1)} %concatenate.3.meta, bf16[512,512]{1,0:T(8,128)(2,1)S(1)} %get-tuple-element.40.xi_ref, bf16[512,512]{1,0:T(8,128)(2,1)S(1)} %get-tuple-element.44.xo_ref, ...), custom_call_target="tpu_custom_call" | custom-call | flops 1600000000 | bytes 12582912 | tf_op jit(solution)/shard_map/cells/pallas_call | solution.py:593
  58.8 1.3 %collective-permute-start.5 = (bf16[7,72,512]{2,1,0:T(8,128)(2,1)S(1)}, bf16[7,72,512]{2,1,0:T(8,128)(2,1)S(1)}, u32[]{:S(2)}, u32[]{:S(2)}) collective-permute-start(bf16[7,72,512]{2,1,0:T(8,128)(2,1)S(1)} %get-tuple-element.56), channel_id=1, source_target_pairs={{16,0},{17,1},{18,2},{19,3},{20,4},{21,5},{22,6},{23,7},{24,8},{25... | collective-permute-start | bytes 1548296 | tf_op jit(solution)/shard_map/ppermute | solution.py:488
  60.1 6.2 %collective-permute-done.7.refs_1_ = bf16[4,16,2176]{2,1,0:T(8,128)(2,1)S(1)} collective-permute-done((bf16[4,16,2176]{2,1,0:T(8,128)(2,1)S(1)}, bf16[4,16,2176]{2,1,0:T(8,128)(2,1)S(1)}, u32[]{:S(2)}, u32[]{:S(2)}) %collective-permute-start.7) | collective-permute-done | bytes 278560 | tf_op jit(solution)/shard_map/ppermute | solution.py:428
  66.3 0.1 add_x.1
  66.4 0.3 collective-permute-start.9
  66.8 4.4 %collective-permute-start.10 = (bf16[1,16,2176]{2,1,0:T(8,128)(2,1)S(1)}, bf16[1,16,2176]{2,1,0:T(8,128)(2,1)S(1)}, u32[]{:S(2)}, u32[]{:S(2)}) collective-permute-start(bf16[1,16,2176]{2,1,0:T(8,128)(2,1)S(1)} %get-tuple-element.63), channel_id=1, source_target_pairs={{0,16},{1,17},{2,18},{3,19},{4,20},{5,21},{6,22},{7,23},{8,24},{9,... | collective-permute-start | bytes 208904 | tf_op jit(solution)/shard_map/ppermute | solution.py:428
  71.2 7.0 %collective-permute-done.9.refs_0_ = bf16[1,16,2176]{2,1,0:T(8,128)(2,1)S(1)} collective-permute-done((bf16[1,16,2176]{2,1,0:T(8,128)(2,1)S(1)}, bf16[1,16,2176]{2,1,0:T(8,128)(2,1)S(1)}, u32[]{:S(2)}, u32[]{:S(2)}) %collective-permute-start.9) | collective-permute-done | bytes 69664 | tf_op jit(solution)/shard_map/ppermute | solution.py:428
  78.1 0.1 collective-permute-done.10.refs_1_
  78.2 1.2 collective-permute-done.11.refs_2_
  79.5 1.7 %collective-permute-start.12 = (bf16[1,16,2176]{2,1,0:T(8,128)(2,1)S(1)}, bf16[1,16,2176]{2,1,0:T(8,128)(2,1)S(1)}, u32[]{:S(2)}, u32[]{:S(2)}) collective-permute-start(bf16[1,16,2176]{2,1,0:T(8,128)(2,1)S(1)} %add_y.1.refs_0_), channel_id=1, source_target_pairs={{0,32},{1,33},{2,34},{3,35},{4,36},{5,37},{6,38},{7,39},{8,40},{9,... | collective-permute-start | bytes 208904 | tf_op jit(solution)/shard_map/ppermute | solution.py:428
  81.1 4.7 %collective-permute-start.13 = (bf16[1,16,2176]{2,1,0:T(8,128)(2,1)S(1)}, bf16[1,16,2176]{2,1,0:T(8,128)(2,1)S(1)}, u32[]{:S(2)}, u32[]{:S(2)}) collective-permute-start(bf16[1,16,2176]{2,1,0:T(8,128)(2,1)S(1)} %add_y.1.refs_0_), channel_id=1, source_target_pairs={{0,64},{1,65},{2,66},{3,67},{4,68},{5,69},{6,70},{7,71},{8,72},{9,... | collective-permute-start | bytes 208904 | tf_op jit(solution)/shard_map/ppermute | solution.py:428
  85.8 1.8 %collective-permute-done.13.refs_2_ = bf16[1,16,2176]{2,1,0:T(8,128)(2,1)S(1)} collective-permute-done((bf16[1,16,2176]{2,1,0:T(8,128)(2,1)S(1)}, bf16[1,16,2176]{2,1,0:T(8,128)(2,1)S(1)}, u32[]{:S(2)}, u32[]{:S(2)}) %collective-permute-start.13) | collective-permute-done | bytes 69664 | tf_op jit(solution)/shard_map/ppermute | solution.py:428
  87.7 3.2 %collective-permute-done.14.refs_3_ = bf16[1,16,2176]{2,1,0:T(8,128)(2,1)S(1)} collective-permute-done((bf16[1,16,2176]{2,1,0:T(8,128)(2,1)S(1)}, bf16[1,16,2176]{2,1,0:T(8,128)(2,1)S(1)}, u32[]{:S(2)}, u32[]{:S(2)}) %collective-permute-start.14) | collective-permute-done | bytes 69664 | tf_op jit(solution)/shard_map/ppermute | solution.py:428
  90.9 4.0 %collective-permute-start.15 = (bf16[1,16,2176]{2,1,0:T(8,128)(2,1)S(1)}, bf16[1,16,2176]{2,1,0:T(8,128)(2,1)S(1)}, u32[]{:S(2)}, u32[]{:S(2)}) collective-permute-start(bf16[1,16,2176]{2,1,0:T(8,128)(2,1)S(1)} %add_z.2.refs_0_), channel_id=1, source_target_pairs={{0,192},{1,193},{2,194},{3,195},{4,196},{5,197},{6,198},{7,199},{8... | collective-permute-start | bytes 208904 | tf_op jit(solution)/shard_map/ppermute | solution.py:428
  94.9 1.8 %collective-permute-done.15.refs_1_ = bf16[1,16,2176]{2,1,0:T(8,128)(2,1)S(1)} collective-permute-done((bf16[1,16,2176]{2,1,0:T(8,128)(2,1)S(1)}, bf16[1,16,2176]{2,1,0:T(8,128)(2,1)S(1)}, u32[]{:S(2)}, u32[]{:S(2)}) %collective-permute-start.15) | collective-permute-done | bytes 69664 | tf_op jit(solution)/shard_map/ppermute | solution.py:428
  96.8 2.4 %collective-permute-start.16 = (bf16[1,16,2176]{2,1,0:T(8,128)(2,1)S(1)}, bf16[1,16,2176]{2,1,0:T(8,128)(2,1)S(1)}, u32[]{:S(2)}, u32[]{:S(2)}) collective-permute-start(bf16[1,16,2176]{2,1,0:T(8,128)(2,1)S(1)} %add_z.3.refs_0_), channel_id=1, source_target_pairs={{0,24},{1,25},{2,26},{3,27},{4,28},{5,29},{6,30},{7,31},{8,0},{9,1... | collective-permute-start | bytes 208904 | tf_op jit(solution)/shard_map/ppermute | solution.py:428
  99.2 0.4 collective-permute-start.17
  99.6 0.5 collective-permute-start.18
  100.1 0.4 collective-permute-done.16.refs_1_
  100.6 3.4 %collective-permute-done.17.refs_2_ = bf16[1,16,2176]{2,1,0:T(8,128)(2,1)S(1)} collective-permute-done((bf16[1,16,2176]{2,1,0:T(8,128)(2,1)S(1)}, bf16[1,16,2176]{2,1,0:T(8,128)(2,1)S(1)}, u32[]{:S(2)}, u32[]{:S(2)}) %collective-permute-start.17) | collective-permute-done | bytes 69664 | tf_op jit(solution)/shard_map/ppermute | solution.py:428
  103.9 0.7 collective-permute-done.18.refs_3_
  104.6 0.1 collective-permute-start.20
  104.7 2.0 %collective-permute-start.21 = (bf16[4,16,2176]{2,1,0:T(8,128)(2,1)S(1)}, bf16[4,16,2176]{2,1,0:T(8,128)(2,1)S(1)}, u32[]{:S(2)}, u32[]{:S(2)}) collective-permute-start(bf16[4,16,2176]{2,1,0:T(8,128)(2,1)S(1)} %join.1._.refs_0_), channel_id=1, source_target_pairs={{0,4},{1,5},{2,6},{3,7},{4,0},{5,1},{6,2},{7,3},{8,12},{9,13},{10,... | collective-permute-start | bytes 835592 | tf_op jit(solution)/shard_map/ppermute | solution.py:428
  106.8 5.1 %collective-permute-start.19 = (bf16[16,8,512]{2,1,0:T(8,128)(2,1)S(1)}, bf16[16,8,512]{2,1,0:T(8,128)(2,1)S(1)}, u32[]{:S(2)}, u32[]{:S(2)}) collective-permute-start(bf16[16,8,512]{2,1,0:T(8,128)(2,1)S(1)} %edge.1), channel_id=1, source_target_pairs={{0,15},{1,0},{2,1},{3,2},{4,3},{5,4},{6,5},{7,6},{8,7},{9,8},{10,9... | collective-permute-start | bytes 393224 | tf_op jit(solution)/shard_map/ppermute | solution.py:488
  111.9 0.1 collective-permute-start.23
  112.0 4.8 %collective-permute-start.24 = (bf16[4,16,2176]{2,1,0:T(8,128)(2,1)S(1)}, bf16[4,16,2176]{2,1,0:T(8,128)(2,1)S(1)}, u32[]{:S(2)}, u32[]{:S(2)}) collective-permute-start(bf16[4,16,2176]{2,1,0:T(8,128)(2,1)S(1)} %collective-permute-done.20.refs_1_), channel_id=1, source_target_pairs={{0,1},{1,0},{2,3},{3,2},{4,5},{5,4},{6,7},{7,6},{8,9},{9,8},{10,11... | collective-permute-start | bytes 835592 | tf_op jit(solution)/shard_map/ppermute | solution.py:428
  116.8 1.7 %collective-permute-start.25 = (bf16[4,16,2176]{2,1,0:T(8,128)(2,1)S(1)}, bf16[4,16,2176]{2,1,0:T(8,128)(2,1)S(1)}, u32[]{:S(2)}, u32[]{:S(2)}) collective-permute-start(bf16[4,16,2176]{2,1,0:T(8,128)(2,1)S(1)} %collective-permute-done.21.refs_2_), channel_id=1, source_target_pairs={{0,1},{1,0},{2,3},{3,2},{4,5},{5,4},{6,7},{7,6},{8,9},{9,8},{10,11... | collective-permute-start | bytes 835592 | tf_op jit(solution)/shard_map/ppermute | solution.py:428
  118.5 2.9 %collective-permute-start.26 = (bf16[4,16,2176]{2,1,0:T(8,128)(2,1)S(1)}, bf16[4,16,2176]{2,1,0:T(8,128)(2,1)S(1)}, u32[]{:S(2)}, u32[]{:S(2)}) collective-permute-start(bf16[4,16,2176]{2,1,0:T(8,128)(2,1)S(1)} %collective-permute-done.22.refs_3_), channel_id=1, source_target_pairs={{0,1},{1,0},{2,3},{3,2},{4,5},{5,4},{6,7},{7,6},{8,9},{9,8},{10,11... | collective-permute-start | bytes 835592 | tf_op jit(solution)/shard_map/ppermute | solution.py:428
  121.4 1.2 add_convert_fusion
  122.6 3.5 %unpack.1 = (f32[512,1536]{1,0:T(8,128)}, f32[512,512]{1,0:T(8,128)}, f32[1,512]{1,0:T(1,128)}, f32[16,225]{1,0:T(8,128)}) custom-call(s32[22]{0:T(128)S(1)} %concatenate.3.meta, bf16[4,16,2176]{2,1,0:T(8,128)(2,1)S(1)} %join.1._.refs_0_, bf16[4,16,2176]{2,1,0:T(8,128)(2,1)S(1)} %collective-permute-done.20.refs_1_, ...), custom_call_target="tpu_custom_call" | custom-call | tf_op jit(solution)/shard_map/unpack/pallas_call | solution.py:627
  (39 shorter events, 0.3 us)
Async XLA Ops:
  0.6 19.9 %copy-start.6 = (s32[16]{0:T(128)S(1)}, s32[16]{0:T(128)}, u32[]{:S(2)}) copy-start(s32[16]{0:T(128)} %mask.1) | copy-start | bytes 196
  0.6 19.8 %copy-start.7 = (s32[2]{0:T(128)S(1)}, s32[2]{0:T(128)}, u32[]{:S(2)}) copy-start(s32[2]{0:T(128)} %param.11) | copy-start | bytes 28
  0.7 19.9 %copy-start.1 = (bf16[512,1536]{1,0:T(8,128)(2,1)S(1)}, bf16[512,1536]{1,0:T(8,128)(2,1)}, u32[]{:S(2)}) copy-start(bf16[512,1536]{1,0:T(8,128)(2,1)} %w_ref.9) | copy-start | bytes 4718596
  3.9 18.3 %copy-start = (bf16[16,64,512]{2,1,0:T(8,128)(2,1)S(1)}, bf16[16,64,512]{2,1,0:T(8,128)(2,1)}, u32[]{:S(2)}) copy-start(bf16[16,64,512]{2,1,0:T(8,128)(2,1)} %cot_ref.7) | copy-start | bytes 3145732
  3.9 18.3 %copy-start.3 = (f32[512]{0:T(512)S(1)}, f32[512]{0:T(512)}, u32[]{:S(2)}) copy-start(f32[512]{0:T(512)} %param.12) | copy-start | bytes 6148
  3.9 18.3 %copy-start.4 = (bf16[512,512]{1,0:T(8,128)(2,1)S(1)}, bf16[512,512]{1,0:T(8,128)(2,1)}, u32[]{:S(2)}) copy-start(bf16[512,512]{1,0:T(8,128)(2,1)} %wo_ref.3) | copy-start | bytes 1572868
  3.9 18.3 %collective-permute-start = (bf16[2,16,8,512]{3,2,1,0:T(8,128)(2,1)}, bf16[2,16,8,512]{3,2,1,0:T(8,128)(2,1)S(1)}, u32[]{:S(2)}, u32[]{:S(2)}) collective-permute-start(bf16[2,16,8,512]{3,2,1,0:T(8,128)(2,1)} %get-tuple-element.37), channel_id=1, source_target_pairs={{0,1},{1,2},{2,3},{3,4},{4,5},{5,6},{6,7},{7,8},{8,9},{9,10},{10,1... | collective-permute-start | bytes 786440 | tf_op jit(solution)/shard_map/ppermute | solution.py:488
  6.6 26.5 %collective-permute-start.1 = (bf16[7,64,512]{2,1,0:T(8,128)(2,1)}, bf16[7,64,512]{2,1,0:T(8,128)(2,1)}, u32[]{:S(2)}, u32[]{:S(2)}) collective-permute-start(bf16[7,64,512]{2,1,0:T(8,128)(2,1)} %get-tuple-element.41), channel_id=1, source_target_pairs={{0,16},{1,17},{2,18},{3,19},{4,20},{5,21},{6,22},{7,23},{8,24},{9,... | collective-permute-start | bytes 1376264 | tf_op jit(solution)/shard_map/ppermute | solution.py:488
  12.2 20.9 %collective-permute-start.2 = (bf16[2,8,8,512]{3,2,1,0:T(8,128)(2,1)}, bf16[2,8,8,512]{3,2,1,0:T(8,128)(2,1)S(1)}, u32[]{:S(2)}, u32[]{:S(2)}) collective-permute-start(bf16[2,8,8,512]{3,2,1,0:T(8,128)(2,1)} %get-tuple-element.42), channel_id=1, source_target_pairs={{0,17},{1,18},{2,19},{3,20},{4,21},{5,22},{6,23},{7,24},{8,25},{9,... | collective-permute-start | bytes 393224 | tf_op jit(solution)/shard_map/ppermute | solution.py:488
  14.9 21.0 %collective-permute-start.3 = (bf16[7,64,512]{2,1,0:T(8,128)(2,1)}, bf16[7,64,512]{2,1,0:T(8,128)(2,1)}, u32[]{:S(2)}, u32[]{:S(2)}) collective-permute-start(bf16[7,64,512]{2,1,0:T(8,128)(2,1)} %get-tuple-element.46), channel_id=1, source_target_pairs={{0,16},{1,17},{2,18},{3,19},{4,20},{5,21},{6,22},{7,23},{8,24},{9,... | collective-permute-start | bytes 1376264 | tf_op jit(solution)/shard_map/ppermute | solution.py:488
  20.6 0.7 copy-start.5
  21.3 1.2 copy-start.2
  47.3 3.0 %collective-permute-start.4 = (bf16[16,16,2176]{2,1,0:T(8,128)(2,1)S(1)}, bf16[16,16,2176]{2,1,0:T(8,128)(2,1)S(1)}, u32[]{:S(2)}, u32[]{:S(2)}) collective-permute-start(bf16[16,16,2176]{2,1,0:T(8,128)(2,1)S(1)} %get-tuple-element.53), channel_id=1, source_target_pairs={{0,1},{1,0},{2,3},{3,2},{4,5},{5,4},{6,7},{7,6},{8,9},{9,8},{10,11... | collective-permute-start | bytes 3342344 | tf_op jit(solution)/shard_map/ppermute | solution.py:428
  50.5 9.7 %collective-permute-start.6 = (bf16[4,16,2176]{2,1,0:T(8,128)(2,1)S(1)}, bf16[4,16,2176]{2,1,0:T(8,128)(2,1)S(1)}, u32[]{:S(2)}, u32[]{:S(2)}) collective-permute-start(bf16[4,16,2176]{2,1,0:T(8,128)(2,1)S(1)} %get-tuple-element.58), channel_id=1, source_target_pairs={{0,2},{1,3},{2,4},{3,5},{4,6},{5,7},{6,0},{7,1},{8,10},{9,11},{10,... | collective-permute-start | bytes 835592 | tf_op jit(solution)/shard_map/ppermute | solution.py:428
  51.8 14.5 %collective-permute-start.7 = (bf16[4,16,2176]{2,1,0:T(8,128)(2,1)S(1)}, bf16[4,16,2176]{2,1,0:T(8,128)(2,1)S(1)}, u32[]{:S(2)}, u32[]{:S(2)}) collective-permute-start(bf16[4,16,2176]{2,1,0:T(8,128)(2,1)S(1)} %get-tuple-element.59), channel_id=1, source_target_pairs={{0,4},{1,5},{2,6},{3,7},{4,0},{5,1},{6,2},{7,3},{8,12},{9,13},{10,... | collective-permute-start | bytes 835592 | tf_op jit(solution)/shard_map/ppermute | solution.py:428
  53.9 12.4 %collective-permute-start.8 = (bf16[4,16,2176]{2,1,0:T(8,128)(2,1)S(1)}, bf16[4,16,2176]{2,1,0:T(8,128)(2,1)S(1)}, u32[]{:S(2)}, u32[]{:S(2)}) collective-permute-start(bf16[4,16,2176]{2,1,0:T(8,128)(2,1)S(1)} %get-tuple-element.60), channel_id=1, source_target_pairs={{0,6},{1,7},{2,0},{3,1},{4,2},{5,3},{6,4},{7,5},{8,14},{9,15},{10,... | collective-permute-start | bytes 835592 | tf_op jit(solution)/shard_map/ppermute | solution.py:428
  58.8 47.9 %collective-permute-start.5 = (bf16[7,72,512]{2,1,0:T(8,128)(2,1)S(1)}, bf16[7,72,512]{2,1,0:T(8,128)(2,1)S(1)}, u32[]{:S(2)}, u32[]{:S(2)}) collective-permute-start(bf16[7,72,512]{2,1,0:T(8,128)(2,1)S(1)} %get-tuple-element.56), channel_id=1, source_target_pairs={{16,0},{17,1},{18,2},{19,3},{20,4},{21,5},{22,6},{23,7},{24,8},{25... | collective-permute-start | bytes 1548296 | tf_op jit(solution)/shard_map/ppermute | solution.py:488
  66.4 11.7 %collective-permute-start.9 = (bf16[1,16,2176]{2,1,0:T(8,128)(2,1)S(1)}, bf16[1,16,2176]{2,1,0:T(8,128)(2,1)S(1)}, u32[]{:S(2)}, u32[]{:S(2)}) collective-permute-start(bf16[1,16,2176]{2,1,0:T(8,128)(2,1)S(1)} %get-tuple-element.62), channel_id=1, source_target_pairs={{0,8},{1,9},{2,10},{3,11},{4,12},{5,13},{6,14},{7,15},{8,16},{9,17... | collective-permute-start | bytes 208904 | tf_op jit(solution)/shard_map/ppermute | solution.py:428
  66.8 11.4 %collective-permute-start.10 = (bf16[1,16,2176]{2,1,0:T(8,128)(2,1)S(1)}, bf16[1,16,2176]{2,1,0:T(8,128)(2,1)S(1)}, u32[]{:S(2)}, u32[]{:S(2)}) collective-permute-start(bf16[1,16,2176]{2,1,0:T(8,128)(2,1)S(1)} %get-tuple-element.63), channel_id=1, source_target_pairs={{0,16},{1,17},{2,18},{3,19},{4,20},{5,21},{6,22},{7,23},{8,24},{9,... | collective-permute-start | bytes 208904 | tf_op jit(solution)/shard_map/ppermute | solution.py:428
  71.2 8.2 %collective-permute-start.11 = (bf16[1,16,2176]{2,1,0:T(8,128)(2,1)S(1)}, bf16[1,16,2176]{2,1,0:T(8,128)(2,1)S(1)}, u32[]{:S(2)}, u32[]{:S(2)}) collective-permute-start(bf16[1,16,2176]{2,1,0:T(8,128)(2,1)S(1)} %get-tuple-element.64), channel_id=1, source_target_pairs={{0,24},{1,25},{2,26},{3,27},{4,28},{5,29},{6,30},{7,31},{8,0},{9,1... | collective-permute-start | bytes 208904 | tf_op jit(solution)/shard_map/ppermute | solution.py:428
  79.5 6.4 %collective-permute-start.12 = (bf16[1,16,2176]{2,1,0:T(8,128)(2,1)S(1)}, bf16[1,16,2176]{2,1,0:T(8,128)(2,1)S(1)}, u32[]{:S(2)}, u32[]{:S(2)}) collective-permute-start(bf16[1,16,2176]{2,1,0:T(8,128)(2,1)S(1)} %add_y.1.refs_0_), channel_id=1, source_target_pairs={{0,32},{1,33},{2,34},{3,35},{4,36},{5,37},{6,38},{7,39},{8,40},{9,... | collective-permute-start | bytes 208904 | tf_op jit(solution)/shard_map/ppermute | solution.py:428
  81.1 6.5 %collective-permute-start.13 = (bf16[1,16,2176]{2,1,0:T(8,128)(2,1)S(1)}, bf16[1,16,2176]{2,1,0:T(8,128)(2,1)S(1)}, u32[]{:S(2)}, u32[]{:S(2)}) collective-permute-start(bf16[1,16,2176]{2,1,0:T(8,128)(2,1)S(1)} %add_y.1.refs_0_), channel_id=1, source_target_pairs={{0,64},{1,65},{2,66},{3,67},{4,68},{5,69},{6,70},{7,71},{8,72},{9,... | collective-permute-start | bytes 208904 | tf_op jit(solution)/shard_map/ppermute | solution.py:428
  85.8 5.1 %collective-permute-start.14 = (bf16[1,16,2176]{2,1,0:T(8,128)(2,1)S(1)}, bf16[1,16,2176]{2,1,0:T(8,128)(2,1)S(1)}, u32[]{:S(2)}, u32[]{:S(2)}) collective-permute-start(bf16[1,16,2176]{2,1,0:T(8,128)(2,1)S(1)} %add_y.1.refs_0_), channel_id=1, source_target_pairs={{0,96},{1,97},{2,98},{3,99},{4,100},{5,101},{6,102},{7,103},{8,104... | collective-permute-start | bytes 208904 | tf_op jit(solution)/shard_map/ppermute | solution.py:428
  90.9 5.8 %collective-permute-start.15 = (bf16[1,16,2176]{2,1,0:T(8,128)(2,1)S(1)}, bf16[1,16,2176]{2,1,0:T(8,128)(2,1)S(1)}, u32[]{:S(2)}, u32[]{:S(2)}) collective-permute-start(bf16[1,16,2176]{2,1,0:T(8,128)(2,1)S(1)} %add_z.2.refs_0_), channel_id=1, source_target_pairs={{0,192},{1,193},{2,194},{3,195},{4,196},{5,197},{6,198},{7,199},{8... | collective-permute-start | bytes 208904 | tf_op jit(solution)/shard_map/ppermute | solution.py:428
  96.8 3.8 %collective-permute-start.16 = (bf16[1,16,2176]{2,1,0:T(8,128)(2,1)S(1)}, bf16[1,16,2176]{2,1,0:T(8,128)(2,1)S(1)}, u32[]{:S(2)}, u32[]{:S(2)}) collective-permute-start(bf16[1,16,2176]{2,1,0:T(8,128)(2,1)S(1)} %add_z.3.refs_0_), channel_id=1, source_target_pairs={{0,24},{1,25},{2,26},{3,27},{4,28},{5,29},{6,30},{7,31},{8,0},{9,1... | collective-permute-start | bytes 208904 | tf_op jit(solution)/shard_map/ppermute | solution.py:428
  99.2 4.7 %collective-permute-start.17 = (bf16[1,16,2176]{2,1,0:T(8,128)(2,1)S(1)}, bf16[1,16,2176]{2,1,0:T(8,128)(2,1)S(1)}, u32[]{:S(2)}, u32[]{:S(2)}) collective-permute-start(bf16[1,16,2176]{2,1,0:T(8,128)(2,1)S(1)} %add_z.3.refs_0_), channel_id=1, source_target_pairs={{0,16},{1,17},{2,18},{3,19},{4,20},{5,21},{6,22},{7,23},{8,24},{9,... | collective-permute-start | bytes 208904 | tf_op jit(solution)/shard_map/ppermute | solution.py:428
  99.6 5.0 %collective-permute-start.18 = (bf16[1,16,2176]{2,1,0:T(8,128)(2,1)S(1)}, bf16[1,16,2176]{2,1,0:T(8,128)(2,1)S(1)}, u32[]{:S(2)}, u32[]{:S(2)}) collective-permute-start(bf16[1,16,2176]{2,1,0:T(8,128)(2,1)S(1)} %add_z.3.refs_0_), channel_id=1, source_target_pairs={{0,8},{1,9},{2,10},{3,11},{4,12},{5,13},{6,14},{7,15},{8,16},{9,17... | collective-permute-start | bytes 208904 | tf_op jit(solution)/shard_map/ppermute | solution.py:428
  104.6 7.4 %collective-permute-start.20 = (bf16[4,16,2176]{2,1,0:T(8,128)(2,1)S(1)}, bf16[4,16,2176]{2,1,0:T(8,128)(2,1)S(1)}, u32[]{:S(2)}, u32[]{:S(2)}) collective-permute-start(bf16[4,16,2176]{2,1,0:T(8,128)(2,1)S(1)} %join.1._.refs_0_), channel_id=1, source_target_pairs={{0,6},{1,7},{2,0},{3,1},{4,2},{5,3},{6,4},{7,5},{8,14},{9,15},{10,... | collective-permute-start | bytes 835592 | tf_op jit(solution)/shard_map/ppermute | solution.py:428
  104.7 12.0 %collective-permute-start.21 = (bf16[4,16,2176]{2,1,0:T(8,128)(2,1)S(1)}, bf16[4,16,2176]{2,1,0:T(8,128)(2,1)S(1)}, u32[]{:S(2)}, u32[]{:S(2)}) collective-permute-start(bf16[4,16,2176]{2,1,0:T(8,128)(2,1)S(1)} %join.1._.refs_0_), channel_id=1, source_target_pairs={{0,4},{1,5},{2,6},{3,7},{4,0},{5,1},{6,2},{7,3},{8,12},{9,13},{10,... | collective-permute-start | bytes 835592 | tf_op jit(solution)/shard_map/ppermute | solution.py:428
  106.7 11.8 %collective-permute-start.22 = (bf16[4,16,2176]{2,1,0:T(8,128)(2,1)S(1)}, bf16[4,16,2176]{2,1,0:T(8,128)(2,1)S(1)}, u32[]{:S(2)}, u32[]{:S(2)}) collective-permute-start(bf16[4,16,2176]{2,1,0:T(8,128)(2,1)S(1)} %join.1._.refs_0_), channel_id=1, source_target_pairs={{0,2},{1,3},{2,4},{3,5},{4,6},{5,7},{6,0},{7,1},{8,10},{9,11},{10,... | collective-permute-start | bytes 835592 | tf_op jit(solution)/shard_map/ppermute | solution.py:428
  106.8 14.6 %collective-permute-start.19 = (bf16[16,8,512]{2,1,0:T(8,128)(2,1)S(1)}, bf16[16,8,512]{2,1,0:T(8,128)(2,1)S(1)}, u32[]{:S(2)}, u32[]{:S(2)}) collective-permute-start(bf16[16,8,512]{2,1,0:T(8,128)(2,1)S(1)} %edge.1), channel_id=1, source_target_pairs={{0,15},{1,0},{2,1},{3,2},{4,3},{5,4},{6,5},{7,6},{8,7},{9,8},{10,9... | collective-permute-start | bytes 393224 | tf_op jit(solution)/shard_map/ppermute | solution.py:488
  111.9 10.7 %collective-permute-start.23 = (bf16[4,16,2176]{2,1,0:T(8,128)(2,1)S(1)}, bf16[4,16,2176]{2,1,0:T(8,128)(2,1)S(1)}, u32[]{:S(2)}, u32[]{:S(2)}) collective-permute-start(bf16[4,16,2176]{2,1,0:T(8,128)(2,1)S(1)} %join.1._.refs_0_), channel_id=1, source_target_pairs={{0,1},{1,0},{2,3},{3,2},{4,5},{5,4},{6,7},{7,6},{8,9},{9,8},{10,11... | collective-permute-start | bytes 835592 | tf_op jit(solution)/shard_map/ppermute | solution.py:428
  112.0 10.6 %collective-permute-start.24 = (bf16[4,16,2176]{2,1,0:T(8,128)(2,1)S(1)}, bf16[4,16,2176]{2,1,0:T(8,128)(2,1)S(1)}, u32[]{:S(2)}, u32[]{:S(2)}) collective-permute-start(bf16[4,16,2176]{2,1,0:T(8,128)(2,1)S(1)} %collective-permute-done.20.refs_1_), channel_id=1, source_target_pairs={{0,1},{1,0},{2,3},{3,2},{4,5},{5,4},{6,7},{7,6},{8,9},{9,8},{10,11... | collective-permute-start | bytes 835592 | tf_op jit(solution)/shard_map/ppermute | solution.py:428
  116.8 5.8 %collective-permute-start.25 = (bf16[4,16,2176]{2,1,0:T(8,128)(2,1)S(1)}, bf16[4,16,2176]{2,1,0:T(8,128)(2,1)S(1)}, u32[]{:S(2)}, u32[]{:S(2)}) collective-permute-start(bf16[4,16,2176]{2,1,0:T(8,128)(2,1)S(1)} %collective-permute-done.21.refs_2_), channel_id=1, source_target_pairs={{0,1},{1,0},{2,3},{3,2},{4,5},{5,4},{6,7},{7,6},{8,9},{9,8},{10,11... | collective-permute-start | bytes 835592 | tf_op jit(solution)/shard_map/ppermute | solution.py:428
  118.5 4.1 %collective-permute-start.26 = (bf16[4,16,2176]{2,1,0:T(8,128)(2,1)S(1)}, bf16[4,16,2176]{2,1,0:T(8,128)(2,1)S(1)}, u32[]{:S(2)}, u32[]{:S(2)}) collective-permute-start(bf16[4,16,2176]{2,1,0:T(8,128)(2,1)S(1)} %collective-permute-done.22.refs_3_), channel_id=1, source_target_pairs={{0,1},{1,0},{2,3},{3,2},{4,5},{5,4},{6,7},{7,6},{8,9},{9,8},{10,11... | collective-permute-start | bytes 835592 | tf_op jit(solution)/shard_map/ppermute | solution.py:428

commit v4 on v1

--- a/solution.py
+++ b/solution.py
@@ -69,8 +69,10 @@
     g_t = gm_t[pl.ds(c0, LANES), lanes]
     k_tok = kv[lanes, pl.ds(c0, LANES)]
     v_tok = kv[lanes, pl.ds(n_chan + c0, LANES)]
-    scores = dot(k_tok, block_diag(q_t, dim))
-    grads = dot(v_tok, block_diag(g_t, dim))
+    q_bd = block_diag(q_t, dim)
+    g_bd = block_diag(g_t, dim)
+    scores = dot(k_tok, q_bd)
+    grads = dot(v_tok, g_bd)
     first = lax.broadcasted_iota(jnp.int32, (CELLS, LANES), 1) < CELLS
     heads = LANES // dim
     mixed, dq, dk, dv = [], [], [], []
@@ -89,13 +91,13 @@
         a2 = jnp.concatenate([jnp.where(first, a, zero), jnp.where(first, zero, a)], 0).astype(jnp.bfloat16)
         ds2 = jnp.concatenate([jnp.where(first, ds, zero), jnp.where(first, zero, ds)], 0).astype(jnp.bfloat16)
         mixed.append(dot(v_t[rows], a2))
-        dv.append(dot(g_t[rows], a2, NT))
+        dv.append(a2)
         dq.append(dot(k_t[rows], ds2) * scale)
-        dk.append(dot(q_t[rows], ds2, NT))
+        dk.append(ds2)
     mix_t[pl.ds(c0, LANES), lanes] = jnp.concatenate(mixed, 0).astype(jnp.bfloat16)
     gp_t[pl.ds(c0, LANES), lanes] = jnp.concatenate(dq, 0).astype(jnp.bfloat16)
-    gp_t[pl.ds(n_chan + c0, LANES), lanes] = jnp.concatenate(dk, 0).astype(jnp.bfloat16)
-    gp_t[pl.ds(2 * n_chan + c0, LANES), lanes] = jnp.concatenate(dv, 0).astype(jnp.bfloat16)
+    gp_t[pl.ds(n_chan + c0, LANES), lanes] = dot(q_bd, jnp.concatenate(dk, 1), NT).astype(jnp.bfloat16)
+    gp_t[pl.ds(2 * n_chan + c0, LANES), lanes] = dot(g_bd, jnp.concatenate(dv, 1), NT).astype(jnp.bfloat16)
 
 
 def place_row(line, shift, out, r, live=None):
@@ -120,7 +122,7 @@
     mask = jnp.concatenate([(live[r][:, :LANES] - 1.0) * 1e30 for r in range(WINDOW)], 0)
     groups = n_chan // LANES
 
-    @pl.loop(0, n_tok // LANES)
+    @pl.loop(0, n_tok // LANES, unroll=2)
     def _(pair):
         for group in range(groups):
             attention_unit(n_chan, dim, scale, bias_ref, mask, proj_t, kv, gm_t, mix_t, gp_t, bsum_ref, pair, group)

time: 123 us -> 122 us (level)
  Pallas kernels: 36.8 us -> 35.5 us
where the time goes in v4:
time: 122 us
  starting transfers between devices  49.6 us (41%)
  Pallas kernels  35.5 us (29%)
  waiting for transfers between devices  33.5 us (27%)
    ppermute x21, starting transfers between devices, move(): return lax.ppermute(array, ('lat', 'lon'), pairs)  30.7 us
    ppermute x21, waiting for transfers between devices, move(): return lax.ppermute(array, ('lat', 'lon'), pairs)  24.3 us
    ppermute x6, starting transfers between devices, ring(): return lax.ppermute(array, ('lat', 'lon'), pairs)  18.9 us
    pallas_call x1, Pallas kernels, local(): pl.pallas_call(functools.partial(outer_kernel, n_head, counts), out_shape...  10.9 us
    pallas_call x1, Pallas kernels, local(): pl.pallas_call(functools.partial(inner_kernel, n_head), out_shape=(tile((...  10.4 us
    ppermute x6, waiting for transfers between devices, ring(): return lax.ppermute(array, ('lat', 'lon'), pairs)  9.19 us
    pallas_call x1, Pallas kernels, input_grad(): pl.pallas_call(cells_kernel, out_shape=(tile((n_rows, n_cols, n_chan)), t...  3.74 us
    pallas_call x1, Pallas kernels, local(): pl.pallas_call(functools.partial(pack_kernel, n_top), out_shape=(tile((2,...  3.19 us
  transfers between devices with their start and end apart: 27, of which 11 were waited for; matrix products, arithmetic and copies ran while one was open for 1% of the time, Pallas kernels for 15%

profile of v4, /device:TPU:1, one launch (start us, length us, event | category | flops | bytes accessed | tf_op | source)
XLA Modules:
  0.0 121.9 jit_solution(8437939986151905466)
XLA Ops:
  0.7 3.2 %pack.1 = (bf16[2,16,8,512]{3,2,1,0:T(8,128)(2,1)}, bf16[7,64,512]{2,1,0:T(8,128)(2,1)}, bf16[7,64,512]{2,1,0:T(8,128)(2,1)}, bf16[2,8,8,512]{3,2,1,0:T(8,128)(2,1)}) custom-call(bf16[16,64,512]{2,1,0:T(8,128)(2,1)} %x_ref.5, bf16[16,64,512]{2,1,0:T(8,128)(2,1)} %cot_ref.7, s32[16]{0:T(128)} %mask.1), custom_call_target="tpu_custom_call" | custom-call | tf_op jit(solution)/shard_map/pack/pallas_call | solution.py:493
  3.9 2.7 %collective-permute-start = (bf16[2,16,8,512]{3,2,1,0:T(8,128)(2,1)}, bf16[2,16,8,512]{3,2,1,0:T(8,128)(2,1)S(1)}, u32[]{:S(2)}, u32[]{:S(2)}) collective-permute-start(bf16[2,16,8,512]{3,2,1,0:T(8,128)(2,1)} %get-tuple-element.37), channel_id=1, source_target_pairs={{0,1},{1,2},{2,3},{3,4},{4,5},{5,6},{6,7},{7,8},{8,9},{9,10},{10,1... | collective-permute-start | bytes 786440 | tf_op jit(solution)/shard_map/ppermute | solution.py:478
  6.6 2.9 %collective-permute-start.1 = (bf16[7,64,512]{2,1,0:T(8,128)(2,1)}, bf16[7,64,512]{2,1,0:T(8,128)(2,1)}, u32[]{:S(2)}, u32[]{:S(2)}) collective-permute-start(bf16[7,64,512]{2,1,0:T(8,128)(2,1)} %get-tuple-element.41), channel_id=1, source_target_pairs={{0,16},{1,17},{2,18},{3,19},{4,20},{5,21},{6,22},{7,23},{8,24},{9,... | collective-permute-start | bytes 1376264 | tf_op jit(solution)/shard_map/ppermute | solution.py:478
  9.5 1.5 %collective-permute-start.2 = (bf16[2,8,8,512]{3,2,1,0:T(8,128)(2,1)}, bf16[2,8,8,512]{3,2,1,0:T(8,128)(2,1)S(1)}, u32[]{:S(2)}, u32[]{:S(2)}) collective-permute-start(bf16[2,8,8,512]{3,2,1,0:T(8,128)(2,1)} %get-tuple-element.42), channel_id=1, source_target_pairs={{0,17},{1,18},{2,19},{3,20},{4,21},{5,22},{6,23},{7,24},{8,25},{9,... | collective-permute-start | bytes 393224 | tf_op jit(solution)/shard_map/ppermute | solution.py:478
  11.0 2.9 %collective-permute-start.3 = (bf16[7,64,512]{2,1,0:T(8,128)(2,1)}, bf16[7,64,512]{2,1,0:T(8,128)(2,1)}, u32[]{:S(2)}, u32[]{:S(2)}) collective-permute-start(bf16[7,64,512]{2,1,0:T(8,128)(2,1)} %get-tuple-element.46), channel_id=1, source_target_pairs={{0,16},{1,17},{2,18},{3,19},{4,20},{5,21},{6,22},{7,23},{8,24},{9,... | collective-permute-start | bytes 1376264 | tf_op jit(solution)/shard_map/ppermute | solution.py:478
  14.0 0.7 copy-done.5
  14.7 0.8 prepare.1
  15.6 0.3 copy-done.2
  15.9 10.4 %inner.1 = (bf16[512,512]{1,0:T(8,128)(2,1)S(1)}, bf16[1536,512]{1,0:T(8,128)(2,1)S(1)}, f32[512,2048]{1,0:T(8,128)S(1)}, f32[16,64,128]{2,1,0:T(8,128)S(1)}) custom-call(s32[22]{0:T(128)S(1)} %concatenate.3.meta, bf16[16,64,512]{2,1,0:T(8,128)(2,1)S(1)} %copy-done.2, bf16[16,64,512]{2,1,0:T(8,128)(2,1)S(1)} %copy-done, ...), custom_call_target="tpu_custom_call" | custom-call | flops 8000000000 | bytes 16777216 | tf_op jit(solution)/shard_map/inner/pallas_call | solution.py:523
  26.3 1.1 collective-permute-done.2.corner_ref
  27.4 2.9 %front.1 = (bf16[512,512]{1,0:T(8,128)(2,1)S(1)}, bf16[512,512]{1,0:T(8,128)(2,1)S(1)}, bf16[1536,512]{1,0:T(8,128)(2,1)S(1)}, bf16[512,1024]{1,0:T(8,128)(2,1)S(1)}) custom-call(s32[22]{0:T(128)S(1)} %concatenate.3.meta, bf16[16,64,512]{2,1,0:T(8,128)(2,1)S(1)} %copy-done.2, bf16[2,16,8,512]{3,2,1,0:T(8,128)(2,1)S(1)} %collective-permute-done.side_ref, ...), custom_call_target="tpu_custom_call" | custom-call | flops 3000000000 | bytes 8388608 | tf_op jit(solution)/shard_map/front/pallas_call | solution.py:546
  30.3 8.1 %collective-permute-done.3.top = bf16[7,64,512]{2,1,0:T(8,128)(2,1)} collective-permute-done((bf16[7,64,512]{2,1,0:T(8,128)(2,1)}, bf16[7,64,512]{2,1,0:T(8,128)(2,1)}, u32[]{:S(2)}, u32[]{:S(2)}) %collective-permute-start.3) | collective-permute-done | bytes 458784 | tf_op jit(solution)/shard_map/ppermute | solution.py:478
  38.4 10.9 %outer.1 = (bf16[1536,512]{1,0:T(8,128)(2,1)S(1)}, f32[16,16,2176]{2,1,0:T(8,128)S(1)}, bf16[16,16,2176]{2,1,0:T(8,128)(2,1)S(1)}) custom-call(s32[22]{0:T(128)S(1)} %concatenate.3.meta, bf16[16,64,512]{2,1,0:T(8,128)(2,1)S(1)} %copy-done, bf16[2,16,8,512]{3,2,1,0:T(8,128)(2,1)S(1)} %collective-permute-done.side_ref, ...), custom_call_target="tpu_custom_call" | custom-call | flops 10000000000 | bytes 25165824 | tf_op jit(solution)/shard_map/outer/pallas_call | solution.py:559
  49.3 0.1 collective-permute-start.4
  49.4 2.7 %collective-permute-done.4.got_ref = bf16[16,16,2176]{2,1,0:T(8,128)(2,1)S(1)} collective-permute-done((bf16[16,16,2176]{2,1,0:T(8,128)(2,1)S(1)}, bf16[16,16,2176]{2,1,0:T(8,128)(2,1)S(1)}, u32[]{:S(2)}, u32[]{:S(2)}) %collective-permute-start.4) | collective-permute-done | bytes 1114144 | tf_op jit(solution)/shard_map/ppermute | solution.py:421
  52.1 0.2 add_c.1
  52.3 0.9 collective-permute-start.6
  53.2 2.5 %collective-permute-start.7 = (bf16[4,16,2176]{2,1,0:T(8,128)(2,1)S(1)}, bf16[4,16,2176]{2,1,0:T(8,128)(2,1)S(1)}, u32[]{:S(2)}, u32[]{:S(2)}) collective-permute-start(bf16[4,16,2176]{2,1,0:T(8,128)(2,1)S(1)} %get-tuple-element.59), channel_id=1, source_target_pairs={{0,4},{1,5},{2,6},{3,7},{4,0},{5,1},{6,2},{7,3},{8,12},{9,13},{10,... | collective-permute-start | bytes 835592 | tf_op jit(solution)/shard_map/ppermute | solution.py:421
  55.7 1.2 collective-permute-start.8
  56.9 3.7 %cells.1 = (bf16[16,64,512]{2,1,0:T(8,128)(2,1)S(1)}, bf16[7,72,512]{2,1,0:T(8,128)(2,1)S(1)}, bf16[16,8,512]{2,1,0:T(8,128)(2,1)S(1)}) custom-call(s32[22]{0:T(128)S(1)} %concatenate.3.meta, bf16[512,512]{1,0:T(8,128)(2,1)S(1)} %get-tuple-element.40.xi_ref, bf16[512,512]{1,0:T(8,128)(2,1)S(1)} %get-tuple-element.44.xo_ref, ...), custom_call_target="tpu_custom_call" | custom-call | flops 1600000000 | bytes 12582912 | tf_op jit(solution)/shard_map/cells/pallas_call | solution.py:583
  60.6 3.5 %collective-permute-start.5 = (bf16[7,72,512]{2,1,0:T(8,128)(2,1)S(1)}, bf16[7,72,512]{2,1,0:T(8,128)(2,1)S(1)}, u32[]{:S(2)}, u32[]{:S(2)}) collective-permute-start(bf16[7,72,512]{2,1,0:T(8,128)(2,1)S(1)} %get-tuple-element.56), channel_id=1, source_target_pairs={{0,240},{1,241},{2,242},{3,243},{4,244},{5,245},{6,246},{7,247},{8... | collective-permute-start | bytes 1548296 | tf_op jit(solution)/shard_map/ppermute | solution.py:478
  64.1 4.1 %collective-permute-done.7.refs_1_ = bf16[4,16,2176]{2,1,0:T(8,128)(2,1)S(1)} collective-permute-done((bf16[4,16,2176]{2,1,0:T(8,128)(2,1)S(1)}, bf16[4,16,2176]{2,1,0:T(8,128)(2,1)S(1)}, u32[]{:S(2)}, u32[]{:S(2)}) %collective-permute-start.7) | collective-permute-done | bytes 278560 | tf_op jit(solution)/shard_map/ppermute | solution.py:421
  68.3 0.1 add_x.1
  68.4 0.8 collective-permute-start.9
  69.3 2.5 %collective-permute-start.11 = (bf16[1,16,2176]{2,1,0:T(8,128)(2,1)S(1)}, bf16[1,16,2176]{2,1,0:T(8,128)(2,1)S(1)}, u32[]{:S(2)}, u32[]{:S(2)}) collective-permute-start(bf16[1,16,2176]{2,1,0:T(8,128)(2,1)S(1)} %get-tuple-element.64), channel_id=1, source_target_pairs={{0,24},{1,25},{2,26},{3,27},{4,28},{5,29},{6,30},{7,31},{8,0},{9,1... | collective-permute-start | bytes 208904 | tf_op jit(solution)/shard_map/ppermute | solution.py:421
  71.7 6.4 %collective-permute-done.9.refs_0_ = bf16[1,16,2176]{2,1,0:T(8,128)(2,1)S(1)} collective-permute-done((bf16[1,16,2176]{2,1,0:T(8,128)(2,1)S(1)}, bf16[1,16,2176]{2,1,0:T(8,128)(2,1)S(1)}, u32[]{:S(2)}, u32[]{:S(2)}) %collective-permute-start.9) | collective-permute-done | bytes 69664 | tf_op jit(solution)/shard_map/ppermute | solution.py:421
  78.2 0.1 collective-permute-start.12
  78.3 3.4 %collective-permute-start.13 = (bf16[1,16,2176]{2,1,0:T(8,128)(2,1)S(1)}, bf16[1,16,2176]{2,1,0:T(8,128)(2,1)S(1)}, u32[]{:S(2)}, u32[]{:S(2)}) collective-permute-start(bf16[1,16,2176]{2,1,0:T(8,128)(2,1)S(1)} %add_y.1.refs_0_), channel_id=1, source_target_pairs={{0,64},{1,65},{2,66},{3,67},{4,68},{5,69},{6,70},{7,71},{8,72},{9,... | collective-permute-start | bytes 208904 | tf_op jit(solution)/shard_map/ppermute | solution.py:421
  81.7 0.1 collective-permute-start.14
  81.8 1.8 %collective-permute-done.13.refs_2_ = bf16[1,16,2176]{2,1,0:T(8,128)(2,1)S(1)} collective-permute-done((bf16[1,16,2176]{2,1,0:T(8,128)(2,1)S(1)}, bf16[1,16,2176]{2,1,0:T(8,128)(2,1)S(1)}, u32[]{:S(2)}, u32[]{:S(2)}) %collective-permute-start.13) | collective-permute-done | bytes 69664 | tf_op jit(solution)/shard_map/ppermute | solution.py:421
  83.6 3.1 %collective-permute-done.14.refs_3_ = bf16[1,16,2176]{2,1,0:T(8,128)(2,1)S(1)} collective-permute-done((bf16[1,16,2176]{2,1,0:T(8,128)(2,1)S(1)}, bf16[1,16,2176]{2,1,0:T(8,128)(2,1)S(1)}, u32[]{:S(2)}, u32[]{:S(2)}) %collective-permute-start.14) | collective-permute-done | bytes 69664 | tf_op jit(solution)/shard_map/ppermute | solution.py:421
  86.7 4.4 %collective-permute-start.15 = (bf16[1,16,2176]{2,1,0:T(8,128)(2,1)S(1)}, bf16[1,16,2176]{2,1,0:T(8,128)(2,1)S(1)}, u32[]{:S(2)}, u32[]{:S(2)}) collective-permute-start(bf16[1,16,2176]{2,1,0:T(8,128)(2,1)S(1)} %add_z.2.refs_0_), channel_id=1, source_target_pairs={{0,192},{1,193},{2,194},{3,195},{4,196},{5,197},{6,198},{7,199},{8... | collective-permute-start | bytes 208904 | tf_op jit(solution)/shard_map/ppermute | solution.py:421
  91.1 1.8 %collective-permute-done.15.refs_1_ = bf16[1,16,2176]{2,1,0:T(8,128)(2,1)S(1)} collective-permute-done((bf16[1,16,2176]{2,1,0:T(8,128)(2,1)S(1)}, bf16[1,16,2176]{2,1,0:T(8,128)(2,1)S(1)}, u32[]{:S(2)}, u32[]{:S(2)}) %collective-permute-start.15) | collective-permute-done | bytes 69664 | tf_op jit(solution)/shard_map/ppermute | solution.py:421
  92.9 2.4 %collective-permute-start.16 = (bf16[1,16,2176]{2,1,0:T(8,128)(2,1)S(1)}, bf16[1,16,2176]{2,1,0:T(8,128)(2,1)S(1)}, u32[]{:S(2)}, u32[]{:S(2)}) collective-permute-start(bf16[1,16,2176]{2,1,0:T(8,128)(2,1)S(1)} %add_z.3.refs_0_), channel_id=1, source_target_pairs={{0,24},{1,25},{2,26},{3,27},{4,28},{5,29},{6,30},{7,31},{8,0},{9,1... | collective-permute-start | bytes 208904 | tf_op jit(solution)/shard_map/ppermute | solution.py:421
  95.4 0.8 collective-permute-start.18
  96.1 0.6 collective-permute-done.16.refs_1_
  96.7 3.4 %collective-permute-done.17.refs_2_ = bf16[1,16,2176]{2,1,0:T(8,128)(2,1)S(1)} collective-permute-done((bf16[1,16,2176]{2,1,0:T(8,128)(2,1)S(1)}, bf16[1,16,2176]{2,1,0:T(8,128)(2,1)S(1)}, u32[]{:S(2)}, u32[]{:S(2)}) %collective-permute-start.17) | collective-permute-done | bytes 69664 | tf_op jit(solution)/shard_map/ppermute | solution.py:421
  100.1 0.4 collective-permute-done.18.refs_3_
  100.5 0.3 collective-permute-start.20
  100.9 2.4 %collective-permute-start.21 = (bf16[4,16,2176]{2,1,0:T(8,128)(2,1)S(1)}, bf16[4,16,2176]{2,1,0:T(8,128)(2,1)S(1)}, u32[]{:S(2)}, u32[]{:S(2)}) collective-permute-start(bf16[4,16,2176]{2,1,0:T(8,128)(2,1)S(1)} %join.1._.refs_0_), channel_id=1, source_target_pairs={{0,4},{1,5},{2,6},{3,7},{4,0},{5,1},{6,2},{7,3},{8,12},{9,13},{10,... | collective-permute-start | bytes 835592 | tf_op jit(solution)/shard_map/ppermute | solution.py:421
  103.2 0.8 collective-permute-start.22
  104.0 5.5 %collective-permute-start.19 = (bf16[16,8,512]{2,1,0:T(8,128)(2,1)S(1)}, bf16[16,8,512]{2,1,0:T(8,128)(2,1)S(1)}, u32[]{:S(2)}, u32[]{:S(2)}) collective-permute-start(bf16[16,8,512]{2,1,0:T(8,128)(2,1)S(1)} %edge.1), channel_id=1, source_target_pairs={{0,15},{1,0},{2,1},{3,2},{4,3},{5,4},{6,5},{7,6},{8,7},{9,8},{10,9... | collective-permute-start | bytes 393224 | tf_op jit(solution)/shard_map/ppermute | solution.py:478
  109.5 0.1 collective-permute-start.23
  109.6 3.3 %collective-permute-start.24 = (bf16[4,16,2176]{2,1,0:T(8,128)(2,1)S(1)}, bf16[4,16,2176]{2,1,0:T(8,128)(2,1)S(1)}, u32[]{:S(2)}, u32[]{:S(2)}) collective-permute-start(bf16[4,16,2176]{2,1,0:T(8,128)(2,1)S(1)} %collective-permute-done.20.refs_1_), channel_id=1, source_target_pairs={{0,1},{1,0},{2,3},{3,2},{4,5},{5,4},{6,7},{7,6},{8,9},{9,8},{10,11... | collective-permute-start | bytes 835592 | tf_op jit(solution)/shard_map/ppermute | solution.py:421
  112.9 1.7 %collective-permute-start.25 = (bf16[4,16,2176]{2,1,0:T(8,128)(2,1)S(1)}, bf16[4,16,2176]{2,1,0:T(8,128)(2,1)S(1)}, u32[]{:S(2)}, u32[]{:S(2)}) collective-permute-start(bf16[4,16,2176]{2,1,0:T(8,128)(2,1)S(1)} %collective-permute-done.21.refs_2_), channel_id=1, source_target_pairs={{0,1},{1,0},{2,3},{3,2},{4,5},{5,4},{6,7},{7,6},{8,9},{9,8},{10,11... | collective-permute-start | bytes 835592 | tf_op jit(solution)/shard_map/ppermute | solution.py:421
  114.6 2.9 %collective-permute-start.26 = (bf16[4,16,2176]{2,1,0:T(8,128)(2,1)S(1)}, bf16[4,16,2176]{2,1,0:T(8,128)(2,1)S(1)}, u32[]{:S(2)}, u32[]{:S(2)}) collective-permute-start(bf16[4,16,2176]{2,1,0:T(8,128)(2,1)S(1)} %collective-permute-done.22.refs_3_), channel_id=1, source_target_pairs={{0,1},{1,0},{2,3},{3,2},{4,5},{5,4},{6,7},{7,6},{8,9},{9,8},{10,11... | collective-permute-start | bytes 835592 | tf_op jit(solution)/shard_map/ppermute | solution.py:421
  117.5 1.2 add_convert_fusion
  118.8 3.1 %unpack.1 = (f32[512,1536]{1,0:T(8,128)}, f32[512,512]{1,0:T(8,128)}, f32[1,512]{1,0:T(1,128)}, f32[16,225]{1,0:T(8,128)}) custom-call(s32[22]{0:T(128)S(1)} %concatenate.3.meta, bf16[4,16,2176]{2,1,0:T(8,128)(2,1)S(1)} %join.1._.refs_0_, bf16[4,16,2176]{2,1,0:T(8,128)(2,1)S(1)} %collective-permute-done.20.refs_1_, ...), custom_call_target="tpu_custom_call" | custom-call | tf_op jit(solution)/shard_map/unpack/pallas_call | solution.py:616
  (39 shorter events, 0.4 us)
Async XLA Ops:
  0.6 13.3 %copy-start.6 = (s32[16]{0:T(128)S(1)}, s32[16]{0:T(128)}, u32[]{:S(2)}) copy-start(s32[16]{0:T(128)} %mask.1) | copy-start | bytes 196
  0.6 13.3 %copy-start.7 = (s32[2]{0:T(128)S(1)}, s32[2]{0:T(128)}, u32[]{:S(2)}) copy-start(s32[2]{0:T(128)} %param.11) | copy-start | bytes 28
  0.7 13.3 %copy-start.1 = (bf16[512,1536]{1,0:T(8,128)(2,1)S(1)}, bf16[512,1536]{1,0:T(8,128)(2,1)}, u32[]{:S(2)}) copy-start(bf16[512,1536]{1,0:T(8,128)(2,1)} %w_ref.9) | copy-start | bytes 4718596
  3.9 11.7 %copy-start = (bf16[16,64,512]{2,1,0:T(8,128)(2,1)S(1)}, bf16[16,64,512]{2,1,0:T(8,128)(2,1)}, u32[]{:S(2)}) copy-start(bf16[16,64,512]{2,1,0:T(8,128)(2,1)} %cot_ref.7) | copy-start | bytes 3145732
  3.9 11.7 %copy-start.3 = (f32[512]{0:T(512)S(1)}, f32[512]{0:T(512)}, u32[]{:S(2)}) copy-start(f32[512]{0:T(512)} %param.12) | copy-start | bytes 6148
  3.9 11.7 %copy-start.4 = (bf16[512,512]{1,0:T(8,128)(2,1)S(1)}, bf16[512,512]{1,0:T(8,128)(2,1)}, u32[]{:S(2)}) copy-start(bf16[512,512]{1,0:T(8,128)(2,1)} %wo_ref.3) | copy-start | bytes 1572868
  3.9 11.7 %collective-permute-start = (bf16[2,16,8,512]{3,2,1,0:T(8,128)(2,1)}, bf16[2,16,8,512]{3,2,1,0:T(8,128)(2,1)S(1)}, u32[]{:S(2)}, u32[]{:S(2)}) collective-permute-start(bf16[2,16,8,512]{3,2,1,0:T(8,128)(2,1)} %get-tuple-element.37), channel_id=1, source_target_pairs={{0,1},{1,2},{2,3},{3,4},{4,5},{5,6},{6,7},{7,8},{8,9},{9,10},{10,1... | collective-permute-start | bytes 786440 | tf_op jit(solution)/shard_map/ppermute | solution.py:478
  6.6 20.9 %collective-permute-start.1 = (bf16[7,64,512]{2,1,0:T(8,128)(2,1)}, bf16[7,64,512]{2,1,0:T(8,128)(2,1)}, u32[]{:S(2)}, u32[]{:S(2)}) collective-permute-start(bf16[7,64,512]{2,1,0:T(8,128)(2,1)} %get-tuple-element.41), channel_id=1, source_target_pairs={{0,16},{1,17},{2,18},{3,19},{4,20},{5,21},{6,22},{7,23},{8,24},{9,... | collective-permute-start | bytes 1376264 | tf_op jit(solution)/shard_map/ppermute | solution.py:478
  9.5 17.9 %collective-permute-start.2 = (bf16[2,8,8,512]{3,2,1,0:T(8,128)(2,1)}, bf16[2,8,8,512]{3,2,1,0:T(8,128)(2,1)S(1)}, u32[]{:S(2)}, u32[]{:S(2)}) collective-permute-start(bf16[2,8,8,512]{3,2,1,0:T(8,128)(2,1)} %get-tuple-element.42), channel_id=1, source_target_pairs={{0,17},{1,18},{2,19},{3,20},{4,21},{5,22},{6,23},{7,24},{8,25},{9,... | collective-permute-start | bytes 393224 | tf_op jit(solution)/shard_map/ppermute | solution.py:478
  11.0 27.4 %collective-permute-start.3 = (bf16[7,64,512]{2,1,0:T(8,128)(2,1)}, bf16[7,64,512]{2,1,0:T(8,128)(2,1)}, u32[]{:S(2)}, u32[]{:S(2)}) collective-permute-start(bf16[7,64,512]{2,1,0:T(8,128)(2,1)} %get-tuple-element.46), channel_id=1, source_target_pairs={{0,16},{1,17},{2,18},{3,19},{4,20},{5,21},{6,22},{7,23},{8,24},{9,... | collective-permute-start | bytes 1376264 | tf_op jit(solution)/shard_map/ppermute | solution.py:478
  14.0 0.7 copy-start.5
  14.7 1.2 %copy-start.2 = (bf16[16,64,512]{2,1,0:T(8,128)(2,1)S(1)}, bf16[16,64,512]{2,1,0:T(8,128)(2,1)}, u32[]{:S(2)}) copy-start(bf16[16,64,512]{2,1,0:T(8,128)(2,1)} %x_ref.5) | copy-start | bytes 3145732
  49.3 2.8 %collective-permute-start.4 = (bf16[16,16,2176]{2,1,0:T(8,128)(2,1)S(1)}, bf16[16,16,2176]{2,1,0:T(8,128)(2,1)S(1)}, u32[]{:S(2)}, u32[]{:S(2)}) collective-permute-start(bf16[16,16,2176]{2,1,0:T(8,128)(2,1)S(1)} %get-tuple-element.53), channel_id=1, source_target_pairs={{0,1},{1,0},{2,3},{3,2},{4,5},{5,4},{6,7},{7,6},{8,9},{9,8},{10,11... | collective-permute-start | bytes 3342344 | tf_op jit(solution)/shard_map/ppermute | solution.py:421
  52.3 11.8 %collective-permute-start.6 = (bf16[4,16,2176]{2,1,0:T(8,128)(2,1)S(1)}, bf16[4,16,2176]{2,1,0:T(8,128)(2,1)S(1)}, u32[]{:S(2)}, u32[]{:S(2)}) collective-permute-start(bf16[4,16,2176]{2,1,0:T(8,128)(2,1)S(1)} %get-tuple-element.58), channel_id=1, source_target_pairs={{0,2},{1,3},{2,4},{3,5},{4,6},{5,7},{6,0},{7,1},{8,10},{9,11},{10,... | collective-permute-start | bytes 835592 | tf_op jit(solution)/shard_map/ppermute | solution.py:421
  53.2 15.1 %collective-permute-start.7 = (bf16[4,16,2176]{2,1,0:T(8,128)(2,1)S(1)}, bf16[4,16,2176]{2,1,0:T(8,128)(2,1)S(1)}, u32[]{:S(2)}, u32[]{:S(2)}) collective-permute-start(bf16[4,16,2176]{2,1,0:T(8,128)(2,1)S(1)} %get-tuple-element.59), channel_id=1, source_target_pairs={{0,4},{1,5},{2,6},{3,7},{4,0},{5,1},{6,2},{7,3},{8,12},{9,13},{10,... | collective-permute-start | bytes 835592 | tf_op jit(solution)/shard_map/ppermute | solution.py:421
  55.7 12.6 %collective-permute-start.8 = (bf16[4,16,2176]{2,1,0:T(8,128)(2,1)S(1)}, bf16[4,16,2176]{2,1,0:T(8,128)(2,1)S(1)}, u32[]{:S(2)}, u32[]{:S(2)}) collective-permute-start(bf16[4,16,2176]{2,1,0:T(8,128)(2,1)S(1)} %get-tuple-element.60), channel_id=1, source_target_pairs={{0,6},{1,7},{2,0},{3,1},{4,2},{5,3},{6,4},{7,5},{8,14},{9,15},{10,... | collective-permute-start | bytes 835592 | tf_op jit(solution)/shard_map/ppermute | solution.py:421
  60.6 43.3 %collective-permute-start.5 = (bf16[7,72,512]{2,1,0:T(8,128)(2,1)S(1)}, bf16[7,72,512]{2,1,0:T(8,128)(2,1)S(1)}, u32[]{:S(2)}, u32[]{:S(2)}) collective-permute-start(bf16[7,72,512]{2,1,0:T(8,128)(2,1)S(1)} %get-tuple-element.56), channel_id=1, source_target_pairs={{0,240},{1,241},{2,242},{3,243},{4,244},{5,245},{6,246},{7,247},{8... | collective-permute-start | bytes 1548296 | tf_op jit(solution)/shard_map/ppermute | solution.py:478
  68.4 9.7 %collective-permute-start.9 = (bf16[1,16,2176]{2,1,0:T(8,128)(2,1)S(1)}, bf16[1,16,2176]{2,1,0:T(8,128)(2,1)S(1)}, u32[]{:S(2)}, u32[]{:S(2)}) collective-permute-start(bf16[1,16,2176]{2,1,0:T(8,128)(2,1)S(1)} %get-tuple-element.62), channel_id=1, source_target_pairs={{0,8},{1,9},{2,10},{3,11},{4,12},{5,13},{6,14},{7,15},{8,16},{9,17... | collective-permute-start | bytes 208904 | tf_op jit(solution)/shard_map/ppermute | solution.py:421
  69.2 8.9 %collective-permute-start.10 = (bf16[1,16,2176]{2,1,0:T(8,128)(2,1)S(1)}, bf16[1,16,2176]{2,1,0:T(8,128)(2,1)S(1)}, u32[]{:S(2)}, u32[]{:S(2)}) collective-permute-start(bf16[1,16,2176]{2,1,0:T(8,128)(2,1)S(1)} %get-tuple-element.63), channel_id=1, source_target_pairs={{0,16},{1,17},{2,18},{3,19},{4,20},{5,21},{6,22},{7,23},{8,24},{9,... | collective-permute-start | bytes 208904 | tf_op jit(solution)/shard_map/ppermute | solution.py:421
  69.3 8.9 %collective-permute-start.11 = (bf16[1,16,2176]{2,1,0:T(8,128)(2,1)S(1)}, bf16[1,16,2176]{2,1,0:T(8,128)(2,1)S(1)}, u32[]{:S(2)}, u32[]{:S(2)}) collective-permute-start(bf16[1,16,2176]{2,1,0:T(8,128)(2,1)S(1)} %get-tuple-element.64), channel_id=1, source_target_pairs={{0,24},{1,25},{2,26},{3,27},{4,28},{5,29},{6,30},{7,31},{8,0},{9,1... | collective-permute-start | bytes 208904 | tf_op jit(solution)/shard_map/ppermute | solution.py:421
  78.2 3.6 %collective-permute-start.12 = (bf16[1,16,2176]{2,1,0:T(8,128)(2,1)S(1)}, bf16[1,16,2176]{2,1,0:T(8,128)(2,1)S(1)}, u32[]{:S(2)}, u32[]{:S(2)}) collective-permute-start(bf16[1,16,2176]{2,1,0:T(8,128)(2,1)S(1)} %add_y.1.refs_0_), channel_id=1, source_target_pairs={{0,32},{1,33},{2,34},{3,35},{4,36},{5,37},{6,38},{7,39},{8,40},{9,... | collective-permute-start | bytes 208904 | tf_op jit(solution)/shard_map/ppermute | solution.py:421
  78.3 5.3 %collective-permute-start.13 = (bf16[1,16,2176]{2,1,0:T(8,128)(2,1)S(1)}, bf16[1,16,2176]{2,1,0:T(8,128)(2,1)S(1)}, u32[]{:S(2)}, u32[]{:S(2)}) collective-permute-start(bf16[1,16,2176]{2,1,0:T(8,128)(2,1)S(1)} %add_y.1.refs_0_), channel_id=1, source_target_pairs={{0,64},{1,65},{2,66},{3,67},{4,68},{5,69},{6,70},{7,71},{8,72},{9,... | collective-permute-start | bytes 208904 | tf_op jit(solution)/shard_map/ppermute | solution.py:421
  81.7 5.0 %collective-permute-start.14 = (bf16[1,16,2176]{2,1,0:T(8,128)(2,1)S(1)}, bf16[1,16,2176]{2,1,0:T(8,128)(2,1)S(1)}, u32[]{:S(2)}, u32[]{:S(2)}) collective-permute-start(bf16[1,16,2176]{2,1,0:T(8,128)(2,1)S(1)} %add_y.1.refs_0_), channel_id=1, source_target_pairs={{0,96},{1,97},{2,98},{3,99},{4,100},{5,101},{6,102},{7,103},{8,104... | collective-permute-start | bytes 208904 | tf_op jit(solution)/shard_map/ppermute | solution.py:421
  86.7 6.2 %collective-permute-start.15 = (bf16[1,16,2176]{2,1,0:T(8,128)(2,1)S(1)}, bf16[1,16,2176]{2,1,0:T(8,128)(2,1)S(1)}, u32[]{:S(2)}, u32[]{:S(2)}) collective-permute-start(bf16[1,16,2176]{2,1,0:T(8,128)(2,1)S(1)} %add_z.2.refs_0_), channel_id=1, source_target_pairs={{0,192},{1,193},{2,194},{3,195},{4,196},{5,197},{6,198},{7,199},{8... | collective-permute-start | bytes 208904 | tf_op jit(solution)/shard_map/ppermute | solution.py:421
  92.9 3.8 %collective-permute-start.16 = (bf16[1,16,2176]{2,1,0:T(8,128)(2,1)S(1)}, bf16[1,16,2176]{2,1,0:T(8,128)(2,1)S(1)}, u32[]{:S(2)}, u32[]{:S(2)}) collective-permute-start(bf16[1,16,2176]{2,1,0:T(8,128)(2,1)S(1)} %add_z.3.refs_0_), channel_id=1, source_target_pairs={{0,24},{1,25},{2,26},{3,27},{4,28},{5,29},{6,30},{7,31},{8,0},{9,1... | collective-permute-start | bytes 208904 | tf_op jit(solution)/shard_map/ppermute | solution.py:421
  95.3 4.8 %collective-permute-start.17 = (bf16[1,16,2176]{2,1,0:T(8,128)(2,1)S(1)}, bf16[1,16,2176]{2,1,0:T(8,128)(2,1)S(1)}, u32[]{:S(2)}, u32[]{:S(2)}) collective-permute-start(bf16[1,16,2176]{2,1,0:T(8,128)(2,1)S(1)} %add_z.3.refs_0_), channel_id=1, source_target_pairs={{0,16},{1,17},{2,18},{3,19},{4,20},{5,21},{6,22},{7,23},{8,24},{9,... | collective-permute-start | bytes 208904 | tf_op jit(solution)/shard_map/ppermute | solution.py:421
  95.4 5.1 %collective-permute-start.18 = (bf16[1,16,2176]{2,1,0:T(8,128)(2,1)S(1)}, bf16[1,16,2176]{2,1,0:T(8,128)(2,1)S(1)}, u32[]{:S(2)}, u32[]{:S(2)}) collective-permute-start(bf16[1,16,2176]{2,1,0:T(8,128)(2,1)S(1)} %add_z.3.refs_0_), channel_id=1, source_target_pairs={{0,8},{1,9},{2,10},{3,11},{4,12},{5,13},{6,14},{7,15},{8,16},{9,17... | collective-permute-start | bytes 208904 | tf_op jit(solution)/shard_map/ppermute | solution.py:421
  100.5 9.0 %collective-permute-start.20 = (bf16[4,16,2176]{2,1,0:T(8,128)(2,1)S(1)}, bf16[4,16,2176]{2,1,0:T(8,128)(2,1)S(1)}, u32[]{:S(2)}, u32[]{:S(2)}) collective-permute-start(bf16[4,16,2176]{2,1,0:T(8,128)(2,1)S(1)} %join.1._.refs_0_), channel_id=1, source_target_pairs={{0,6},{1,7},{2,0},{3,1},{4,2},{5,3},{6,4},{7,5},{8,14},{9,15},{10,... | collective-permute-start | bytes 835592 | tf_op jit(solution)/shard_map/ppermute | solution.py:421
  100.9 12.0 %collective-permute-start.21 = (bf16[4,16,2176]{2,1,0:T(8,128)(2,1)S(1)}, bf16[4,16,2176]{2,1,0:T(8,128)(2,1)S(1)}, u32[]{:S(2)}, u32[]{:S(2)}) collective-permute-start(bf16[4,16,2176]{2,1,0:T(8,128)(2,1)S(1)} %join.1._.refs_0_), channel_id=1, source_target_pairs={{0,4},{1,5},{2,6},{3,7},{4,0},{5,1},{6,2},{7,3},{8,12},{9,13},{10,... | collective-permute-start | bytes 835592 | tf_op jit(solution)/shard_map/ppermute | solution.py:421
  103.2 11.4 %collective-permute-start.22 = (bf16[4,16,2176]{2,1,0:T(8,128)(2,1)S(1)}, bf16[4,16,2176]{2,1,0:T(8,128)(2,1)S(1)}, u32[]{:S(2)}, u32[]{:S(2)}) collective-permute-start(bf16[4,16,2176]{2,1,0:T(8,128)(2,1)S(1)} %join.1._.refs_0_), channel_id=1, source_target_pairs={{0,2},{1,3},{2,4},{3,5},{4,6},{5,7},{6,0},{7,1},{8,10},{9,11},{10,... | collective-permute-start | bytes 835592 | tf_op jit(solution)/shard_map/ppermute | solution.py:421
  104.0 13.5 %collective-permute-start.19 = (bf16[16,8,512]{2,1,0:T(8,128)(2,1)S(1)}, bf16[16,8,512]{2,1,0:T(8,128)(2,1)S(1)}, u32[]{:S(2)}, u32[]{:S(2)}) collective-permute-start(bf16[16,8,512]{2,1,0:T(8,128)(2,1)S(1)} %edge.1), channel_id=1, source_target_pairs={{0,15},{1,0},{2,1},{3,2},{4,3},{5,4},{6,5},{7,6},{8,7},{9,8},{10,9... | collective-permute-start | bytes 393224 | tf_op jit(solution)/shard_map/ppermute | solution.py:478
  109.5 9.3 %collective-permute-start.23 = (bf16[4,16,2176]{2,1,0:T(8,128)(2,1)S(1)}, bf16[4,16,2176]{2,1,0:T(8,128)(2,1)S(1)}, u32[]{:S(2)}, u32[]{:S(2)}) collective-permute-start(bf16[4,16,2176]{2,1,0:T(8,128)(2,1)S(1)} %join.1._.refs_0_), channel_id=1, source_target_pairs={{0,1},{1,0},{2,3},{3,2},{4,5},{5,4},{6,7},{7,6},{8,9},{9,8},{10,11... | collective-permute-start | bytes 835592 | tf_op jit(solution)/shard_map/ppermute | solution.py:421
  109.6 9.2 %collective-permute-start.24 = (bf16[4,16,2176]{2,1,0:T(8,128)(2,1)S(1)}, bf16[4,16,2176]{2,1,0:T(8,128)(2,1)S(1)}, u32[]{:S(2)}, u32[]{:S(2)}) collective-permute-start(bf16[4,16,2176]{2,1,0:T(8,128)(2,1)S(1)} %collective-permute-done.20.refs_1_), channel_id=1, source_target_pairs={{0,1},{1,0},{2,3},{3,2},{4,5},{5,4},{6,7},{7,6},{8,9},{9,8},{10,11... | collective-permute-start | bytes 835592 | tf_op jit(solution)/shard_map/ppermute | solution.py:421
  112.9 5.8 %collective-permute-start.25 = (bf16[4,16,2176]{2,1,0:T(8,128)(2,1)S(1)}, bf16[4,16,2176]{2,1,0:T(8,128)(2,1)S(1)}, u32[]{:S(2)}, u32[]{:S(2)}) collective-permute-start(bf16[4,16,2176]{2,1,0:T(8,128)(2,1)S(1)} %collective-permute-done.21.refs_2_), channel_id=1, source_target_pairs={{0,1},{1,0},{2,3},{3,2},{4,5},{5,4},{6,7},{7,6},{8,9},{9,8},{10,11... | collective-permute-start | bytes 835592 | tf_op jit(solution)/shard_map/ppermute | solution.py:421
  114.6 4.1 %collective-permute-start.26 = (bf16[4,16,2176]{2,1,0:T(8,128)(2,1)S(1)}, bf16[4,16,2176]{2,1,0:T(8,128)(2,1)S(1)}, u32[]{:S(2)}, u32[]{:S(2)}) collective-permute-start(bf16[4,16,2176]{2,1,0:T(8,128)(2,1)S(1)} %collective-permute-done.22.refs_3_), channel_id=1, source_target_pairs={{0,1},{1,0},{2,3},{3,2},{4,5},{5,4},{6,7},{7,6},{8,9},{9,8},{10,11... | collective-permute-start | bytes 835592 | tf_op jit(solution)/shard_map/ppermute | solution.py:421
